TPU v7x, 256 devices: a whole 4x4x8 slice. The times are simulated.
256 devices in a mesh: dp: 32 (over z_lo, x, y), space: 8 (over z_hi, core).
Axes of the slice: x: 4, y: 4, z: 8 (z_hi: 4, z_lo: 2; z = z_hi * 2 + z_lo), core: 2. Of those that a mesh axis runs over, the one named last changes fastest.
Arguments:
- images: bfloat16 [32, 1024, 1024], P('dp', 'space'), may hold values from -6 to 6
- cotangent: bfloat16 [32, 1024, 1024], P('dp', 'space'), may hold values from -6 to 6
- w_qkv: bfloat16 [1024, 3072], P('dp'), may hold values from -0.1875 to 0.1875
- w_out: bfloat16 [1024, 1024], P('dp'), may hold values from -0.1875 to 0.1875
- film: bfloat16 [1000, 2048], replicated, may hold values from -1 to 1
- timesteps: int32 [32], P('dp'), may hold values from 0 to 999
Outputs:
- branch_grad: bfloat16 [32, 1024, 1024], P('dp', 'space')
- grad_qkv: float32 [1024, 3072], P('dp')
- grad_out: float32 [1024, 1024], P('dp')
All inputs are finite; a program needn't handle non-finite values.
Results may differ from a plain program's by a relative error of at most 0.034.
Values may be sent and summed in bfloat16 or wider, within the bound.
No kernel may reach another device: no remote copies, remote signals or barrier semaphores. Data moves between devices by JAX's collectives and lax.ppermute only.
A program may use at most 128 MiB of HBM per device.

v0:
```python
import jax
import jax.numpy as jnp
from jax import lax
from jax.sharding import PartitionSpec as P

HEAD = 64


def body(images, cotangent, w_qkv, w_out, film, timesteps):
    imgs, rows, channel_width = images.shape
    heads = channel_width // HEAD
    total = imgs * rows
    onehot = (timesteps[:, None] == lax.iota(jnp.int32, film.shape[0])[None, :]).astype(
        jnp.bfloat16
    )
    feature_rows = jnp.dot(onehot, film, preferred_element_type=jnp.float32)
    xf = images.astype(jnp.float32)
    mean_x = jnp.mean(xf, -1, keepdims=True)
    centered_input = xf - mean_x
    inverse_deviation = lax.rsqrt(
        jnp.mean(centered_input * centered_input, -1, keepdims=True) + 1e-05
    )
    normalized_input = centered_input * inverse_deviation
    scale_factor = 1.0 + feature_rows[:, None, :channel_width]
    normalized_output = (
        normalized_input * scale_factor + feature_rows[:, None, channel_width:]
    ).astype(jnp.bfloat16)
    flat = normalized_output.reshape(total, channel_width)
    contract_last = (((1,), (1,)), ((), ()))
    full_qkv = lax.all_gather(w_qkv, "dp", axis=0, tiled=True)
    qkv = jnp.dot(flat, full_qkv, preferred_element_type=jnp.float32)
    qkv = qkv.astype(jnp.bfloat16).reshape(imgs, rows, 3 * channel_width)
    query = qkv[..., :channel_width].reshape(imgs, rows, heads, HEAD)
    own_keys = qkv[..., channel_width : 2 * channel_width].reshape(imgs, rows, heads, HEAD)
    own_vals = qkv[..., 2 * channel_width :].reshape(imgs, rows, heads, HEAD)
    keyval = lax.all_gather(qkv[..., channel_width:], "space", axis=1, tiled=True)
    keys = keyval[..., :channel_width].reshape(imgs, -1, heads, HEAD)
    values = keyval[..., channel_width:].reshape(imgs, -1, heads, HEAD)
    scores = jnp.einsum("irhd,ishd->ihrs", query, keys, preferred_element_type=jnp.float32) * 0.125
    top = jnp.max(scores, -1, keepdims=True)
    lse = top + jnp.log(jnp.sum(jnp.exp(scores - top), -1, keepdims=True))
    probs = jnp.exp(scores - lse)
    attended = jnp.einsum(
        "ihrs,ishd->irhd", probs.astype(jnp.bfloat16), values, preferred_element_type=jnp.float32
    ).astype(jnp.bfloat16)
    att_flat = attended.reshape(total, channel_width)
    cot_flat = cotangent.reshape(total, channel_width)
    d_att = lax.dot_general(
        cot_flat,
        lax.all_gather(w_out, "dp", axis=0, tiled=True),
        contract_last,
        preferred_element_type=jnp.float32,
    ).astype(jnp.bfloat16)
    d_att = d_att.reshape(imgs, rows, heads, HEAD)
    delta = jnp.sum(d_att.astype(jnp.float32) * attended.astype(jnp.float32), -1)
    dprob = jnp.einsum("irhd,ishd->ihrs", d_att, values, preferred_element_type=jnp.float32)
    dscore = (probs * (dprob - jnp.transpose(delta, (0, 2, 1))[..., None])).astype(jnp.bfloat16)
    dquery = (
        0.125 * jnp.einsum("ihrs,ishd->irhd", dscore, keys, preferred_element_type=jnp.float32)
    ).astype(jnp.bfloat16)
    lse_rows = jnp.transpose(lse[..., 0], (0, 2, 1))
    query_wide = query.astype(jnp.float32)
    d_att_wide = d_att.astype(jnp.float32)
    q_wide = lax.all_gather(query_wide, "space", axis=1, tiled=True)
    d_wide = lax.all_gather(d_att_wide, "space", axis=1, tiled=True)
    lse_piece = lax.all_gather(lse_rows, "space", axis=1, tiled=True)
    delta_piece = lax.all_gather(delta, "space", axis=1, tiled=True)
    q_piece = q_wide.astype(jnp.bfloat16)
    d_piece = d_wide.astype(jnp.bfloat16)
    local = (
        jnp.einsum("irhd,ishd->ihrs", q_piece, own_keys, preferred_element_type=jnp.float32) * 0.125
    )
    weights = jnp.exp(local - jnp.transpose(lse_piece, (0, 2, 1))[..., None])
    dval_acc = jnp.einsum(
        "ihrs,irhd->ishd", weights.astype(jnp.bfloat16), d_piece, preferred_element_type=jnp.float32
    )
    local_dprob = jnp.einsum(
        "irhd,ishd->ihrs", d_piece, own_vals, preferred_element_type=jnp.float32
    )
    local_ds = (weights * (local_dprob - jnp.transpose(delta_piece, (0, 2, 1))[..., None])).astype(
        jnp.bfloat16
    )
    dkey_acc = jnp.einsum("ihrs,irhd->ishd", local_ds, q_piece, preferred_element_type=jnp.float32)
    dkey = dkey_acc
    dval = dval_acc
    dkey = (0.125 * dkey).astype(jnp.bfloat16)
    dval = dval.astype(jnp.bfloat16)
    dqkv = jnp.concatenate(
        [
            dquery.reshape(total, channel_width),
            dkey.reshape(total, channel_width),
            dval.reshape(total, channel_width),
        ],
        -1,
    )
    dnormed = lax.dot_general(dqkv, full_qkv, contract_last, preferred_element_type=jnp.float32)
    normalized_gradient = dnormed.reshape(imgs, rows, channel_width) * scale_factor
    residual_branch = inverse_deviation * (
        normalized_gradient
        - jnp.mean(normalized_gradient, -1, keepdims=True)
        - normalized_input * jnp.mean(normalized_gradient * normalized_input, -1, keepdims=True)
    )
    contract_first = (((0,), (0,)), ((), ()))
    columns = flat
    grad_q = lax.psum_scatter(
        lax.dot_general(columns, dqkv, contract_first, preferred_element_type=jnp.float32).astype(
            jnp.bfloat16
        ),
        "dp",
        scatter_dimension=0,
        tiled=True,
    ).astype(jnp.float32)
    columns = att_flat
    grad_o = lax.psum_scatter(
        lax.dot_general(
            columns, cot_flat, contract_first, preferred_element_type=jnp.float32
        ).astype(jnp.bfloat16),
        "dp",
        scatter_dimension=0,
        tiled=True,
    ).astype(jnp.float32)
    grad_q, grad_o = (
        lax.psum(grad_q.astype(jnp.bfloat16), "space").astype(jnp.float32),
        lax.psum(grad_o.astype(jnp.bfloat16), "space").astype(jnp.float32),
    )
    return (residual_branch.astype(jnp.bfloat16), grad_q, grad_o)


def solution(mesh):
    return jax.shard_map(
        body,
        mesh=mesh,
        in_specs=(
            P("dp", "space", None),
            P("dp", "space", None),
            P("dp", None),
            P("dp", None),
            P(),
            P("dp"),
        ),
        out_specs=(P("dp", "space", None), P("dp", None), P("dp", None)),
        check_vma=False,
    )
```

profile of v0, /device:TPU:1, one launch (start us, length us, event | category | flops | bytes accessed | tf_op | source)
XLA Modules:
  0.0 898.3 jit_solution(2856872827682827432)
XLA Ops:
  11.6 2.9 fusion.73
  14.6 146.3 %all-gather.7.cloned.1.call-done = bf16[1024,3072]{1,0:T(8,128)(2,1)} async-done(((bf16[32,3072]{1,0:T(8,128)(2,1)}), bf16[1024,3072]{1,0:T(8,128)(2,1)}) %all-gather.7.cloned.1.call-update) | async-done | bytes 6291472 | tf_op jit(solution)/shard_map/all_gather | solution.py:30
  160.9 3.9 fusion.12
  167.5 148.9 %all-gather.11.cloned.1.call-done = bf16[1024,1024]{1,0:T(8,128)(2,1)} async-done(((bf16[32,1024]{1,0:T(8,128)(2,1)}), bf16[1024,1024]{1,0:T(8,128)(2,1)}) %all-gather.11.cloned.1.call-update) | async-done | bytes 2097168 | tf_op jit(solution)/shard_map/all_gather | solution.py:50
  316.4 2.4 convolution_convert_fusion.3
  320.7 68.8 %all-gather.9.cloned.1.call-done = bf16[1,1024,2048]{2,1,0:T(8,128)(2,1)} async-done(((bf16[1,128,2048]{2,1,0:T(8,128)(2,1)}), bf16[1,1024,2048]{2,1,0:T(8,128)(2,1)}) %all-gather.9.cloned.1.call-update) | async-done | bytes 4194320 | tf_op jit(solution)/shard_map/all_gather | solution.py:36
  389.5 4.6 fusion.71
  394.1 2.9 copy.17
  397.0 3.9 copy.20
  400.9 2.3 multiply_reduce_fusion
  408.8 2.0 convolution_convert_fusion.2
  412.8 20.0 %all-gather.13.cloned.1.call-done = bf16[1,1024,16,64]{1,3,2,0:T(8,128)(2,1)} async-done(((bf16[1,128,16,64]{1,3,2,0:T(8,128)(2,1)}), bf16[1,1024,16,64]{1,3,2,0:T(8,128)(2,1)}) %all-gather.13.cloned.1.call-update) | async-done | bytes 2097168 | tf_op jit(solution)/shard_map/all_gather | solution.py:64
  432.8 6.2 fusion.21
  439.0 15.1 %all-gather = f32[1024,16]{0,1:T(8,128)S(1)} all-gather(f32[128,16]{0,1:T(8,128)S(1)} %get-tuple-element.15), channel_id=2, replica_groups=mesh['dp'=32,'space'=8] {'space'}, dimensions={0}, use_global_device_ids=true | all-gather | bytes 73728 | tf_op jit(solution)/shard_map/all_gather | solution.py:67
  454.1 16.9 %all_gather.25 = f32[1,1024,16]{1,2,0:T(8,128)S(1)} all-gather(f32[1,128,16]{1,2,0:T(8,128)S(1)} %bitcast.125), channel_id=1, replica_groups=mesh['dp'=32,'space'=8] {'space'}, dimensions={1}, use_global_device_ids=true | all-gather | bytes 73728 | tf_op jit(solution)/shard_map/all_gather | solution.py:66
  471.0 2.2 all-gather.15.cloned.1.call-done
  473.2 5.5 fusion.38
  478.7 7.6 fusion.29
  486.3 9.0 fusion.30
  495.2 4.6 convolution_convert_fusion
  500.0 5.1 fusion.55
  505.2 111.2 %reduce-scatter.5.cloned.1.call-done = bf16[32,1024]{1,0:T(8,128)(2,1)} async-done(((bf16[1024,1024]{1,0:T(8,128)(2,1)}), bf16[32,1024]{1,0:T(8,128)(2,1)}) %reduce-scatter.5.cloned.1.call-update) | async-done | bytes 65552 | tf_op jit(solution)/shard_map/reduce_scatter | solution.py:114
  616.4 177.5 %reduce-scatter.3.cloned.1.call-done = bf16[32,3072]{1,0:T(8,128)(2,1)} async-done(((bf16[1024,3072]{1,0:T(8,128)(2,1)}), bf16[32,3072]{1,0:T(8,128)(2,1)}) %reduce-scatter.3.cloned.1.call-update) | async-done | bytes 196624 | tf_op jit(solution)/shard_map/reduce_scatter | solution.py:105
  794.8 93.5 %all-reduce.3.cloned.1.call-done = (bf16[32,3072]{1,0:T(8,128)(2,1)}, bf16[32,1024]{1,0:T(8,128)(2,1)}) async-done(((bf16[32,3072]{1,0:T(8,128)(2,1)}, bf16[32,1024]{1,0:T(8,128)(2,1)}), (bf16[32,3072]{1,0:T(8,128)(2,1)}, bf16[32,1024]{1,0:T(8,128)(2,1)})) %all-reduce.3.cloned.1.call-update) | async-done | bytes 262160 | tf_op jit(solution)/shard_map/psum | solution.py:123
  (52 shorter events, 20.0 us)
Async XLA Ops:
  7.2 309.3 %copy-start = (bf16[1,128,1024]{2,1,0:T(8,128)(2,1)S(1)}, bf16[1,128,1024]{2,1,0:T(8,128)(2,1)}, u32[]{:S(2)}) copy-start(bf16[1,128,1024]{2,1,0:T(8,128)(2,1)} %param.7) | copy-start | bytes 786436
  7.2 153.7 %copy-start.2 = (bf16[1,128,1024]{2,1,0:T(8,128)(2,1)S(1)}, bf16[1,128,1024]{2,1,0:T(8,128)(2,1)}, u32[]{:S(2)}) copy-start(bf16[1,128,1024]{2,1,0:T(8,128)(2,1)} %param.6) | copy-start | bytes 786436
  7.2 153.7 %all-gather.7.cloned.1.call-start = ((), (), s32[]{:S(2)}) async-start(), calls=%async_computation.2 | async-start | bytes 6488064 | tf_op jit(solution)/shard_map/all_gather | solution.py:30
  7.9 308.5 %all-gather.11.cloned.1.call-start = ((), (), s32[]{:S(2)}) async-start(), calls=%async_computation.4 | async-start | bytes 2162688 | tf_op jit(solution)/shard_map/all_gather | solution.py:50
  8.7 380.8 %all-gather.9.cloned.1.call-start = ((), (), s32[]{:S(2)}) async-start(), calls=%async_computation.3 | async-start | bytes 4718592 | tf_op jit(solution)/shard_map/all_gather | solution.py:36
  165.7 267.1 %all-gather.13.cloned.1.call-start = ((), (), s32[]{:S(2)}) async-start(), calls=%async_computation.5 | async-start | bytes 2359296 | tf_op jit(solution)/shard_map/all_gather | solution.py:64
  167.5 305.7 %all-gather.15.cloned.1.call-start = ((), (), s32[]{:S(2)}) async-start(), calls=%async_computation.6 | async-start | bytes 2359296 | tf_op jit(solution)/shard_map/all_gather | solution.py:65
  319.8 296.6 %reduce-scatter.5.cloned.1.call-start = ((), (), s32[]{:S(2)}) async-start(), calls=%async_computation.8 | async-start | bytes 2162688 | tf_op jit(solution)/shard_map/reduce_scatter | solution.py:114
  403.2 3.6 copy-start.1
  403.2 3.6 copy-start.3
  408.8 3.0 copy-start.5
  408.8 3.1 copy-start.4
  410.9 383.0 %reduce-scatter.3.cloned.1.call-start = ((), (), s32[]{:S(2)}) async-start(), calls=%async_computation.7 | async-start | bytes 6488064 | tf_op jit(solution)/shard_map/reduce_scatter | solution.py:105
  499.9 388.4 %all-reduce.3.cloned.1.call-start = ((), (), s32[]{:S(2)}) async-start(), calls=%async_computation.9 | async-start | bytes 524288 | tf_op jit(solution)/shard_map/psum | solution.py:123
Sparse Core Ops, SparseCore 0:
  9.8 151.0 all-gather.6
  162.7 153.6 all-gather.10
  318.3 71.1 all-gather.8
  391.2 41.5 all-gather.12
  434.5 38.6 all-gather.14
  475.5 140.8 reduce-scatter.4
  619.1 174.6 reduce-scatter.2
  796.7 91.4 all-reduce.2
where the time goes:
time: 899 us; the launch traced here: 898 us
  waiting for transfers between devices  770 us (86%)
  matrix products  53.5 us (6%)
  blocking collectives  32 us (4%)
  local copies, waits for them, and re-layouts  18.6 us (2%)
  between operations  15 us (2%)
  other arithmetic  9.07 us (1%)
    reduce_scatter x1, waiting for transfers between devices, body(): lax.psum_scatter(lax.dot_general(columns, dqkv, contract_first, preferred...  177 us
    all_gather x1, waiting for transfers between devices, body(): lax.all_gather(w_out, 'dp', axis=0, tiled=True)  149 us
    all_gather x1, waiting for transfers between devices, body(): full_qkv = lax.all_gather(w_qkv, 'dp', axis=0, tiled=True)  146 us
    reduce_scatter x1, waiting for transfers between devices, body(): lax.psum_scatter(lax.dot_general(columns, cot_flat, contract_first, prefe...  111 us
    psum x1, waiting for transfers between devices, body(): lax.psum(grad_q.astype(jnp.bfloat16), 'space').astype(jnp.float32)  93.5 us
    all_gather x1, waiting for transfers between devices, body(): lax.all_gather(qkv[..., channel_width:], 'space', axis=1, tiled=True)  68.8 us
    all_gather x1, waiting for transfers between devices, body(): q_wide = lax.all_gather(query_wide, 'space', axis=1, tiled=True)  20 us
  transfers between devices with their start and end apart: 8, of which 8 were waited for; matrix products, arithmetic and copies ran while one was open for 8% of the time, Pallas kernels for 0%

commit v1 on v0

v1 whole, which is shorter than its diff:
```python
import jax
import jax.numpy as jnp
from jax import lax
from jax.experimental import pallas as pl
from jax.experimental.pallas import tpu as pltpu
from jax.sharding import PartitionSpec as P

C = 1024
Z = 4
PAIR = 128
BLOCK = 256
F32 = jnp.float32
BF16 = jnp.bfloat16


def nt(a, b):
    return lax.dot_general(a, b, (((1,), (1,)), ((), ())), preferred_element_type=F32)


def tn(a, b):
    return lax.dot_general(a, b, (((0,), (0,)), ((), ())), preferred_element_type=F32)


def attention_kernel(qkv_ref, d_ref, att_ref, dqkv_ref, dk_acc, dv_acc):
    cells = qkv_ref.shape[0]
    lane = lax.broadcasted_iota(jnp.int32, (1, PAIR), 1)
    keep = [lane < PAIR // 2, lane >= PAIR // 2]
    dk_acc[...] = jnp.zeros_like(dk_acc)
    dv_acc[...] = jnp.zeros_like(dv_acc)
    k = qkv_ref[:, PAIR : 2 * PAIR]
    v = qkv_ref[:, 2 * PAIR :]

    @pl.loop(0, cells // BLOCK)
    def _(step):
        rows = pl.ds(pl.multiple_of(step * BLOCK, BLOCK), BLOCK)
        q = qkv_ref[rows, :PAIR] * jnp.bfloat16(0.125)
        d = d_ref[rows, :]
        zero = jnp.zeros_like(q)
        att, dq = jnp.zeros((BLOCK, PAIR), F32), jnp.zeros((BLOCK, PAIR), F32)
        dk, dv = dk_acc[...], dv_acc[...]
        for mine in keep:
            qh = jnp.where(mine, q, zero)
            dh = jnp.where(mine, d, zero)
            scores = nt(qh, k)
            e = jnp.exp(scores - jnp.max(scores, -1, keepdims=True))
            p = e * (1.0 / jnp.sum(e, -1, keepdims=True))
            pb = p.astype(BF16)
            o = jnp.dot(pb, v, preferred_element_type=F32).astype(BF16).astype(F32)
            att = jnp.where(mine, o, att)
            delta = jnp.sum(dh.astype(F32) * o, -1, keepdims=True)
            ds = (p * (nt(dh, v) - delta)).astype(BF16)
            dq = jnp.where(mine, jnp.dot(ds, k, preferred_element_type=F32), dq)
            dk = dk + tn(ds, qh)
            dv = dv + tn(pb, dh)
        dk_acc[...] = dk
        dv_acc[...] = dv
        att_ref[rows, :] = att.astype(BF16)
        dqkv_ref[rows, :PAIR] = (0.125 * dq).astype(BF16)

    dqkv_ref[:, PAIR : 2 * PAIR] = dk_acc[...].astype(BF16)
    dqkv_ref[:, 2 * PAIR :] = dv_acc[...].astype(BF16)


def attention(qkv, d_att):
    cells = qkv.shape[0]
    return pl.pallas_call(
        attention_kernel,
        out_shape=(
            jax.ShapeDtypeStruct((cells, PAIR), BF16),
            jax.ShapeDtypeStruct((cells, 3 * PAIR), BF16),
        ),
        scratch_shapes=[pltpu.VMEM((cells, PAIR), F32)] * 2,
        compiler_params=pltpu.CompilerParams(vmem_limit_bytes=48 * 2**20),
        cost_estimate=pl.CostEstimate(
            flops=2 * 6 * 2 * cells * cells * PAIR, bytes_accessed=2**21, transcendentals=2 * cells * cells
        ),
    )(qkv, d_att)


def turn(x, by):
    pairs = [(z * 2 + c, (z + by) % Z * 2 + c) for z in range(Z) for c in range(2)]
    return lax.ppermute(x, "space", pairs)


def swap(x):
    return lax.ppermute(x, "space", [(i, i ^ 1) for i in range(2 * Z)])


def transpose_devices(x):
    at = lambda t, y, s: (t * 4 + y) * 8 + s
    pairs = [(at(t, y, s), at(s, y, t)) for t in range(8) for y in range(4) for s in range(8)]
    return lax.ppermute(x, ("dp", "space"), pairs)


def gather_cells(x):
    mine = jnp.concatenate([x] + [turn(x, by) for by in range(1, Z)], 0)
    return jnp.concatenate([mine, swap(mine)], 0)


def body(images, cotangent, w_qkv, w_out, film, timesteps):
    rows = images.shape[1]
    place = lax.axis_index("space")
    w_rows = w_qkv.shape[0]
    w_part = lax.dynamic_slice_in_dim(w_qkv.reshape(w_rows, 3, 8, PAIR), place, 1, 2)
    w_part = w_part.reshape(w_rows, 3 * PAIR)
    o_part = transpose_devices(lax.dynamic_slice_in_dim(w_out, place * PAIR, PAIR, 1))
    part = jnp.concatenate([w_part, o_part], 1)
    parts = lax.all_to_all(
        jnp.broadcast_to(part[None], (32,) + part.shape), "dp", 0, 0, tiled=True
    )
    wq = parts[..., : 3 * PAIR].reshape(C, 3 * PAIR)
    wo = parts[..., 3 * PAIR :].reshape(8, 4 * w_rows, PAIR)
    wo = jnp.transpose(wo, (1, 0, 2)).reshape(4 * w_rows, C)

    feature_row = lax.dynamic_slice_in_dim(film, timesteps[0], 1, 0).astype(F32)
    xf = images[0].astype(F32)
    mean_x = jnp.mean(xf, -1, keepdims=True)
    centered = xf - mean_x
    inverse = lax.rsqrt(jnp.mean(centered * centered, -1, keepdims=True) + 1e-05)
    xhat = centered * inverse
    scale = 1.0 + feature_row[:, :C]
    normed = (xhat * scale + feature_row[:, C:]).astype(BF16)
    normed_all = gather_cells(normed)
    cot_all = gather_cells(cotangent[0])

    qkv = jnp.dot(normed_all, wq, preferred_element_type=F32).astype(BF16)
    d_att = nt(cot_all, wo).astype(BF16)
    att, dqkv = attention(qkv, d_att)

    partial = nt(dqkv, wq).astype(BF16)
    half = Z * rows
    chip = partial[:half].astype(F32) + swap(partial[half:]).astype(F32)
    dnormed = chip[:rows]
    for by in range(1, Z):
        dnormed = dnormed + turn(chip[by * rows : (by + 1) * rows].astype(BF16), Z - by).astype(F32)
    dxhat = dnormed * scale
    branch = inverse * (
        dxhat
        - jnp.mean(dxhat, -1, keepdims=True)
        - xhat * jnp.mean(dxhat * xhat, -1, keepdims=True)
    )

    gq = tn(normed_all, dqkv).astype(BF16).reshape(32, w_rows, 3 * PAIR)
    go = tn(att, cot_all).astype(BF16).reshape(4 * w_rows, 8, PAIR)
    go = jnp.transpose(go, (1, 0, 2)).reshape(32, w_rows, PAIR)
    sent = lax.all_to_all(jnp.concatenate([gq, go], -1), "dp", 0, 0, tiled=True)
    total = jnp.sum(sent.astype(F32), 0).astype(BF16)
    mine = jnp.concatenate([total[:, : 3 * PAIR], transpose_devices(total[:, 3 * PAIR :])], 1)
    every = lax.all_gather(mine, "space", axis=0, tiled=False).astype(F32)
    every = jnp.transpose(every.reshape(8, w_rows, 4, PAIR), (1, 2, 0, 3))
    grad_q = every[:, :3].reshape(w_rows, 3 * C)
    grad_o = every[:, 3].reshape(w_rows, C)
    return branch.astype(BF16)[None], grad_q, grad_o


def solution(mesh):
    return jax.shard_map(
        body,
        mesh=mesh,
        in_specs=(
            P("dp", "space", None),
            P("dp", "space", None),
            P("dp", None),
            P("dp", None),
            P(),
            P("dp"),
        ),
        out_specs=(P("dp", "space", None), P("dp", None), P("dp", None)),
        check_vma=False,
    )
```

time: 899 us -> 187 us (0.21)
  waiting for transfers between devices: 770 us -> 49.6 us
  starting transfers between devices: 0.32 us -> 65.9 us
  matrix products: 53.5 us -> 9.1 us
  between operations: 15 us -> 1.62 us
  Pallas kernels: 0 us -> 10.3 us
    all_gather x5 -> x0, waiting for transfers between devices: 386 us -> none  [the longest x1 149 us: body(): lax.all_gather(w_out, 'dp', axis=0, tiled=True)]
    reduce_scatter x2 -> x0, waiting for transfers between devices: 289 us -> none  [the longest x1 177 us: body(): lax.psum_scatter(lax.dot_general(columns, dqkv, contract_first, preferred...]
    psum x1 -> x0, waiting for transfers between devices: 93.5 us -> none  [body(): lax.psum(grad_q.astype(jnp.bfloat16), 'space').astype(jnp.float32)]
    ppermute x0 -> x14, waiting for transfers between devices: none -> 49.6 us  [the longest x9 49.3 us: turn(): return lax.ppermute(x, 'space', pairs)]
    dot_general x12 -> x5, matrix products: 53.5 us -> 9.1 us  [the longest x2 3.3 us: tn(): lax.dot_general(a, b, (((0,), (0,)), ((), ())), preferred_element_type=F32)]
    ppermute x0 -> x14, starting transfers between devices: none -> 40.1 us  [the longest x9 26.2 us: turn(): return lax.ppermute(x, 'space', pairs)]
    all_to_all x0 -> x2, starting transfers between devices: none -> 25.8 us  [the longest x1 18.9 us: body(): lax.all_to_all(jnp.broadcast_to(part[None], (32,) + part.shape), 'dp', 0,...]
    slice x8 -> x9, local copies, waits for them, and re-layouts: 14.9 us -> 2.51 us  [the longest x1 1.07 us: body(): chip = partial[:half].astype(F32) + swap(partial[half:]).astype(F32)]
  transfers between devices with their start and end apart: 8 -> 16, of which waited for: 8 -> 7; matrix products, arithmetic and copies ran while one was open for 8% -> 10% of each run, Pallas kernels for 0% -> 0%
where the time goes in v1:
time: 187 us; the launch traced here: 186 us
  starting transfers between devices  65.9 us (35%)
  waiting for transfers between devices  49.6 us (27%)
  blocking collectives  27.3 us (15%)
  local copies, waits for them, and re-layouts  16.6 us (9%)
  Pallas kernels  10.3 us (6%)
  matrix products  9.1 us (5%)
  other arithmetic  5.74 us (3%)
    ppermute x9, waiting for transfers between devices, turn(): return lax.ppermute(x, 'space', pairs)  49.3 us
    all_gather x1, blocking collectives, body(): every = lax.all_gather(mine, 'space', axis=0, tiled=False).astype(F32)  27.3 us
    ppermute x9, starting transfers between devices, turn(): return lax.ppermute(x, 'space', pairs)  26.2 us
    all_to_all x1, starting transfers between devices, body(): lax.all_to_all(jnp.broadcast_to(part[None], (32,) + part.shape), 'dp', 0,...  18.9 us
    ppermute x2, starting transfers between devices, transpose_devices(): return lax.ppermute(x, ('dp', 'space'), pairs)  11.2 us
    pallas_call x1, Pallas kernels, attention(): pl.pallas_call(attention_kernel, out_shape=(jax.ShapeDtypeStruct((cells,...  10.3 us
    unnamed x26, local copies, waits for them, and re-layouts  9.68 us
    all_to_all x1, starting transfers between devices, body(): sent = lax.all_to_all(jnp.concatenate([gq, go], -1), 'dp', 0, 0, tiled=True)  6.94 us
  transfers between devices with their start and end apart: 16, of which 7 were waited for; matrix products, arithmetic and copies ran while one was open for 10% of the time, Pallas kernels for 0%

profile of v1, /device:TPU:1, one launch (start us, length us, event | category | flops | bytes accessed | tf_op | source)
XLA Modules:
  0.0 186.1 jit_solution(6477593780806336042)
XLA Ops:
  0.6 6.9 %collective-permute-start.7 = (bf16[128,1024]{1,0:T(8,128)(2,1)}, bf16[128,1024]{1,0:T(8,128)(2,1)S(1)}, u32[]{:S(2)}, u32[]{:S(2)}) collective-permute-start(bf16[128,1024]{1,0:T(8,128)(2,1)} %bitcast.89), channel_id=1, source_target_pairs={{0,6},{1,7},{2,0},{3,1},{4,2},{5,3},{6,4},{7,5},{8,14},{9,15},{10,... | collective-permute-start | bytes 786440 | tf_op jit(solution)/shard_map/ppermute | solution.py:82
  8.6 2.3 %collective-permute-start.5 = (bf16[128,1024]{1,0:T(8,128)(2,1)}, bf16[128,1024]{1,0:T(8,128)(2,1)S(1)}, u32[]{:S(2)}, u32[]{:S(2)}) collective-permute-start(bf16[128,1024]{1,0:T(8,128)(2,1)} %bitcast.91), channel_id=1, source_target_pairs={{0,2},{1,3},{2,4},{3,5},{4,6},{5,7},{6,0},{7,1},{8,10},{9,11},{10,... | collective-permute-start | bytes 786440 | tf_op jit(solution)/shard_map/ppermute | solution.py:82
  10.8 4.5 %collective-permute-start.4 = (bf16[32,128]{1,0:T(8,128)(2,1)S(1)}, bf16[32,128]{1,0:T(8,128)(2,1)S(1)}, u32[]{:S(2)}, u32[]{:S(2)}) collective-permute-start(bf16[32,128]{1,0:T(8,128)(2,1)S(1)} %constant_dynamic-slice_fusion), channel_id=1, source_target_pairs={{0,0},{1,32},{2,64},{3,96},{4,128},{5,160},{6,192},{7,224},{8,8},{... | collective-permute-start | bytes 24584 | tf_op jit(solution)/shard_map/ppermute | solution.py:92
  20.5 18.9 %all-to-all-start = ((bf16[32,32,512]{2,1,0:T(8,128)(2,1)}), bf16[32,32,512]{2,1,0:T(8,128)(2,1)S(1)}, u32[]{:S(2)}, u32[]{:S(2)}) async-start(bf16[32,32,512]{2,1,0:T(8,128)(2,1)} %broadcast_in_dim.4), calls=%async_computation | async-start | bytes 2097152 | tf_op jit(solution)/shard_map/all_to_all | solution.py:108
  40.4 7.3 %collective-permute-start.2 = (bf16[128,1024]{0,1:T(8,128)(2,1)S(1)}, bf16[128,1024]{0,1:T(8,128)(2,1)S(1)}, u32[]{:S(2)}, u32[]{:S(2)}) collective-permute-start(bf16[128,1024]{0,1:T(8,128)(2,1)S(1)} %get-tuple-element.20), channel_id=1, source_target_pairs={{0,6},{1,7},{2,0},{3,1},{4,2},{5,3},{6,4},{7,5},{8,14},{9,15},{10,... | collective-permute-start | bytes 786440 | tf_op jit(solution)/shard_map/ppermute | solution.py:82
  47.8 2.2 %collective-permute-start = (bf16[128,1024]{0,1:T(8,128)(2,1)S(1)}, bf16[128,1024]{0,1:T(8,128)(2,1)S(1)}, u32[]{:S(2)}, u32[]{:S(2)}) collective-permute-start(bf16[128,1024]{0,1:T(8,128)(2,1)S(1)} %get-tuple-element.20), channel_id=1, source_target_pairs={{0,2},{1,3},{2,4},{3,5},{4,6},{5,7},{6,0},{7,1},{8,10},{9,11},{10,... | collective-permute-start | bytes 786440 | tf_op jit(solution)/shard_map/ppermute | solution.py:82
  50.1 1.6 collective-permute-start.8
  51.7 1.5 collective-permute-done.2
  53.2 16.9 %collective-permute-done.1 = bf16[128,1024]{0,1:T(8,128)(2,1)S(1)} collective-permute-done((bf16[128,1024]{0,1:T(8,128)(2,1)S(1)}, bf16[128,1024]{0,1:T(8,128)(2,1)S(1)}, u32[]{:S(2)}, u32[]{:S(2)}) %collective-permute-start.1) | collective-permute-done | bytes 262176 | tf_op jit(solution)/shard_map/ppermute | solution.py:82
  70.1 11.1 %collective-permute-done = bf16[128,1024]{0,1:T(8,128)(2,1)S(1)} collective-permute-done((bf16[128,1024]{0,1:T(8,128)(2,1)S(1)}, bf16[128,1024]{0,1:T(8,128)(2,1)S(1)}, u32[]{:S(2)}, u32[]{:S(2)}) %collective-permute-start) | collective-permute-done | bytes 262176 | tf_op jit(solution)/shard_map/ppermute | solution.py:82
  89.6 1.8 copy.19
  91.4 1.6 convolution_convert_fusion.4.d_ref
  93.1 2.9 %convolution_convert_fusion.2.qkv_ref = bf16[1024,384]{1,0:T(8,128)(2,1)S(1)} fusion(bf16[1024,1024]{0,1:T(8,128)(2,1)} %constant_dynamic-update-slice_fusion, bf16[1024,384]{1,0:T(8,128)(2,1)S(1)} %bitcast.94), kind=kOutput, calls=%fused_computation.3 | convolution fusion | flops 805699584 | bytes 3670016 | tf_op jit(solution)/shard_map/dot_general | solution.py:126
  96.0 10.3 %shard_map.85 = (bf16[1024,128]{1,0:T(8,128)(2,1)S(1)}, bf16[1024,384]{1,0:T(8,128)(2,1)S(1)}) custom-call(bf16[1024,384]{1,0:T(8,128)(2,1)S(1)} %convolution_convert_fusion.2.qkv_ref, bf16[1024,128]{1,0:T(8,128)(2,1)S(1)} %convolution_convert_fusion.4.d_ref), custom_call_target="tpu_custom_call" | custom-call | flops 3221225472 | bytes 2097152 | tf_op jit(solution)/shard_map/pallas_call | solution.py:66
  109.3 2.8 %convolution_convert_fusion.1 = bf16[1024,384]{1,0:T(8,128)(2,1)S(1)} fusion(bf16[1024,1024]{0,1:T(8,128)(2,1)} %constant_dynamic-update-slice_fusion, bf16[1024,384]{1,0:T(8,128)(2,1)S(1)} %get-tuple-element.5), kind=kOutput, calls=%fused_computation.2 | convolution fusion | flops 805699584 | bytes 3670016 | tf_op jit(solution)/shard_map/dot_general | solution.py:21
  113.2 6.9 %all-to-all-start.1 = ((bf16[32,32,512]{2,1,0:T(8,128)(2,1)}), bf16[32,32,512]{2,1,0:T(8,128)(2,1)S(1)}, u32[]{:S(2)}, u32[]{:S(2)}) async-start(bf16[32,32,512]{2,1,0:T(8,128)(2,1)} %pad_maximum_fusion.2), calls=%async_computation.1 | async-start | bytes 2097152 | tf_op jit(solution)/shard_map/all_to_all | solution.py:146
  120.2 1.7 convert_add_fusion
  122.8 2.5 %collective-permute-start.12 = (bf16[128,1024]{0,1:T(8,128)(2,1)S(1)}, bf16[128,1024]{0,1:T(8,128)(2,1)S(1)}, u32[]{:S(2)}, u32[]{:S(2)}) collective-permute-start(bf16[128,1024]{0,1:T(8,128)(2,1)S(1)} %get-tuple-element.24), channel_id=1, source_target_pairs={{0,2},{1,3},{2,4},{3,5},{4,6},{5,7},{6,0},{7,1},{8,10},{9,11},{10,... | collective-permute-start | bytes 786440 | tf_op jit(solution)/shard_map/ppermute | solution.py:82
  125.2 3.2 %collective-permute-start.11 = (bf16[128,1024]{0,1:T(8,128)(2,1)S(1)}, bf16[128,1024]{0,1:T(8,128)(2,1)S(1)}, u32[]{:S(2)}, u32[]{:S(2)}) collective-permute-start(bf16[128,1024]{0,1:T(8,128)(2,1)S(1)} %get-tuple-element.25), channel_id=1, source_target_pairs={{0,4},{1,5},{2,6},{3,7},{4,0},{5,1},{6,2},{7,3},{8,12},{9,13},{10,... | collective-permute-start | bytes 786440 | tf_op jit(solution)/shard_map/ppermute | solution.py:82
  128.4 2.7 %collective-permute-done.10 = bf16[128,1024]{0,1:T(8,128)(2,1)S(1)} collective-permute-done((bf16[128,1024]{0,1:T(8,128)(2,1)S(1)}, bf16[128,1024]{0,1:T(8,128)(2,1)S(1)}, u32[]{:S(2)}, u32[]{:S(2)}) %collective-permute-start.10) | collective-permute-done | bytes 262176 | tf_op jit(solution)/shard_map/ppermute | solution.py:82
  131.1 13.4 %collective-permute-done.12 = bf16[128,1024]{0,1:T(8,128)(2,1)S(1)} collective-permute-done((bf16[128,1024]{0,1:T(8,128)(2,1)S(1)}, bf16[128,1024]{0,1:T(8,128)(2,1)S(1)}, u32[]{:S(2)}, u32[]{:S(2)}) %collective-permute-start.12) | collective-permute-done | bytes 262176 | tf_op jit(solution)/shard_map/ppermute | solution.py:82
  144.5 3.7 %collective-permute-done.11 = bf16[128,1024]{0,1:T(8,128)(2,1)S(1)} collective-permute-done((bf16[128,1024]{0,1:T(8,128)(2,1)S(1)}, bf16[128,1024]{0,1:T(8,128)(2,1)S(1)}, u32[]{:S(2)}, u32[]{:S(2)}) %collective-permute-start.11) | collective-permute-done | bytes 262176 | tf_op jit(solution)/shard_map/ppermute | solution.py:82
  148.7 6.7 %collective-permute-start.13 = (bf16[32,128]{1,0:T(8,128)(2,1)S(1)}, bf16[32,128]{1,0:T(8,128)(2,1)S(1)}, u32[]{:S(2)}, u32[]{:S(2)}) collective-permute-start(bf16[32,128]{1,0:T(8,128)(2,1)S(1)} %slice.70), channel_id=1, source_target_pairs={{0,0},{1,32},{2,64},{3,96},{4,128},{5,160},{6,192},{7,224},{8,8},{... | collective-permute-start | bytes 24584 | tf_op jit(solution)/shard_map/ppermute | solution.py:92
  156.7 27.3 %all-gather = bf16[256,512]{1,0:T(8,128)(2,1)S(1)} all-gather(bf16[32,512]{1,0:T(8,128)(2,1)S(1)} %pad_maximum_fusion.4), channel_id=2, replica_groups=mesh['dp'=32,'space'=8] {'space'}, dimensions={0}, use_global_device_ids=true | all-gather | bytes 294912 | tf_op jit(solution)/shard_map/all_gather | solution.py:149
  (75 shorter events, 23.8 us)
Async XLA Ops:
  0.6 10.2 %copy-start = (bf16[32,1024]{1,0:T(8,128)(2,1)S(1)}, bf16[32,1024]{1,0:T(8,128)(2,1)}, u32[]{:S(2)}) copy-start(bf16[32,1024]{1,0:T(8,128)(2,1)} %param.9) | copy-start | bytes 196612
  0.6 47.2 %collective-permute-start.7 = (bf16[128,1024]{1,0:T(8,128)(2,1)}, bf16[128,1024]{1,0:T(8,128)(2,1)S(1)}, u32[]{:S(2)}, u32[]{:S(2)}) collective-permute-start(bf16[128,1024]{1,0:T(8,128)(2,1)} %bitcast.89), channel_id=1, source_target_pairs={{0,6},{1,7},{2,0},{3,1},{4,2},{5,3},{6,4},{7,5},{8,14},{9,15},{10,... | collective-permute-start | bytes 786440 | tf_op jit(solution)/shard_map/ppermute | solution.py:82
  7.6 42.4 %collective-permute-start.6 = (bf16[128,1024]{1,0:T(8,128)(2,1)}, bf16[128,1024]{1,0:T(8,128)(2,1)S(1)}, u32[]{:S(2)}, u32[]{:S(2)}) collective-permute-start(bf16[128,1024]{1,0:T(8,128)(2,1)} %bitcast.90), channel_id=1, source_target_pairs={{0,4},{1,5},{2,6},{3,7},{4,0},{5,1},{6,2},{7,3},{8,12},{9,13},{10,... | collective-permute-start | bytes 786440 | tf_op jit(solution)/shard_map/ppermute | solution.py:82
  8.6 41.5 %collective-permute-start.5 = (bf16[128,1024]{1,0:T(8,128)(2,1)}, bf16[128,1024]{1,0:T(8,128)(2,1)S(1)}, u32[]{:S(2)}, u32[]{:S(2)}) collective-permute-start(bf16[128,1024]{1,0:T(8,128)(2,1)} %bitcast.91), channel_id=1, source_target_pairs={{0,2},{1,3},{2,4},{3,5},{4,6},{5,7},{6,0},{7,1},{8,10},{9,11},{10,... | collective-permute-start | bytes 786440 | tf_op jit(solution)/shard_map/ppermute | solution.py:82
  10.8 8.5 %collective-permute-start.4 = (bf16[32,128]{1,0:T(8,128)(2,1)S(1)}, bf16[32,128]{1,0:T(8,128)(2,1)S(1)}, u32[]{:S(2)}, u32[]{:S(2)}) collective-permute-start(bf16[32,128]{1,0:T(8,128)(2,1)S(1)} %constant_dynamic-slice_fusion), channel_id=1, source_target_pairs={{0,0},{1,32},{2,64},{3,96},{4,128},{5,160},{6,192},{7,224},{8,8},{... | collective-permute-start | bytes 24584 | tf_op jit(solution)/shard_map/ppermute | solution.py:92
  19.2 30.8 %copy-start.1 = (bf16[1,128,1024]{2,1,0:T(8,128)(2,1)S(1)}, bf16[1,128,1024]{2,1,0:T(8,128)(2,1)}, u32[]{:S(2)}) copy-start(bf16[1,128,1024]{2,1,0:T(8,128)(2,1)} %param.7) | copy-start | bytes 786436
  20.5 68.3 %all-to-all-start = ((bf16[32,32,512]{2,1,0:T(8,128)(2,1)}), bf16[32,32,512]{2,1,0:T(8,128)(2,1)S(1)}, u32[]{:S(2)}, u32[]{:S(2)}) async-start(bf16[32,32,512]{2,1,0:T(8,128)(2,1)} %broadcast_in_dim.4), calls=%async_computation | async-start | bytes 2097152 | tf_op jit(solution)/shard_map/all_to_all | solution.py:108
  40.4 42.0 %copy-start.2 = (bf16[1,128,1024]{2,1,0:T(8,128)(2,1)S(1)}, bf16[1,128,1024]{2,1,0:T(8,128)(2,1)}, u32[]{:S(2)}) copy-start(bf16[1,128,1024]{2,1,0:T(8,128)(2,1)} %param.7) | copy-start | bytes 786436
  40.4 12.8 %collective-permute-start.2 = (bf16[128,1024]{0,1:T(8,128)(2,1)S(1)}, bf16[128,1024]{0,1:T(8,128)(2,1)S(1)}, u32[]{:S(2)}, u32[]{:S(2)}) collective-permute-start(bf16[128,1024]{0,1:T(8,128)(2,1)S(1)} %get-tuple-element.20), channel_id=1, source_target_pairs={{0,6},{1,7},{2,0},{3,1},{4,2},{5,3},{6,4},{7,5},{8,14},{9,15},{10,... | collective-permute-start | bytes 786440 | tf_op jit(solution)/shard_map/ppermute | solution.py:82
  47.8 22.3 %collective-permute-start.1 = (bf16[128,1024]{0,1:T(8,128)(2,1)S(1)}, bf16[128,1024]{0,1:T(8,128)(2,1)S(1)}, u32[]{:S(2)}, u32[]{:S(2)}) collective-permute-start(bf16[128,1024]{0,1:T(8,128)(2,1)S(1)} %get-tuple-element.20), channel_id=1, source_target_pairs={{0,4},{1,5},{2,6},{3,7},{4,0},{5,1},{6,2},{7,3},{8,12},{9,13},{10,... | collective-permute-start | bytes 786440 | tf_op jit(solution)/shard_map/ppermute | solution.py:82
  47.8 33.5 %copy-start.3 = (bf16[128,1024]{1,0:T(8,128)(2,1)}, bf16[128,1024]{1,0:T(8,128)(2,1)S(1)}, u32[]{:S(2)}) copy-start(bf16[128,1024]{1,0:T(8,128)(2,1)S(1)} %collective-permute-done.7) | copy-start | bytes 786436
  47.8 33.4 %collective-permute-start = (bf16[128,1024]{0,1:T(8,128)(2,1)S(1)}, bf16[128,1024]{0,1:T(8,128)(2,1)S(1)}, u32[]{:S(2)}, u32[]{:S(2)}) collective-permute-start(bf16[128,1024]{0,1:T(8,128)(2,1)S(1)} %get-tuple-element.20), channel_id=1, source_target_pairs={{0,2},{1,3},{2,4},{3,5},{4,6},{5,7},{6,0},{7,1},{8,10},{9,11},{10,... | collective-permute-start | bytes 786440 | tf_op jit(solution)/shard_map/ppermute | solution.py:82
  50.0 31.3 %copy-start.4 = (bf16[128,1024]{1,0:T(8,128)(2,1)}, bf16[128,1024]{1,0:T(8,128)(2,1)S(1)}, u32[]{:S(2)}) copy-start(bf16[128,1024]{1,0:T(8,128)(2,1)S(1)} %collective-permute-done.6) | copy-start | bytes 786436
  50.0 31.3 %copy-start.5 = (bf16[128,1024]{1,0:T(8,128)(2,1)}, bf16[128,1024]{1,0:T(8,128)(2,1)S(1)}, u32[]{:S(2)}) copy-start(bf16[128,1024]{1,0:T(8,128)(2,1)S(1)} %collective-permute-done.5) | copy-start | bytes 786436
  50.1 37.5 %collective-permute-start.8 = (bf16[512,1024]{1,0:T(8,128)(2,1)S(1)}, bf16[512,1024]{1,0:T(8,128)(2,1)S(1)}, u32[]{:S(2)}, u32[]{:S(2)}) collective-permute-start(bf16[512,1024]{1,0:T(8,128)(2,1)S(1)} %pad_maximum_fusion.1), channel_id=1, source_target_pairs={{0,1},{1,0},{2,3},{3,2},{4,5},{5,4},{6,7},{7,6},{8,9},{9,8},{10,11... | collective-permute-start | bytes 3145736 | tf_op jit(solution)/shard_map/ppermute | solution.py:86
  81.3 6.4 %collective-permute-start.3 = (bf16[512,1024]{0,1:T(8,128)(2,1)S(1)}, bf16[512,1024]{0,1:T(8,128)(2,1)S(1)}, u32[]{:S(2)}, u32[]{:S(2)}) collective-permute-start(bf16[512,1024]{0,1:T(8,128)(2,1)S(1)} %pad_maximum_fusion), channel_id=1, source_target_pairs={{0,1},{1,0},{2,3},{3,2},{4,5},{5,4},{6,7},{7,6},{8,9},{9,8},{10,11... | collective-permute-start | bytes 3145736 | tf_op jit(solution)/shard_map/ppermute | solution.py:86
  109.2 10.9 %collective-permute-start.9 = (bf16[512,1024]{0,1:T(8,128)(2,1)}, bf16[512,1024]{0,1:T(8,128)(2,1)}, u32[]{:S(2)}, u32[]{:S(2)}) collective-permute-start(bf16[512,1024]{0,1:T(8,128)(2,1)} %slice.64), channel_id=1, source_target_pairs={{0,1},{1,0},{2,3},{3,2},{4,5},{5,4},{6,7},{7,6},{8,9},{9,8},{10,11... | collective-permute-start | bytes 3145736 | tf_op jit(solution)/shard_map/ppermute | solution.py:86
  113.2 35.3 %all-to-all-start.1 = ((bf16[32,32,512]{2,1,0:T(8,128)(2,1)}), bf16[32,32,512]{2,1,0:T(8,128)(2,1)S(1)}, u32[]{:S(2)}, u32[]{:S(2)}) async-start(bf16[32,32,512]{2,1,0:T(8,128)(2,1)} %pad_maximum_fusion.2), calls=%async_computation.1 | async-start | bytes 2097152 | tf_op jit(solution)/shard_map/all_to_all | solution.py:146
  122.0 9.1 %collective-permute-start.10 = (bf16[128,1024]{0,1:T(8,128)(2,1)S(1)}, bf16[128,1024]{0,1:T(8,128)(2,1)S(1)}, u32[]{:S(2)}, u32[]{:S(2)}) collective-permute-start(bf16[128,1024]{0,1:T(8,128)(2,1)S(1)} %get-tuple-element.23), channel_id=1, source_target_pairs={{0,6},{1,7},{2,0},{3,1},{4,2},{5,3},{6,4},{7,5},{8,14},{9,15},{10,... | collective-permute-start | bytes 786440 | tf_op jit(solution)/shard_map/ppermute | solution.py:82
  122.8 21.8 %collective-permute-start.12 = (bf16[128,1024]{0,1:T(8,128)(2,1)S(1)}, bf16[128,1024]{0,1:T(8,128)(2,1)S(1)}, u32[]{:S(2)}, u32[]{:S(2)}) collective-permute-start(bf16[128,1024]{0,1:T(8,128)(2,1)S(1)} %get-tuple-element.24), channel_id=1, source_target_pairs={{0,2},{1,3},{2,4},{3,5},{4,6},{5,7},{6,0},{7,1},{8,10},{9,11},{10,... | collective-permute-start | bytes 786440 | tf_op jit(solution)/shard_map/ppermute | solution.py:82
  125.2 23.0 %collective-permute-start.11 = (bf16[128,1024]{0,1:T(8,128)(2,1)S(1)}, bf16[128,1024]{0,1:T(8,128)(2,1)S(1)}, u32[]{:S(2)}, u32[]{:S(2)}) collective-permute-start(bf16[128,1024]{0,1:T(8,128)(2,1)S(1)} %get-tuple-element.25), channel_id=1, source_target_pairs={{0,4},{1,5},{2,6},{3,7},{4,0},{5,1},{6,2},{7,3},{8,12},{9,13},{10,... | collective-permute-start | bytes 786440 | tf_op jit(solution)/shard_map/ppermute | solution.py:82
  148.7 8.1 %collective-permute-start.13 = (bf16[32,128]{1,0:T(8,128)(2,1)S(1)}, bf16[32,128]{1,0:T(8,128)(2,1)S(1)}, u32[]{:S(2)}, u32[]{:S(2)}) collective-permute-start(bf16[32,128]{1,0:T(8,128)(2,1)S(1)} %slice.70), channel_id=1, source_target_pairs={{0,0},{1,32},{2,64},{3,96},{4,128},{5,160},{6,192},{7,224},{8,8},{... | collective-permute-start | bytes 24584 | tf_op jit(solution)/shard_map/ppermute | solution.py:92

commit v2 on v1

v2 whole, which is shorter than its diff:
```python
import jax
import jax.numpy as jnp
from jax import lax
from jax.experimental import pallas as pl
from jax.experimental.pallas import tpu as pltpu
from jax.sharding import PartitionSpec as P

C = 1024
Z = 4
XY = 16
ROWS = 32
CELLS = 128
PAIR = 128
QKV = 3 * PAIR
PIECES = 10
BLOCK = 256
F32 = jnp.float32
BF16 = jnp.bfloat16
FAR = pl.BlockSpec(memory_space=pltpu.HBM)
WHOLE = pl.BlockSpec(memory_space=pltpu.VMEM)
SCALARS = pl.BlockSpec(memory_space=pltpu.SMEM)
CHEAP = pl.CostEstimate(flops=0, bytes_accessed=0, transcendentals=0)
SMALL = pltpu.CompilerParams(vmem_limit_bytes=8 * 2**20)
PARAMS = pltpu.CompilerParams(vmem_limit_bytes=58 * 2**20)


def nt(a, b):
    return lax.dot_general(a, b, (((1,), (1,)), ((), ())), preferred_element_type=F32)


def tn(a, b):
    return lax.dot_general(a, b, (((0,), (0,)), ((), ())), preferred_element_type=F32)


def nn(a, b):
    return jnp.dot(a, b, preferred_element_type=F32)


def struct(shape, dtype=BF16):
    return jax.ShapeDtypeStruct(shape, dtype)


def heads():
    lane = lax.broadcasted_iota(jnp.int32, (1, PAIR), 1)
    return lane < PAIR // 2, lane >= PAIR // 2


def load(pieces, whole, sems):
    copies, at = [], 0
    for i, piece in enumerate(pieces):
        rows = piece.shape[0]
        copies.append(pltpu.make_async_copy(piece, whole.at[at : at + rows, :], sems.at[i]))
        at += rows
    for copy in copies:
        copy.start()
    return copies


def attention_kernel(where, *refs):
    pieces, parts, rest = refs[:PIECES], refs[PIECES : PIECES + 4], refs[PIECES + 4 :]
    dqkv, wq, sent, x, qkv, wo, att, d_att, dk_acc, dv_acc, sems = rest
    copies = load(pieces, x, sems)
    for far, part in enumerate(parts):
        col = lax.rem(where[2] - far + 4, 4)
        for lo in range(2):
            half = slice(lo * ROWS, (lo + 1) * ROWS)
            columns = pl.ds(pl.multiple_of((lo * 4 + col) * PAIR, PAIR), PAIR)
            for y in range(4):
                at = pl.multiple_of(((lo * 4 + col) * 4 + y) * ROWS, ROWS)
                wq[pl.ds(at, ROWS), :] = part[y, half, :QKV]
                wo[y * ROWS : (y + 1) * ROWS, columns] = part[y, half, QKV:]
    for copy in copies:
        copy.wait()
    qkv[...] = nn(x[:, :C], wq[...]).astype(BF16)
    d_att[...] = nt(x[:, C:], wo[...]).astype(BF16)
    dk_acc[...] = jnp.zeros_like(dk_acc)
    dv_acc[...] = jnp.zeros_like(dv_acc)
    k = qkv[:, PAIR : 2 * PAIR]
    v = qkv[:, 2 * PAIR :]

    @pl.loop(0, qkv.shape[0] // BLOCK)
    def _(step):
        rows = pl.ds(pl.multiple_of(step * BLOCK, BLOCK), BLOCK)
        q = qkv[rows, :PAIR] * jnp.bfloat16(0.125)
        d = d_att[rows, :]
        zero = jnp.zeros_like(q)
        a, dq = jnp.zeros((BLOCK, PAIR), F32), jnp.zeros((BLOCK, PAIR), F32)
        dk, dv = dk_acc[...], dv_acc[...]
        for mine in heads():
            qh = jnp.where(mine, q, zero)
            dh = jnp.where(mine, d, zero)
            scores = nt(qh, k)
            e = jnp.exp(scores - jnp.max(scores, -1, keepdims=True))
            p = e * (1.0 / jnp.sum(e, -1, keepdims=True))
            pb = p.astype(BF16)
            o = nn(pb, v).astype(BF16).astype(F32)
            a = jnp.where(mine, o, a)
            delta = jnp.sum(dh.astype(F32) * o, -1, keepdims=True)
            ds = (p * (nt(dh, v) - delta)).astype(BF16)
            dq = jnp.where(mine, nn(ds, k), dq)
            dk = dk + tn(ds, qh)
            dv = dv + tn(pb, dh)
        dk_acc[...] = dk
        dv_acc[...] = dv
        att[rows, :] = a.astype(BF16)
        dqkv[rows, :PAIR] = (0.125 * dq).astype(BF16)

    dqkv[:, PAIR : 2 * PAIR] = dk_acc[...].astype(BF16)
    dqkv[:, 2 * PAIR :] = dv_acc[...].astype(BF16)
    grad = tn(x[:, :C], dqkv[...]).astype(BF16)
    for lo in range(2):
        for xy in range(XY):
            at = (lo * XY + xy) * ROWS
            sent[xy, lo * ROWS : (lo + 1) * ROWS, :QKV] = grad[at : at + ROWS, :]
    grad = tn(att[...], x[:, C:]).astype(BF16)
    for xy in range(XY):
        x, y = divmod(xy, 4)
        for lo in range(2):
            at = (lo * 4 + x) * PAIR
            sent[xy, lo * ROWS : (lo + 1) * ROWS, QKV:] = grad[
                y * ROWS : (y + 1) * ROWS, at : at + PAIR
            ]


def attention(where, pieces, parts):
    cells = 8 * CELLS
    return pl.pallas_call(
        attention_kernel,
        in_specs=[SCALARS] + [FAR] * PIECES + [WHOLE] * 4,
        out_shape=(
            struct((cells, QKV)),
            struct((C, QKV)),
            struct((XY, 2 * ROWS, QKV + PAIR)),
        ),
        scratch_shapes=[
            pltpu.VMEM((cells, 2 * C), BF16),
            pltpu.VMEM((cells, QKV), BF16),
            pltpu.VMEM((PAIR, C), BF16),
            pltpu.VMEM((cells, PAIR), BF16),
            pltpu.VMEM((cells, PAIR), BF16),
            pltpu.VMEM((cells, PAIR), F32),
            pltpu.VMEM((cells, PAIR), F32),
            pltpu.SemaphoreType.DMA((PIECES,)),
        ],
        compiler_params=PARAMS,
        cost_estimate=pl.CostEstimate(
            flops=2**34, bytes_accessed=2**23, transcendentals=2 * cells * cells
        ),
    )(where, *pieces, *parts)


def dnormed_kernel(dqkv, wq, out, *mine):
    half = Z * CELLS
    out[...] = nt(dqkv[half:, :], wq[...]).astype(BF16)
    for i, piece in enumerate(mine):
        piece[...] = nt(dqkv[i * CELLS : (i + 1) * CELLS, :], wq[...]).astype(BF16)


def dnormed_terms(dqkv, wq):
    return pl.pallas_call(
        dnormed_kernel,
        out_shape=(struct((Z * CELLS, C)), *[struct((CELLS, C))] * Z),
        compiler_params=PARAMS,
        cost_estimate=CHEAP,
    )(dqkv, wq)


def normalize(image, row):
    xf = image.astype(F32)
    centered = xf - jnp.mean(xf, -1, keepdims=True)
    inverse = lax.rsqrt(jnp.mean(centered * centered, -1, keepdims=True) + 1e-05)
    return centered * inverse, inverse, 1.0 + row[:, :C].astype(F32)


def prepare_kernel(where, image, cot, row, w_qkv, w_out, x, w_part, o_part):
    xhat, _, scale = normalize(image[...], row[...])
    x[:, :C] = (xhat * scale + row[:, C:].astype(F32)).astype(BF16)
    x[:, C:] = cot[...]
    for part in range(3):
        at = pl.multiple_of(part * C + where[0] * PAIR, PAIR)
        w_part[:, part * PAIR : (part + 1) * PAIR] = w_qkv[:, pl.ds(at, PAIR)]
    for lo in range(2):
        at = pl.multiple_of(lo * 4 * PAIR + lax.rem(where[0], 4) * PAIR, PAIR)
        o_part[lo * ROWS : (lo + 1) * ROWS, :] = w_out[:, pl.ds(at, PAIR)]


def prepare(where, image, cot, row, w_qkv, w_out):
    return pl.pallas_call(
        prepare_kernel,
        in_specs=[SCALARS] + [WHOLE] * 5,
        out_shape=(
            struct((CELLS, 2 * C)),
            struct((ROWS, QKV)),
            struct((2 * ROWS, PAIR)),
        ),
        cost_estimate=CHEAP,
        compiler_params=PARAMS,
    )(where, image, cot, row, w_qkv, w_out)


def pack_kernel(where, w_part, w_far, o_part, packed):
    low = where[1] == 0
    near, far = w_part[...], w_far[...]
    packed[:ROWS, :QKV] = jnp.where(low, near, far)
    packed[ROWS:, :QKV] = jnp.where(low, far, near)
    packed[:, QKV:] = o_part[...]


def pack(where, w_part, w_far, o_part):
    return pl.pallas_call(
        pack_kernel,
        in_specs=[SCALARS] + [WHOLE] * 3,
        out_shape=struct((2 * ROWS, QKV + PAIR)),
        cost_estimate=CHEAP,
        compiler_params=SMALL,
    )(where, w_part, w_far, o_part)


def join_kernel(where, *refs):
    pieces, joined = refs[:-1], refs[-1]
    for far, piece in enumerate(pieces):
        joined[lax.rem(where[3] - far + 4, 4)] = piece[...]


def join(where, pieces):
    return pl.pallas_call(
        join_kernel,
        in_specs=[SCALARS] + [WHOLE] * 4,
        out_shape=struct((4, 2 * ROWS, QKV + PAIR)),
        cost_estimate=CHEAP,
        compiler_params=SMALL,
    )(where, *pieces)


def total_kernel(where, sent, near, far, go):
    total = sent[0].astype(F32)
    for xy in range(1, XY):
        total = total + sent[xy].astype(F32)
    go[...] = total[:, QKV:].astype(BF16)
    low = where[1] == 0
    first, second = total[:ROWS, :QKV], total[ROWS:, :QKV]
    near[...] = jnp.where(low, first, second)
    far[...] = jnp.where(low, second, first).astype(BF16)


def add_up(where, sent):
    return pl.pallas_call(
        total_kernel,
        in_specs=[SCALARS, WHOLE],
        out_shape=(struct((ROWS, QKV), F32), struct((ROWS, QKV)), struct((2 * ROWS, PAIR))),
        cost_estimate=CHEAP,
        compiler_params=SMALL,
    )(where, sent)


def finish_kernel(image, row, *refs):
    pieces, branch = refs[:-1], refs[-1]
    xhat, inverse, scale = normalize(image[...], row[...])
    dnormed = pieces[0][...].astype(F32)
    for piece in pieces[1:]:
        dnormed = dnormed + piece[...].astype(F32)
    dxhat = dnormed * scale
    mean = jnp.mean(dxhat, -1, keepdims=True)
    along = jnp.mean(dxhat * xhat, -1, keepdims=True)
    branch[...] = (inverse * (dxhat - mean - xhat * along)).astype(BF16)


def finish(image, row, pieces):
    return pl.pallas_call(
        finish_kernel,
        out_shape=struct((CELLS, C)),
        in_specs=[WHOLE] * (2 + len(pieces)),
        cost_estimate=CHEAP,
        compiler_params=SMALL,
    )(image, row, *pieces)


def place_kernel(where, near, other, grad_q, grad_o):
    pieces = [near.at[i] for i in range(Z)] + [other.at[i] for i in range(Z)]
    z, core = where[0] // 2, lax.rem(where[0], 2)
    lane = lax.broadcasted_iota(jnp.int32, (1, 4 * PAIR), 1) // PAIR
    halves = [jnp.zeros((ROWS, 4 * PAIR), F32), jnp.zeros((ROWS, 4 * PAIR), F32)]
    for i, piece in enumerate(pieces):
        far, other = i % 4, i // 4
        place = (z ^ far) * 2 + (core if other == 0 else 1 - core)
        for part in range(3):
            at = pl.multiple_of(part * C + place * PAIR, PAIR)
            grad_q[:, pl.ds(at, PAIR)] = piece[:, part * PAIR : (part + 1) * PAIR].astype(F32)
        mine = lane == lax.rem(place, 4)
        for lo in range(2):
            at = QKV + lo * PAIR
            value = piece[:, at : at + PAIR].astype(F32)
            halves[lo] = halves[lo] + jnp.where(mine, jnp.concatenate([value] * 4, 1), 0.0)
    grad_o[:, : 4 * PAIR] = halves[0]
    grad_o[:, 4 * PAIR :] = halves[1]


def place(near, other, where):
    return pl.pallas_call(
        place_kernel,
        in_specs=[SCALARS] + [WHOLE] * 2,
        out_shape=(struct((ROWS, 3 * C), F32), struct((ROWS, C), F32)),
        cost_estimate=CHEAP,
        compiler_params=SMALL,
    )(where, near, other)


def turn(x, by):
    pairs = [(z * 2 + c, (z + by) % Z * 2 + c) for z in range(Z) for c in range(2)]
    return lax.ppermute(x, "space", pairs)


def swap(x):
    return lax.ppermute(x, "space", [(i, i ^ 1) for i in range(2 * Z)])


def swap_lo(x):
    return lax.ppermute(x, "dp", [(i, i ^ XY) for i in range(2 * XY)])


def transpose_devices(x):
    at = lambda t, y, s: (t * 4 + y) * 8 + s
    pairs = [(at(t, y, s), at(s, y, t)) for t in range(8) for y in range(4) for s in range(8)]
    return lax.ppermute(x, ("dp", "space"), pairs)


def turn_dp(x, by_x, by_y):
    at = lambda lo, col, y: (lo * 4 + col % 4) * 4 + y % 4
    pairs = [
        (at(lo, col, y), at(lo, col + by_x, y + by_y))
        for lo in range(2)
        for col in range(4)
        for y in range(4)
    ]
    return lax.ppermute(x, "dp", pairs)


def over_xy(x):
    groups = [list(range(XY)), list(range(XY, 2 * XY))]
    return lax.all_to_all(x, "dp", 0, 0, axis_index_groups=groups, tiled=True)


def meet(x, by):
    pairs = [(z * 2 + c, (z ^ by) * 2 + c) for z in range(Z) for c in range(2)]
    return lax.ppermute(x, "space", pairs)


def after(x, *others):
    return lax.optimization_barrier((x, others))[0]


def body(images, cotangent, w_qkv, w_out, film, timesteps):
    space, dp = lax.axis_index("space"), lax.axis_index("dp")
    where = jnp.stack([space, dp // XY, lax.rem(dp // 4, 4), lax.rem(dp, 4)])
    row = lax.dynamic_slice_in_dim(film, timesteps[0], 1, 0)
    image = images[0]
    x, w_part, o_part = prepare(where, image, cotangent[0], row, w_qkv, w_out)
    w_far, o_part = swap_lo(w_part), transpose_devices(o_part)
    x = after(x, w_far, o_part)
    one, three = turn(x, 1), turn(x, 3)
    packed = pack(where, w_part, w_far, o_part)
    packed = [packed] + [turn_dp(packed, 0, by) for by in range(1, 4)]
    parts = join(where, packed)
    parts = [parts] + [turn_dp(parts, by, 0) for by in range(1, 4)]
    half = CELLS // 2
    two = turn(after(one[:half], *packed), 1), turn(after(three[half:], *packed), 3)
    pieces = [after(x, *parts), after(one, *parts), *two, after(three, *parts)]
    pieces += [swap(piece) for piece in pieces]
    dqkv, wq, grads = attention(where, pieces, parts)
    grads = over_xy(grads)

    out, *mine = dnormed_terms(dqkv, wq)
    other = swap(out)
    sums = [
        (piece.astype(F32) + other[i * CELLS : (i + 1) * CELLS].astype(F32)).astype(BF16)
        for i, piece in enumerate(mine)
    ]
    own, one, two, three = sums[0], turn(sums[1], 3), turn(sums[2], 2), turn(sums[3], 1)

    near, far, go = add_up(where, after(grads, one, two, three))
    go = transpose_devices(go)
    gq = (near + swap_lo(far).astype(F32)).astype(BF16)
    mine = jnp.concatenate([gq, go[:ROWS], go[ROWS:]], 1)
    every = jnp.stack([mine, meet(mine, 1)])
    every = jnp.concatenate([every, meet(every, 2)], 0)
    grad_q, grad_o = place(every, swap(every), where)
    branch = finish(image, row, (own, one, two, three))
    return branch[None], grad_q, grad_o


def solution(mesh):
    return jax.shard_map(
        body,
        mesh=mesh,
        in_specs=(
            P("dp", "space", None),
            P("dp", "space", None),
            P("dp", None),
            P("dp", None),
            P(),
            P("dp"),
        ),
        out_specs=(P("dp", "space", None), P("dp", None), P("dp", None)),
        check_vma=False,
    )
```

time: 187 us -> 157 us (0.84)
  blocking collectives: 27.3 us -> 0 us
  Pallas kernels: 10.3 us -> 28.6 us
  waiting for transfers between devices: 49.6 us -> 63.6 us
  local copies, waits for them, and re-layouts: 16.6 us -> 4.19 us
  starting transfers between devices: 65.9 us -> 55.2 us
  matrix products: 9.1 us -> 0 us
  other arithmetic: 5.74 us -> 2.92 us
    all_gather x1 -> x0, blocking collectives: 27.3 us -> none  [body(): every = lax.all_gather(mine, 'space', axis=0, tiled=False).astype(F32)]
    ppermute x0 -> x10, waiting for transfers between devices: none -> 22.3 us  [the longest x6 15.8 us: turn_dp(): return lax.ppermute(x, 'dp', pairs)]
    all_to_all x2 -> x1, starting transfers between devices: 25.8 us -> 3.65 us  [over_xy(): return lax.all_to_all(x, 'dp', 0, 0, axis_index_groups=groups, tiled=True)]
    ppermute x9 -> x7, waiting for transfers between devices: 49.3 us -> 27.3 us  [turn(): return lax.ppermute(x, 'space', pairs)]
    ppermute x0 -> x10, starting transfers between devices: none -> 19.2 us  [the longest x6 7.87 us: turn_dp(): return lax.ppermute(x, 'dp', pairs)]
    pallas_call x1 -> x8, Pallas kernels: 10.3 us -> 28.6 us  [the longest x1 18.2 us: attention(): pl.pallas_call(attention_kernel, in_specs=[SCALARS] + [FAR] * PIECES + [W...]
    all_to_all x2 -> x1, waiting for transfers between devices: 0.01 us -> 11.2 us  [over_xy(): return lax.all_to_all(x, 'dp', 0, 0, axis_index_groups=groups, tiled=True)]
    ppermute x9 -> x7, starting transfers between devices: 26.2 us -> 16.8 us  [turn(): return lax.ppermute(x, 'space', pairs)]
  transfers between devices with their start and end apart: 16 -> 27, of which waited for: 7 -> 16; matrix products, arithmetic and copies ran while one was open for 10% -> 1% of each run, Pallas kernels for 0% -> 1%
where the time goes in v2:
time: 157 us; the launch traced here: 156 us
  waiting for transfers between devices  63.6 us (41%)
  starting transfers between devices  55.2 us (35%)
  Pallas kernels  28.6 us (18%)
  local copies, waits for them, and re-layouts  4.19 us (3%)
  other arithmetic  2.92 us (2%)
  between operations  1.58 us (1%)
    ppermute x7, waiting for transfers between devices, turn(): return lax.ppermute(x, 'space', pairs)  27.3 us
    pallas_call x1, Pallas kernels, attention(): pl.pallas_call(attention_kernel, in_specs=[SCALARS] + [FAR] * PIECES + [W...  18.2 us
    ppermute x7, starting transfers between devices, turn(): return lax.ppermute(x, 'space', pairs)  16.8 us
    ppermute x6, waiting for transfers between devices, turn_dp(): return lax.ppermute(x, 'dp', pairs)  15.8 us
    all_to_all x1, waiting for transfers between devices, over_xy(): return lax.all_to_all(x, 'dp', 0, 0, axis_index_groups=groups, tiled=True)  11.2 us
    ppermute x7, starting transfers between devices, swap(): return lax.ppermute(x, 'space', [(i, i ^ 1) for i in range(2 * Z)])  7.94 us
    ppermute x6, starting transfers between devices, turn_dp(): return lax.ppermute(x, 'dp', pairs)  7.87 us
    ppermute x2, starting transfers between devices, transpose_devices(): return lax.ppermute(x, ('dp', 'space'), pairs)  7.54 us
  transfers between devices with their start and end apart: 27, of which 16 were waited for; matrix products, arithmetic and copies ran while one was open for 1% of the time, Pallas kernels for 1%

profile of v2, /device:TPU:1, one launch (start us, length us, event | category | flops | bytes accessed | tf_op | source)
XLA Modules:
  0.0 156.1 jit_solution(17328699938694011651)
XLA Ops:
  5.5 2.5 %collective-permute-start = (bf16[32,384]{1,0:T(8,128)(2,1)}, bf16[32,384]{1,0:T(8,128)(2,1)S(1)}, u32[]{:S(2)}, u32[]{:S(2)}) collective-permute-start(bf16[32,384]{1,0:T(8,128)(2,1)} %get-tuple-element.27.w_part), channel_id=1, source_target_pairs={{0,128},{8,136},{16,144},{24,152},{32,160},{40,168},{48,176},{56,1... | collective-permute-start | bytes 73736 | tf_op jit(solution)/shard_map/ppermute | solution.py:318
  7.9 3.9 %collective-permute-start.1 = (bf16[64,128]{1,0:T(8,128)(2,1)}, bf16[64,128]{1,0:T(8,128)(2,1)S(1)}, u32[]{:S(2)}, u32[]{:S(2)}) collective-permute-start(bf16[64,128]{1,0:T(8,128)(2,1)} %get-tuple-element.28), channel_id=1, source_target_pairs={{0,0},{1,32},{2,64},{3,96},{4,128},{5,160},{6,192},{7,224},{8,8},{... | collective-permute-start | bytes 49160 | tf_op jit(solution)/shard_map/ppermute | solution.py:324
  13.5 9.9 %collective-permute-start.10 = (bf16[128,2048]{1,0:T(8,128)(2,1)}, bf16[128,2048]{1,0:T(8,128)(2,1)S(1)}, u32[]{:S(2)}, u32[]{:S(2)}) collective-permute-start(bf16[128,2048]{1,0:T(8,128)(2,1)} %get-tuple-element.30.refs_0_), channel_id=1, source_target_pairs={{0,6},{1,7},{2,0},{3,1},{4,2},{5,3},{6,4},{7,5},{8,14},{9,15},{10,... | collective-permute-start | bytes 1572872 | tf_op jit(solution)/shard_map/ppermute | solution.py:310
  25.3 2.8 %collective-permute-start.4 = (bf16[64,512]{1,0:T(8,128)(2,1)S(1)}, bf16[64,512]{1,0:T(8,128)(2,1)S(1)}, u32[]{:S(2)}, u32[]{:S(2)}) collective-permute-start(bf16[64,512]{1,0:T(8,128)(2,1)S(1)} %shard_map.86.refs_0_), channel_id=1, source_target_pairs={{0,24},{8,0},{16,8},{24,16},{32,56},{40,32},{48,40},{56,48},{64,88... | collective-permute-start | bytes 196616 | tf_op jit(solution)/shard_map/ppermute | solution.py:335
  29.4 3.6 %collective-permute-done.3.refs_2_ = bf16[64,512]{1,0:T(8,128)(2,1)S(1)} collective-permute-done((bf16[64,512]{1,0:T(8,128)(2,1)S(1)}, bf16[64,512]{1,0:T(8,128)(2,1)S(1)}, u32[]{:S(2)}, u32[]{:S(2)}) %collective-permute-start.3) | collective-permute-done | bytes 65568 | tf_op jit(solution)/shard_map/ppermute | solution.py:335
  34.4 3.9 %collective-permute-start.6 = (bf16[4,64,512]{2,1,0:T(8,128)(2,1)S(1)}, bf16[4,64,512]{2,1,0:T(8,128)(2,1)S(1)}, u32[]{:S(2)}, u32[]{:S(2)}) collective-permute-start(bf16[4,64,512]{2,1,0:T(8,128)(2,1)S(1)} %shard_map.87.refs_10_), channel_id=1, source_target_pairs={{0,64},{8,72},{16,80},{24,88},{32,96},{40,104},{48,112},{56,120},{... | collective-permute-start | bytes 786440 | tf_op jit(solution)/shard_map/ppermute | solution.py:335
  38.3 2.3 %collective-permute-done.7.refs_13_ = bf16[4,64,512]{2,1,0:T(8,128)(2,1)S(1)} collective-permute-done((bf16[4,64,512]{2,1,0:T(8,128)(2,1)S(1)}, bf16[4,64,512]{2,1,0:T(8,128)(2,1)S(1)}, u32[]{:S(2)}, u32[]{:S(2)}) %collective-permute-start.7) | collective-permute-done | bytes 262176 | tf_op jit(solution)/shard_map/ppermute | solution.py:335
  40.6 2.4 %collective-permute-done.6.refs_12_ = bf16[4,64,512]{2,1,0:T(8,128)(2,1)S(1)} collective-permute-done((bf16[4,64,512]{2,1,0:T(8,128)(2,1)S(1)}, bf16[4,64,512]{2,1,0:T(8,128)(2,1)S(1)}, u32[]{:S(2)}, u32[]{:S(2)}) %collective-permute-start.6) | collective-permute-done | bytes 262176 | tf_op jit(solution)/shard_map/ppermute | solution.py:335
  43.0 6.5 %collective-permute-done.5.refs_11_ = bf16[4,64,512]{2,1,0:T(8,128)(2,1)S(1)} collective-permute-done((bf16[4,64,512]{2,1,0:T(8,128)(2,1)S(1)}, bf16[4,64,512]{2,1,0:T(8,128)(2,1)S(1)}, u32[]{:S(2)}, u32[]{:S(2)}) %collective-permute-start.5) | collective-permute-done | bytes 262176 | tf_op jit(solution)/shard_map/ppermute | solution.py:335
  51.3 2.8 %collective-permute-start.11 = (bf16[64,2048]{1,0:T(8,128)(2,1)S(1)}, bf16[64,2048]{1,0:T(8,128)(2,1)S(1)}, u32[]{:S(2)}, u32[]{:S(2)}) collective-permute-start(bf16[64,2048]{1,0:T(8,128)(2,1)S(1)} %slice.33), channel_id=1, source_target_pairs={{0,6},{1,7},{2,0},{3,1},{4,2},{5,3},{6,4},{7,5},{8,14},{9,15},{10,... | collective-permute-start | bytes 786440 | tf_op jit(solution)/shard_map/ppermute | solution.py:310
  54.8 9.9 %collective-permute-done.11.refs_3_ = bf16[64,2048]{1,0:T(8,128)(2,1)S(1)} collective-permute-done((bf16[64,2048]{1,0:T(8,128)(2,1)S(1)}, bf16[64,2048]{1,0:T(8,128)(2,1)S(1)}, u32[]{:S(2)}, u32[]{:S(2)}) %collective-permute-start.11) | collective-permute-done | bytes 262176 | tf_op jit(solution)/shard_map/ppermute | solution.py:310
  65.2 3.8 %collective-permute-done.9.refs_2_ = bf16[64,2048]{1,0:T(8,128)(2,1)S(1)} collective-permute-done((bf16[64,2048]{1,0:T(8,128)(2,1)S(1)}, bf16[64,2048]{1,0:T(8,128)(2,1)S(1)}, u32[]{:S(2)}, u32[]{:S(2)}) %collective-permute-start.9) | collective-permute-done | bytes 262176 | tf_op jit(solution)/shard_map/ppermute | solution.py:310
  72.5 18.2 %shard_map.88 = (bf16[1024,384]{1,0:T(8,128)(2,1)}, bf16[1024,384]{1,0:T(8,128)(2,1)}, bf16[16,64,512]{2,1,0:T(8,128)(2,1)}) custom-call(s32[4]{0:T(128)} %pad_add_fusion.where, bf16[128,2048]{1,0:T(8,128)(2,1)} %get-tuple-element.30.refs_0_, bf16[128,2048]{1,0:T(8,128)(2,1)} %copy-done.7, bf16[64,2048]{1,0:T(8,128)(2,1)} %copy-done.15, ...), custom_call_target="tpu_custom_call" | custom-call | flops 17179869184 | bytes 8388608 | tf_op jit(solution)/shard_map/pallas_call | solution.py:127
  90.7 3.8 %shard_map.89 = (bf16[512,1024]{1,0:T(8,128)(2,1)}, bf16[128,1024]{1,0:T(8,128)(2,1)}, bf16[128,1024]{1,0:T(8,128)(2,1)}, bf16[128,1024]{1,0:T(8,128)(2,1)}, bf16[128,1024]{1,0:T(8,128)(2,1)}) custom-call(bf16[1024,384]{1,0:T(8,128)(2,1)} %get-tuple-element.35.dqkv, bf16[1024,384]{1,0:T(8,128)(2,1)} %get-tuple-element.36.wq), custom_call_target="tpu_custom_call" | custom-call | tf_op jit(solution)/shard_map/pallas_call | solution.py:160
  94.9 3.7 %all-to-all-start = ((bf16[16,64,512]{2,1,0:T(8,128)(2,1)}), bf16[16,64,512]{2,1,0:T(8,128)(2,1)S(1)}, u32[]{:S(2)}, u32[]{:S(2)}) async-start(bf16[16,64,512]{2,1,0:T(8,128)(2,1)} %get-tuple-element.42), calls=%async_computation | async-start | bytes 2097152 | tf_op jit(solution)/shard_map/all_to_all | solution.py:340
  98.6 2.3 %add_convert_fusion = (bf16[128,1024]{1,0:T(8,128)(2,1)}, bf16[128,1024]{1,0:T(8,128)(2,1)}, bf16[128,1024]{1,0:T(8,128)(2,1)}, bf16[128,1024]{1,0:T(8,128)(2,1)S(1)}) fusion(bf16[128,1024]{1,0:T(8,128)(2,1)} %get-tuple-element.41, bf16[512,1024]{1,0:T(8,128)(2,1)S(1)} %collective-permute-done.17, bf16[128,1024]{1,0:T(8,128)(2,1)} %get-tuple-element.40, ...), kind=kLoop, calls=%fused_computation | loop fusion | flops 2097152 | bytes 3145728 | tf_op jit(solution)/shard_map/convert_element_type | solution.py:375
  104.8 11.2 %all-to-all-done.sent = bf16[16,64,512]{2,1,0:T(8,128)(2,1)S(1)} async-done(((bf16[16,64,512]{2,1,0:T(8,128)(2,1)}), bf16[16,64,512]{2,1,0:T(8,128)(2,1)S(1)}, u32[]{:S(2)}, u32[]{:S(2)}) %all-to-all-start) | async-done | bytes 1048608 | tf_op jit(solution)/shard_map/all_to_all | solution.py:340
  116.0 4.5 %collective-permute-done.20.refs_3_ = bf16[128,1024]{1,0:T(8,128)(2,1)S(1)} collective-permute-done((bf16[128,1024]{1,0:T(8,128)(2,1)}, bf16[128,1024]{1,0:T(8,128)(2,1)S(1)}, u32[]{:S(2)}, u32[]{:S(2)}) %collective-permute-start.20) | collective-permute-done | bytes 262176 | tf_op jit(solution)/shard_map/ppermute | solution.py:310
  120.5 9.1 %collective-permute-done.18.refs_1_ = bf16[128,1024]{1,0:T(8,128)(2,1)S(1)} collective-permute-done((bf16[128,1024]{1,0:T(8,128)(2,1)}, bf16[128,1024]{1,0:T(8,128)(2,1)S(1)}, u32[]{:S(2)}, u32[]{:S(2)}) %collective-permute-start.18) | collective-permute-done | bytes 262176 | tf_op jit(solution)/shard_map/ppermute | solution.py:310
  130.3 3.6 %collective-permute-start.22 = (bf16[64,128]{1,0:T(8,128)(2,1)S(1)}, bf16[64,128]{1,0:T(8,128)(2,1)S(1)}, u32[]{:S(2)}, u32[]{:S(2)}) collective-permute-start(bf16[64,128]{1,0:T(8,128)(2,1)S(1)} %get-tuple-element.46), channel_id=1, source_target_pairs={{0,0},{1,32},{2,64},{3,96},{4,128},{5,160},{6,192},{7,224},{8,8},{... | collective-permute-start | bytes 49160 | tf_op jit(solution)/shard_map/ppermute | solution.py:324
  133.9 3.0 %collective-permute-start.21 = (bf16[32,384]{1,0:T(8,128)(2,1)S(1)}, bf16[32,384]{1,0:T(8,128)(2,1)S(1)}, u32[]{:S(2)}, u32[]{:S(2)}) collective-permute-start(bf16[32,384]{1,0:T(8,128)(2,1)S(1)} %get-tuple-element.45), channel_id=1, source_target_pairs={{0,128},{8,136},{16,144},{24,152},{32,160},{40,168},{48,176},{56,1... | collective-permute-start | bytes 73736 | tf_op jit(solution)/shard_map/ppermute | solution.py:318
  142.0 4.0 %collective-permute-start.24 = (bf16[2,32,640]{2,1,0:T(8,128)(2,1)S(1)}, bf16[2,32,640]{2,1,0:T(8,128)(2,1)S(1)}, u32[]{:S(2)}, u32[]{:S(2)}) collective-permute-start(bf16[2,32,640]{2,1,0:T(8,128)(2,1)S(1)} %pad_maximum_fusion.1), channel_id=1, source_target_pairs={{0,4},{1,5},{2,6},{3,7},{4,0},{5,1},{6,2},{7,3},{8,12},{9,13},{10,... | collective-permute-start | bytes 245768 | tf_op jit(solution)/shard_map/ppermute | solution.py:345
  146.0 3.4 %collective-permute-done.24 = bf16[2,32,640]{2,1,0:T(8,128)(2,1)S(1)} collective-permute-done((bf16[2,32,640]{2,1,0:T(8,128)(2,1)S(1)}, bf16[2,32,640]{2,1,0:T(8,128)(2,1)S(1)}, u32[]{:S(2)}, u32[]{:S(2)}) %collective-permute-start.24) | collective-permute-done | bytes 81952 | tf_op jit(solution)/shard_map/ppermute | solution.py:345
  149.5 4.0 %collective-permute-start.25 = (bf16[4,32,640]{2,1,0:T(8,128)(2,1)S(1)}, bf16[4,32,640]{2,1,0:T(8,128)(2,1)S(1)}, u32[]{:S(2)}, u32[]{:S(2)}) collective-permute-start(bf16[4,32,640]{2,1,0:T(8,128)(2,1)S(1)} %pad_maximum_fusion.near), channel_id=1, source_target_pairs={{0,1},{1,0},{2,3},{3,2},{4,5},{5,4},{6,7},{7,6},{8,9},{9,8},{10,11... | collective-permute-start | bytes 491528 | tf_op jit(solution)/shard_map/ppermute | solution.py:314
  (84 shorter events, 29.4 us)
Async XLA Ops:
  5.5 8.0 %collective-permute-start = (bf16[32,384]{1,0:T(8,128)(2,1)}, bf16[32,384]{1,0:T(8,128)(2,1)S(1)}, u32[]{:S(2)}, u32[]{:S(2)}) collective-permute-start(bf16[32,384]{1,0:T(8,128)(2,1)} %get-tuple-element.27.w_part), channel_id=1, source_target_pairs={{0,128},{8,136},{16,144},{24,152},{32,160},{40,168},{48,176},{56,1... | collective-permute-start | bytes 73736 | tf_op jit(solution)/shard_map/ppermute | solution.py:318
  7.9 5.6 %collective-permute-start.1 = (bf16[64,128]{1,0:T(8,128)(2,1)}, bf16[64,128]{1,0:T(8,128)(2,1)S(1)}, u32[]{:S(2)}, u32[]{:S(2)}) collective-permute-start(bf16[64,128]{1,0:T(8,128)(2,1)} %get-tuple-element.28), channel_id=1, source_target_pairs={{0,0},{1,32},{2,64},{3,96},{4,128},{5,160},{6,192},{7,224},{8,8},{... | collective-permute-start | bytes 49160 | tf_op jit(solution)/shard_map/ppermute | solution.py:324
  13.5 37.7 %collective-permute-start.10 = (bf16[128,2048]{1,0:T(8,128)(2,1)}, bf16[128,2048]{1,0:T(8,128)(2,1)S(1)}, u32[]{:S(2)}, u32[]{:S(2)}) collective-permute-start(bf16[128,2048]{1,0:T(8,128)(2,1)} %get-tuple-element.30.refs_0_), channel_id=1, source_target_pairs={{0,6},{1,7},{2,0},{3,1},{4,2},{5,3},{6,4},{7,5},{8,14},{9,15},{10,... | collective-permute-start | bytes 1572872 | tf_op jit(solution)/shard_map/ppermute | solution.py:310
  23.4 30.9 %collective-permute-start.8 = (bf16[128,2048]{1,0:T(8,128)(2,1)}, bf16[128,2048]{1,0:T(8,128)(2,1)S(1)}, u32[]{:S(2)}, u32[]{:S(2)}) collective-permute-start(bf16[128,2048]{1,0:T(8,128)(2,1)} %get-tuple-element.30.refs_0_), channel_id=1, source_target_pairs={{0,2},{1,3},{2,4},{3,5},{4,6},{5,7},{6,0},{7,1},{8,10},{9,11},{10,... | collective-permute-start | bytes 1572872 | tf_op jit(solution)/shard_map/ppermute | solution.py:310
  25.3 4.1 %collective-permute-start.4 = (bf16[64,512]{1,0:T(8,128)(2,1)S(1)}, bf16[64,512]{1,0:T(8,128)(2,1)S(1)}, u32[]{:S(2)}, u32[]{:S(2)}) collective-permute-start(bf16[64,512]{1,0:T(8,128)(2,1)S(1)} %shard_map.86.refs_0_), channel_id=1, source_target_pairs={{0,24},{8,0},{16,8},{24,16},{32,56},{40,32},{48,40},{56,48},{64,88... | collective-permute-start | bytes 196616 | tf_op jit(solution)/shard_map/ppermute | solution.py:335
  28.1 4.9 %collective-permute-start.3 = (bf16[64,512]{1,0:T(8,128)(2,1)S(1)}, bf16[64,512]{1,0:T(8,128)(2,1)S(1)}, u32[]{:S(2)}, u32[]{:S(2)}) collective-permute-start(bf16[64,512]{1,0:T(8,128)(2,1)S(1)} %shard_map.86.refs_0_), channel_id=1, source_target_pairs={{0,16},{8,24},{16,0},{24,8},{32,48},{40,56},{48,32},{56,40},{64,80... | collective-permute-start | bytes 196616 | tf_op jit(solution)/shard_map/ppermute | solution.py:335
  28.5 5.3 %collective-permute-start.2 = (bf16[64,512]{1,0:T(8,128)(2,1)S(1)}, bf16[64,512]{1,0:T(8,128)(2,1)S(1)}, u32[]{:S(2)}, u32[]{:S(2)}) collective-permute-start(bf16[64,512]{1,0:T(8,128)(2,1)S(1)} %shard_map.86.refs_0_), channel_id=1, source_target_pairs={{0,8},{8,16},{16,24},{24,0},{32,40},{40,48},{48,56},{56,32},{64,72... | collective-permute-start | bytes 196616 | tf_op jit(solution)/shard_map/ppermute | solution.py:335
  34.3 6.3 %collective-permute-start.7 = (bf16[4,64,512]{2,1,0:T(8,128)(2,1)S(1)}, bf16[4,64,512]{2,1,0:T(8,128)(2,1)S(1)}, u32[]{:S(2)}, u32[]{:S(2)}) collective-permute-start(bf16[4,64,512]{2,1,0:T(8,128)(2,1)S(1)} %shard_map.87.refs_10_), channel_id=1, source_target_pairs={{0,96},{8,104},{16,112},{24,120},{32,0},{40,8},{48,16},{56,24},{64... | collective-permute-start | bytes 786440 | tf_op jit(solution)/shard_map/ppermute | solution.py:335
  34.4 8.6 %collective-permute-start.6 = (bf16[4,64,512]{2,1,0:T(8,128)(2,1)S(1)}, bf16[4,64,512]{2,1,0:T(8,128)(2,1)S(1)}, u32[]{:S(2)}, u32[]{:S(2)}) collective-permute-start(bf16[4,64,512]{2,1,0:T(8,128)(2,1)S(1)} %shard_map.87.refs_10_), channel_id=1, source_target_pairs={{0,64},{8,72},{16,80},{24,88},{32,96},{40,104},{48,112},{56,120},{... | collective-permute-start | bytes 786440 | tf_op jit(solution)/shard_map/ppermute | solution.py:335
  38.3 11.2 %collective-permute-start.5 = (bf16[4,64,512]{2,1,0:T(8,128)(2,1)S(1)}, bf16[4,64,512]{2,1,0:T(8,128)(2,1)S(1)}, u32[]{:S(2)}, u32[]{:S(2)}) collective-permute-start(bf16[4,64,512]{2,1,0:T(8,128)(2,1)S(1)} %shard_map.87.refs_10_), channel_id=1, source_target_pairs={{0,32},{8,40},{16,48},{24,56},{32,64},{40,72},{48,80},{56,88},{64,... | collective-permute-start | bytes 786440 | tf_op jit(solution)/shard_map/ppermute | solution.py:335
  49.6 20.3 %collective-permute-start.12 = (bf16[128,2048]{1,0:T(8,128)(2,1)}, bf16[128,2048]{1,0:T(8,128)(2,1)S(1)}, u32[]{:S(2)}, u32[]{:S(2)}) collective-permute-start(bf16[128,2048]{1,0:T(8,128)(2,1)} %get-tuple-element.30.refs_0_), channel_id=1, source_target_pairs={{0,1},{1,0},{2,3},{3,2},{4,5},{5,4},{6,7},{7,6},{8,9},{9,8},{10,11... | collective-permute-start | bytes 1572872 | tf_op jit(solution)/shard_map/ppermute | solution.py:314
  51.3 13.4 %collective-permute-start.11 = (bf16[64,2048]{1,0:T(8,128)(2,1)S(1)}, bf16[64,2048]{1,0:T(8,128)(2,1)S(1)}, u32[]{:S(2)}, u32[]{:S(2)}) collective-permute-start(bf16[64,2048]{1,0:T(8,128)(2,1)S(1)} %slice.33), channel_id=1, source_target_pairs={{0,6},{1,7},{2,0},{3,1},{4,2},{5,3},{6,4},{7,5},{8,14},{9,15},{10,... | collective-permute-start | bytes 786440 | tf_op jit(solution)/shard_map/ppermute | solution.py:310
  54.1 15.8 %collective-permute-start.16 = (bf16[128,2048]{1,0:T(8,128)(2,1)S(1)}, bf16[128,2048]{1,0:T(8,128)(2,1)S(1)}, u32[]{:S(2)}, u32[]{:S(2)}) collective-permute-start(bf16[128,2048]{1,0:T(8,128)(2,1)S(1)} %collective-permute-done.10.refs_4_), channel_id=1, source_target_pairs={{0,1},{1,0},{2,3},{3,2},{4,5},{5,4},{6,7},{7,6},{8,9},{9,8},{10,11... | collective-permute-start | bytes 1572872 | tf_op jit(solution)/shard_map/ppermute | solution.py:314
  54.4 14.6 %collective-permute-start.9 = (bf16[64,2048]{1,0:T(8,128)(2,1)S(1)}, bf16[64,2048]{1,0:T(8,128)(2,1)S(1)}, u32[]{:S(2)}, u32[]{:S(2)}) collective-permute-start(bf16[64,2048]{1,0:T(8,128)(2,1)S(1)} %slice.32), channel_id=1, source_target_pairs={{0,2},{1,3},{2,4},{3,5},{4,6},{5,7},{6,0},{7,1},{8,10},{9,11},{10,... | collective-permute-start | bytes 786440 | tf_op jit(solution)/shard_map/ppermute | solution.py:310
  54.5 16.5 %collective-permute-start.13 = (bf16[128,2048]{1,0:T(8,128)(2,1)S(1)}, bf16[128,2048]{1,0:T(8,128)(2,1)S(1)}, u32[]{:S(2)}, u32[]{:S(2)}) collective-permute-start(bf16[128,2048]{1,0:T(8,128)(2,1)S(1)} %collective-permute-done.8.refs_1_), channel_id=1, source_target_pairs={{0,1},{1,0},{2,3},{3,2},{4,5},{5,4},{6,7},{7,6},{8,9},{9,8},{10,11... | collective-permute-start | bytes 1572872 | tf_op jit(solution)/shard_map/ppermute | solution.py:314
  64.7 5.1 %collective-permute-start.15 = (bf16[64,2048]{1,0:T(8,128)(2,1)S(1)}, bf16[64,2048]{1,0:T(8,128)(2,1)S(1)}, u32[]{:S(2)}, u32[]{:S(2)}) collective-permute-start(bf16[64,2048]{1,0:T(8,128)(2,1)S(1)} %collective-permute-done.11.refs_3_), channel_id=1, source_target_pairs={{0,1},{1,0},{2,3},{3,2},{4,5},{5,4},{6,7},{7,6},{8,9},{9,8},{10,11... | collective-permute-start | bytes 786440 | tf_op jit(solution)/shard_map/ppermute | solution.py:314
  94.9 21.1 %all-to-all-start = ((bf16[16,64,512]{2,1,0:T(8,128)(2,1)}), bf16[16,64,512]{2,1,0:T(8,128)(2,1)S(1)}, u32[]{:S(2)}, u32[]{:S(2)}) async-start(bf16[16,64,512]{2,1,0:T(8,128)(2,1)} %get-tuple-element.42), calls=%async_computation | async-start | bytes 2097152 | tf_op jit(solution)/shard_map/all_to_all | solution.py:340
  100.9 19.7 %collective-permute-start.20 = (bf16[128,1024]{1,0:T(8,128)(2,1)}, bf16[128,1024]{1,0:T(8,128)(2,1)S(1)}, u32[]{:S(2)}, u32[]{:S(2)}) collective-permute-start(bf16[128,1024]{1,0:T(8,128)(2,1)} %get-tuple-element.49), channel_id=1, source_target_pairs={{0,2},{1,3},{2,4},{3,5},{4,6},{5,7},{6,0},{7,1},{8,10},{9,11},{10,... | collective-permute-start | bytes 786440 | tf_op jit(solution)/shard_map/ppermute | solution.py:310
  100.9 19.6 %collective-permute-start.19 = (bf16[128,1024]{1,0:T(8,128)(2,1)}, bf16[128,1024]{1,0:T(8,128)(2,1)S(1)}, u32[]{:S(2)}, u32[]{:S(2)}) collective-permute-start(bf16[128,1024]{1,0:T(8,128)(2,1)} %get-tuple-element.50), channel_id=1, source_target_pairs={{0,4},{1,5},{2,6},{3,7},{4,0},{5,1},{6,2},{7,3},{8,12},{9,13},{10,... | collective-permute-start | bytes 786440 | tf_op jit(solution)/shard_map/ppermute | solution.py:310
  103.2 26.5 %collective-permute-start.18 = (bf16[128,1024]{1,0:T(8,128)(2,1)}, bf16[128,1024]{1,0:T(8,128)(2,1)S(1)}, u32[]{:S(2)}, u32[]{:S(2)}) collective-permute-start(bf16[128,1024]{1,0:T(8,128)(2,1)} %get-tuple-element.51), channel_id=1, source_target_pairs={{0,6},{1,7},{2,0},{3,1},{4,2},{5,3},{6,4},{7,5},{8,14},{9,15},{10,... | collective-permute-start | bytes 786440 | tf_op jit(solution)/shard_map/ppermute | solution.py:310
  130.3 6.6 %collective-permute-start.22 = (bf16[64,128]{1,0:T(8,128)(2,1)S(1)}, bf16[64,128]{1,0:T(8,128)(2,1)S(1)}, u32[]{:S(2)}, u32[]{:S(2)}) collective-permute-start(bf16[64,128]{1,0:T(8,128)(2,1)S(1)} %get-tuple-element.46), channel_id=1, source_target_pairs={{0,0},{1,32},{2,64},{3,96},{4,128},{5,160},{6,192},{7,224},{8,8},{... | collective-permute-start | bytes 49160 | tf_op jit(solution)/shard_map/ppermute | solution.py:324
  133.9 4.2 %collective-permute-start.21 = (bf16[32,384]{1,0:T(8,128)(2,1)S(1)}, bf16[32,384]{1,0:T(8,128)(2,1)S(1)}, u32[]{:S(2)}, u32[]{:S(2)}) collective-permute-start(bf16[32,384]{1,0:T(8,128)(2,1)S(1)} %get-tuple-element.45), channel_id=1, source_target_pairs={{0,128},{8,136},{16,144},{24,152},{32,160},{40,168},{48,176},{56,1... | collective-permute-start | bytes 73736 | tf_op jit(solution)/shard_map/ppermute | solution.py:318
  142.0 7.4 %collective-permute-start.24 = (bf16[2,32,640]{2,1,0:T(8,128)(2,1)S(1)}, bf16[2,32,640]{2,1,0:T(8,128)(2,1)S(1)}, u32[]{:S(2)}, u32[]{:S(2)}) collective-permute-start(bf16[2,32,640]{2,1,0:T(8,128)(2,1)S(1)} %pad_maximum_fusion.1), channel_id=1, source_target_pairs={{0,4},{1,5},{2,6},{3,7},{4,0},{5,1},{6,2},{7,3},{8,12},{9,13},{10,... | collective-permute-start | bytes 245768 | tf_op jit(solution)/shard_map/ppermute | solution.py:345
  149.5 5.2 %collective-permute-start.25 = (bf16[4,32,640]{2,1,0:T(8,128)(2,1)S(1)}, bf16[4,32,640]{2,1,0:T(8,128)(2,1)S(1)}, u32[]{:S(2)}, u32[]{:S(2)}) collective-permute-start(bf16[4,32,640]{2,1,0:T(8,128)(2,1)S(1)} %pad_maximum_fusion.near), channel_id=1, source_target_pairs={{0,1},{1,0},{2,3},{3,2},{4,5},{5,4},{6,7},{7,6},{8,9},{9,8},{10,11... | collective-permute-start | bytes 491528 | tf_op jit(solution)/shard_map/ppermute | solution.py:314
  (21 other events, 342.1 us)

commit v3 on v2

v3 whole, which is shorter than its diff:
```python
import jax
import jax.numpy as jnp
from jax import lax
from jax.experimental import pallas as pl
from jax.experimental.pallas import tpu as pltpu
from jax.sharding import PartitionSpec as P

C = 1024
Z = 4
XY = 16
ROWS = 32
CELLS = 128
PAIR = 128
QKV = 3 * PAIR
PIECES = 10
F32 = jnp.float32
BF16 = jnp.bfloat16
FAR = pl.BlockSpec(memory_space=pltpu.HBM)
WHOLE = pl.BlockSpec(memory_space=pltpu.VMEM)
SCALARS = pl.BlockSpec(memory_space=pltpu.SMEM)
CHEAP = pl.CostEstimate(flops=0, bytes_accessed=0, transcendentals=0)
SMALL = pltpu.CompilerParams(vmem_limit_bytes=8 * 2**20)
PARAMS = pltpu.CompilerParams(vmem_limit_bytes=58 * 2**20)


def nt(a, b):
    return lax.dot_general(a, b, (((1,), (1,)), ((), ())), preferred_element_type=F32)


def tn(a, b):
    return lax.dot_general(a, b, (((0,), (0,)), ((), ())), preferred_element_type=F32)


def nn(a, b):
    return jnp.dot(a, b, preferred_element_type=F32)


def struct(shape, dtype=BF16):
    return jax.ShapeDtypeStruct(shape, dtype)


def heads():
    lane = lax.broadcasted_iota(jnp.int32, (1, PAIR), 1)
    return lane < PAIR // 2, lane >= PAIR // 2


def attention_kernel(where, *refs):
    pieces, parts, rest = refs[:PIECES], refs[PIECES : PIECES + 4], refs[PIECES + 4 :]
    grads, *results = rest[:7]
    x, weights, wq, wo, qkv, att, d_att, dqkv, turned, sent, terms, sems = rest[7:]
    copies, at = [], 0
    for i, part in enumerate(parts):
        copies.append(pltpu.make_async_copy(part, weights.at[i], sems.at[PIECES + i]))
    for i, piece in enumerate(pieces):
        to = x.at[at : at + piece.shape[0], :]
        copies.append(pltpu.make_async_copy(piece, to, sems.at[i]))
        at += piece.shape[0]
    for copy in copies:
        copy.start()
    for far in range(4):
        copies[far].wait()
        col = lax.rem(where[2] - far + 4, 4)
        for lo in range(2):
            half = slice(lo * ROWS, (lo + 1) * ROWS)
            columns = pl.ds(pl.multiple_of((lo * 4 + col) * PAIR, PAIR), PAIR)
            for y in range(4):
                at = pl.multiple_of(((lo * 4 + col) * 4 + y) * ROWS, ROWS)
                wq[pl.ds(at, ROWS), :] = weights[far, y, half, :QKV]
                wo[y * ROWS : (y + 1) * ROWS, columns] = weights[far, y, half, QKV:]
    cells = Z * CELLS
    for core in range(2):
        rows = slice(core * cells, (core + 1) * cells)
        for copy in copies[4 + core * PIECES // 2 : 4 + (core + 1) * PIECES // 2]:
            copy.wait()
        qkv[rows, :] = nn(x[rows, :C], wq[...]).astype(BF16)
        d_att[rows, :] = nt(x[rows, C:], wo[...]).astype(BF16)
    q = qkv[:, :PAIR] * jnp.bfloat16(0.125)
    k = qkv[:, PAIR : 2 * PAIR]
    v = qkv[:, 2 * PAIR :]
    d = d_att[...]
    zero = jnp.zeros_like(q)
    for head, mine_head in enumerate(heads()):
        qh = jnp.where(mine_head, q, zero)
        dh = jnp.where(mine_head, d, zero)
        scores = nt(qh, k)
        e = jnp.exp(scores - jnp.max(scores, -1, keepdims=True))
        p = e * (1.0 / jnp.sum(e, -1, keepdims=True))
        pb = p.astype(BF16)
        o = nn(pb, v).astype(BF16).astype(F32)
        delta = jnp.sum(dh.astype(F32) * o, -1, keepdims=True)
        ds = (p * (nt(dh, v) - delta)).astype(BF16)
        dq = (0.125 * nn(ds, k)).astype(BF16)
        dk, dv = tn(qh, ds), tn(dh, pb)
        if head == 0:
            att[...] = o.astype(BF16)
            dqkv[:, :PAIR] = dq
            turned[:PAIR, :] = dk
            turned[PAIR:, :] = dv
        else:
            att[...] = jnp.where(mine_head, o.astype(BF16), att[...])
            dqkv[:, :PAIR] = jnp.where(mine_head, dq, dqkv[:, :PAIR])
            turned[:PAIR, :] += dk
            turned[PAIR:, :] += dv

    dqkv[:, PAIR:] = turned[...].T.astype(BF16)
    grad = tn(dqkv[...], x[:, :C]).T.astype(BF16)
    for lo in range(2):
        for xy in range(XY):
            at = (lo * XY + xy) * ROWS
            sent[xy, lo * ROWS : (lo + 1) * ROWS, :QKV] = grad[at : at + ROWS, :]
    grad = tn(att[...], x[:, C:]).astype(BF16)
    for xy in range(XY):
        col, y = divmod(xy, 4)
        for lo in range(2):
            at = (lo * 4 + col) * PAIR
            sent[xy, lo * ROWS : (lo + 1) * ROWS, QKV:] = grad[
                y * ROWS : (y + 1) * ROWS, at : at + PAIR
            ]
    copies = [pltpu.make_async_copy(sent, grads, sems.at[0])]
    copies[0].start()
    far, near = results[0], results[1]
    order = [(Z + 2, far)]
    order += [(Z + spot, near.at[i * CELLS : (i + 1) * CELLS]) for i, spot in enumerate((0, 1, 3))]
    order += list(zip((2, 0, 1, 3), results[2:]))
    for i, (spot, to) in enumerate(order):
        rows = slice(spot * CELLS, (spot + 1) * CELLS)
        terms[rows, :] = nt(dqkv[rows, :], wq[...]).astype(BF16)
        copies.append(pltpu.make_async_copy(terms.at[rows, :], to, sems.at[i + 1]))
        copies[-1].start()
    for copy in copies:
        copy.wait()


def attention(where, pieces, parts):
    cells = 8 * CELLS
    return pl.pallas_call(
        attention_kernel,
        in_specs=[SCALARS] + [FAR] * (PIECES + 4),
        out_specs=[FAR] * 7,
        out_shape=(
            struct((XY, 2 * ROWS, QKV + PAIR)),
            struct((CELLS, C)),
            struct((3 * CELLS, C)),
            *[struct((CELLS, C))] * Z,
        ),
        scratch_shapes=[
            pltpu.VMEM((cells, 2 * C), BF16),
            pltpu.VMEM((4, 4, 2 * ROWS, QKV + PAIR), BF16),
            pltpu.VMEM((C, QKV), BF16),
            pltpu.VMEM((PAIR, C), BF16),
            pltpu.VMEM((cells, QKV), BF16),
            pltpu.VMEM((cells, PAIR), BF16),
            pltpu.VMEM((cells, PAIR), BF16),
            pltpu.VMEM((cells, QKV), BF16),
            pltpu.VMEM((2 * PAIR, cells), F32),
            pltpu.VMEM((XY, 2 * ROWS, QKV + PAIR), BF16),
            pltpu.VMEM((cells, C), BF16),
            pltpu.SemaphoreType.DMA((PIECES + 4,)),
        ],
        compiler_params=PARAMS,
        cost_estimate=pl.CostEstimate(
            flops=2**34, bytes_accessed=2**23, transcendentals=2 * cells * cells
        ),
    )(where, *pieces, *parts)


def normalize(image, row):
    xf = image.astype(F32)
    centered = xf - jnp.mean(xf, -1, keepdims=True)
    inverse = lax.rsqrt(jnp.mean(centered * centered, -1, keepdims=True) + 1e-05)
    return centered * inverse, inverse, 1.0 + row[:, :C].astype(F32)


def prepare_kernel(image, cot, row, x):
    xhat, _, scale = normalize(image[...], row[...])
    x[:, :C] = (xhat * scale + row[:, C:].astype(F32)).astype(BF16)
    x[:, C:] = cot[...]


def prepare(image, cot, row):
    return pl.pallas_call(
        prepare_kernel,
        in_specs=[WHOLE] * 3,
        out_shape=struct((CELLS, 2 * C)),
        cost_estimate=CHEAP,
        compiler_params=PARAMS,
    )(image, cot, row)


def cut_kernel(w_qkv, w_out, w_part, o_part, sems):
    space = lax.axis_index("space")
    copies = []
    for part in range(3):
        at = pl.multiple_of(part * C + space * PAIR, PAIR)
        to = w_part.at[:, part * PAIR : (part + 1) * PAIR]
        copies.append(pltpu.make_async_copy(w_qkv.at[:, pl.ds(at, PAIR)], to, sems.at[part]))
    for lo in range(2):
        at = pl.multiple_of(lo * 4 * PAIR + lax.rem(space, 4) * PAIR, PAIR)
        to = o_part.at[lo * ROWS : (lo + 1) * ROWS, :]
        copies.append(pltpu.make_async_copy(w_out.at[:, pl.ds(at, PAIR)], to, sems.at[3 + lo]))
    for copy in copies:
        copy.start()
    for copy in copies:
        copy.wait()


def cut(w_qkv, w_out):
    return pl.pallas_call(
        cut_kernel,
        in_specs=[FAR] * 2,
        out_shape=(struct((ROWS, QKV)), struct((2 * ROWS, PAIR))),
        scratch_shapes=[pltpu.SemaphoreType.DMA((5,))],
        cost_estimate=CHEAP,
        compiler_params=PARAMS,
    )(w_qkv, w_out)


def pack_kernel(where, w_part, w_far, o_part, packed):
    low = where[1] == 0
    near, far = w_part[...], w_far[...]
    packed[:ROWS, :QKV] = jnp.where(low, near, far)
    packed[ROWS:, :QKV] = jnp.where(low, far, near)
    packed[:, QKV:] = o_part[...]


def pack(where, w_part, w_far, o_part):
    return pl.pallas_call(
        pack_kernel,
        in_specs=[SCALARS] + [WHOLE] * 3,
        out_shape=struct((2 * ROWS, QKV + PAIR)),
        cost_estimate=CHEAP,
        compiler_params=SMALL,
    )(where, w_part, w_far, o_part)


def join_kernel(where, *refs):
    pieces, joined = refs[:-1], refs[-1]
    for far, piece in enumerate(pieces):
        joined[lax.rem(where[3] - far + 4, 4)] = piece[...]


def join(where, pieces):
    return pl.pallas_call(
        join_kernel,
        in_specs=[SCALARS] + [WHOLE] * 4,
        out_shape=struct((4, 2 * ROWS, QKV + PAIR)),
        cost_estimate=CHEAP,
        compiler_params=SMALL,
    )(where, *pieces)


def total_kernel(where, sent, near, far, go):
    total = sent[0].astype(F32)
    for xy in range(1, XY):
        total = total + sent[xy].astype(F32)
    go[...] = total[:, QKV:].astype(BF16)
    low = where[1] == 0
    first, second = total[:ROWS, :QKV], total[ROWS:, :QKV]
    near[...] = jnp.where(low, first, second)
    far[...] = jnp.where(low, second, first).astype(BF16)


def add_up(where, sent):
    return pl.pallas_call(
        total_kernel,
        in_specs=[SCALARS, WHOLE],
        out_shape=(struct((ROWS, QKV), F32), struct((ROWS, QKV)), struct((2 * ROWS, PAIR))),
        cost_estimate=CHEAP,
        compiler_params=SMALL,
    )(where, sent)


def finish_kernel(image, row, *refs):
    pieces, branch = refs[:-1], refs[-1]
    xhat, inverse, scale = normalize(image[...], row[...])
    dnormed = pieces[0][...].astype(F32)
    for piece in pieces[1:]:
        dnormed = dnormed + piece[...].astype(F32)
    dxhat = dnormed * scale
    mean = jnp.mean(dxhat, -1, keepdims=True)
    along = jnp.mean(dxhat * xhat, -1, keepdims=True)
    branch[...] = (inverse * (dxhat - mean - xhat * along)).astype(BF16)


def finish(image, row, pieces):
    return pl.pallas_call(
        finish_kernel,
        out_shape=struct((CELLS, C)),
        in_specs=[WHOLE] * (2 + len(pieces)),
        cost_estimate=CHEAP,
        compiler_params=SMALL,
    )(image, row, *pieces)


def place_kernel(where, *refs):
    pieces, (grad_q, grad_o) = refs[:-2], refs[-2:]
    z, core = where[0] // 2, lax.rem(where[0], 2)
    lane = lax.broadcasted_iota(jnp.int32, (1, 4 * PAIR), 1) // PAIR
    halves = [jnp.zeros((ROWS, 4 * PAIR), F32), jnp.zeros((ROWS, 4 * PAIR), F32)]
    for i, piece in enumerate(pieces):
        far, other = i % 4, i // 4
        place = lax.rem(z - far + Z, Z) * 2 + (core if other == 0 else 1 - core)
        for part in range(3):
            at = pl.multiple_of(part * C + place * PAIR, PAIR)
            grad_q[:, pl.ds(at, PAIR)] = piece[:, part * PAIR : (part + 1) * PAIR].astype(F32)
        mine = lane == lax.rem(place, 4)
        for lo in range(2):
            at = QKV + lo * PAIR
            value = piece[:, at : at + PAIR].astype(F32)
            halves[lo] = halves[lo] + jnp.where(mine, jnp.concatenate([value] * 4, 1), 0.0)
    grad_o[:, : 4 * PAIR] = halves[0]
    grad_o[:, 4 * PAIR :] = halves[1]


def place(pieces, where):
    return pl.pallas_call(
        place_kernel,
        in_specs=[SCALARS] + [WHOLE] * 8,
        out_shape=(struct((ROWS, 3 * C), F32), struct((ROWS, C), F32)),
        cost_estimate=CHEAP,
        compiler_params=SMALL,
    )(where, *pieces)


def turn(x, by):
    pairs = [(z * 2 + c, (z + by) % Z * 2 + c) for z in range(Z) for c in range(2)]
    return lax.ppermute(x, "space", pairs)


def swap(x):
    return lax.ppermute(x, "space", [(i, i ^ 1) for i in range(2 * Z)])


def swap_lo(x):
    return lax.ppermute(x, "dp", [(i, i ^ XY) for i in range(2 * XY)])


def transpose_devices(x):
    at = lambda t, y, s: (t * 4 + y) * 8 + s
    pairs = [(at(t, y, s), at(s, y, t)) for t in range(8) for y in range(4) for s in range(8)]
    return lax.ppermute(x, ("dp", "space"), pairs)


def turn_dp(x, by_x, by_y):
    at = lambda lo, col, y: (lo * 4 + col % 4) * 4 + y % 4
    pairs = [
        (at(lo, col, y), at(lo, col + by_x, y + by_y))
        for lo in range(2)
        for col in range(4)
        for y in range(4)
    ]
    return lax.ppermute(x, "dp", pairs)


def over_xy(x):
    groups = [list(range(XY)), list(range(XY, 2 * XY))]
    return lax.all_to_all(x, "dp", 0, 0, axis_index_groups=groups, tiled=True)


def add(a, b):
    return (a.astype(F32) + b.astype(F32)).astype(BF16)


def after(x, *others):
    return lax.optimization_barrier((x, others))[0]


def body(images, cotangent, w_qkv, w_out, film, timesteps):
    space, dp = lax.axis_index("space"), lax.axis_index("dp")
    where = jnp.stack([space, dp // XY, lax.rem(dp // 4, 4), lax.rem(dp, 4)])
    row = lax.dynamic_slice_in_dim(film, timesteps[0], 1, 0)
    image = images[0]
    w_part, o_part = cut(w_qkv, w_out)
    w_far, o_part = swap_lo(w_part), transpose_devices(o_part)
    x = prepare(image, cotangent[0], row)
    x = after(x, w_far, o_part)
    one, three = turn(x, 1), turn(x, 3)
    packed = pack(where, w_part, w_far, o_part)
    packed = [packed] + [turn_dp(packed, 0, by) for by in range(1, 4)]
    parts = join(where, packed)
    x = after(x, *packed)
    parts = [parts] + [turn_dp(parts, by, 0) for by in range(1, 4)]
    one, three = after((one, three), parts[1], parts[2])
    half = CELLS // 2
    pieces = [x, one, turn(one[:half], 1), turn(three[half:], 3), three]
    pieces += [swap(piece) for piece in pieces]
    grads, far, near, two, own, one, three = attention(where, pieces, parts)
    grads = over_xy(grads)

    two = add(two, swap(far))
    near = swap(near)
    own, one, three = (
        add(piece, near[i * CELLS : (i + 1) * CELLS]) for i, piece in enumerate((own, one, three))
    )
    two = turn(two, 2)

    near, far, go = add_up(where, after(grads, two))
    go = transpose_devices(go)
    gq = (near + swap_lo(far).astype(F32)).astype(BF16)
    mine = jnp.concatenate([gq, go[:ROWS], go[ROWS:]], 1)
    one, three = turn(after(one, mine), 3), turn(after(three, mine), 1)
    every = [mine] + [turn(mine, by) for by in range(1, Z)]
    grad_q, grad_o = place(every + [swap(piece) for piece in every], where)
    branch = finish(image, row, (own, one, two, three))
    return branch[None], grad_q, grad_o


def solution(mesh):
    return jax.shard_map(
        body,
        mesh=mesh,
        in_specs=(
            P("dp", "space", None),
            P("dp", "space", None),
            P("dp", None),
            P("dp", None),
            P(),
            P("dp"),
        ),
        out_specs=(P("dp", "space", None), P("dp", None), P("dp", None)),
        check_vma=False,
    )
```

time: 157 us -> 145 us (0.924)
  waiting for transfers between devices: 63.6 us -> 45.9 us
  starting transfers between devices: 55.2 us -> 67.7 us
  Pallas kernels: 28.6 us -> 23.5 us
    all_to_all x1, waiting for transfers between devices: 11.2 us -> 0.01 us  [over_xy(): return lax.all_to_all(x, 'dp', 0, 0, axis_index_groups=groups, tiled=True)]
    ppermute x7 -> x11, starting transfers between devices: 7.94 us -> 18.7 us  [swap(): return lax.ppermute(x, 'space', [(i, i ^ 1) for i in range(2 * Z)])]
    ppermute x6, waiting for transfers between devices: 15.8 us -> 8.75 us  [turn_dp(): return lax.ppermute(x, 'dp', pairs)]
    ppermute x2 -> x0, starting transfers between devices: 5.9 us -> none  [meet(): return lax.ppermute(x, 'space', pairs)]
    ppermute x2 -> x0, waiting for transfers between devices: 5.33 us -> none  [meet(): return lax.ppermute(x, 'space', pairs)]
    pallas_call x4, Pallas kernels: 25.6 us -> 20.5 us  [the longest x1 15.5 us: attention(): pl.pallas_call(attention_kernel, in_specs=[SCALARS] + [FAR] * (PIECES + 4...]
    ppermute x7 -> x10, waiting for transfers between devices: 27.3 us -> 31.5 us  [turn(): return lax.ppermute(x, 'space', pairs)]
    ppermute x2, starting transfers between devices: 5.47 us -> 9.19 us  [swap_lo(): return lax.ppermute(x, 'dp', [(i, i ^ XY) for i in range(2 * XY)])]
  transfers between devices with their start and end apart: 27 -> 32, of which waited for: 16 -> 13; matrix products, arithmetic and copies ran while one was open for 1% -> 2% of each run, Pallas kernels for 1% -> 4%
where the time goes in v3:
time: 145 us
  starting transfers between devices  67.7 us (47%)
  waiting for transfers between devices  45.9 us (32%)
  Pallas kernels  23.5 us (16%)
  local copies, waits for them, and re-layouts  4.49 us (3%)
  between operations  1.64 us (1%)
    ppermute x10, waiting for transfers between devices, turn(): return lax.ppermute(x, 'space', pairs)  31.5 us
    ppermute x11, starting transfers between devices, swap(): return lax.ppermute(x, 'space', [(i, i ^ 1) for i in range(2 * Z)])  18.7 us
    ppermute x10, starting transfers between devices, turn(): return lax.ppermute(x, 'space', pairs)  18.1 us
    pallas_call x1, Pallas kernels, attention(): pl.pallas_call(attention_kernel, in_specs=[SCALARS] + [FAR] * (PIECES + 4...  15.5 us
    ppermute x2, starting transfers between devices, swap_lo(): return lax.ppermute(x, 'dp', [(i, i ^ XY) for i in range(2 * XY)])  9.19 us
    ppermute x6, waiting for transfers between devices, turn_dp(): return lax.ppermute(x, 'dp', pairs)  8.75 us
    ppermute x6, starting transfers between devices, turn_dp(): return lax.ppermute(x, 'dp', pairs)  8.41 us
    ppermute x2, starting transfers between devices, transpose_devices(): return lax.ppermute(x, ('dp', 'space'), pairs)  8.19 us
  transfers between devices with their start and end apart: 32, of which 13 were waited for; matrix products, arithmetic and copies ran while one was open for 2% of the time, Pallas kernels for 4%

profile of v3, /device:TPU:1, one launch (start us, length us, event | category | flops | bytes accessed | tf_op | source)
XLA Modules:
  0.0 144.6 jit_solution(15298354279378299386)
XLA Ops:
  2.1 4.5 %collective-permute-start.1 = (bf16[64,128]{1,0:T(8,128)(2,1)}, bf16[64,128]{1,0:T(8,128)(2,1)S(1)}, u32[]{:S(2)}, u32[]{:S(2)}) collective-permute-start(bf16[64,128]{1,0:T(8,128)(2,1)} %get-tuple-element.25), channel_id=1, source_target_pairs={{0,0},{1,32},{2,64},{3,96},{4,128},{5,160},{6,192},{7,224},{8,8},{... | collective-permute-start | bytes 49160 | tf_op jit(solution)/shard_map/ppermute | solution.py:341
  6.6 7.0 %collective-permute-start = (bf16[32,384]{1,0:T(8,128)(2,1)}, bf16[32,384]{1,0:T(8,128)(2,1)S(1)}, u32[]{:S(2)}, u32[]{:S(2)}) collective-permute-start(bf16[32,384]{1,0:T(8,128)(2,1)} %get-tuple-element.24.w_part), channel_id=1, source_target_pairs={{0,128},{8,136},{16,144},{24,152},{32,160},{40,168},{48,176},{56,1... | collective-permute-start | bytes 73736 | tf_op jit(solution)/shard_map/ppermute | solution.py:335
  15.6 2.1 %shard_map.85.refs_0_ = bf16[128,2048]{1,0:T(8,128)(2,1)} custom-call(bf16[128,1024]{1,0:T(8,128)(2,1)} %bitcast.11, bf16[128,1024]{1,0:T(8,128)(2,1)} %bitcast.13, bf16[1,2048]{1,0:T(2,128)(2,1)} %constant_dynamic-slice_fusion.row), custom_call_target="tpu_custom_call" | custom-call | tf_op jit(solution)/shard_map/pallas_call | solution.py:181
  17.7 2.0 %collective-permute-start.6 = (bf16[128,2048]{1,0:T(8,128)(2,1)}, bf16[128,2048]{1,0:T(8,128)(2,1)S(1)}, u32[]{:S(2)}, u32[]{:S(2)}) collective-permute-start(bf16[128,2048]{1,0:T(8,128)(2,1)} %shard_map.85.refs_0_), channel_id=1, source_target_pairs={{0,6},{1,7},{2,0},{3,1},{4,2},{5,3},{6,4},{7,5},{8,14},{9,15},{10,... | collective-permute-start | bytes 1572872 | tf_op jit(solution)/shard_map/ppermute | solution.py:327
  21.5 2.8 %collective-permute-start.4 = (bf16[64,512]{1,0:T(8,128)(2,1)S(1)}, bf16[64,512]{1,0:T(8,128)(2,1)S(1)}, u32[]{:S(2)}, u32[]{:S(2)}) collective-permute-start(bf16[64,512]{1,0:T(8,128)(2,1)S(1)} %shard_map.87.refs_0_), channel_id=1, source_target_pairs={{0,24},{8,0},{16,8},{24,16},{32,56},{40,32},{48,40},{56,48},{64,88... | collective-permute-start | bytes 196616 | tf_op jit(solution)/shard_map/ppermute | solution.py:352
  25.6 3.6 %collective-permute-done.3.refs_2_ = bf16[64,512]{1,0:T(8,128)(2,1)S(1)} collective-permute-done((bf16[64,512]{1,0:T(8,128)(2,1)S(1)}, bf16[64,512]{1,0:T(8,128)(2,1)S(1)}, u32[]{:S(2)}, u32[]{:S(2)}) %collective-permute-start.3) | collective-permute-done | bytes 65568 | tf_op jit(solution)/shard_map/ppermute | solution.py:352
  35.0 2.6 %collective-permute-done.8.refs_12_ = bf16[4,64,512]{2,1,0:T(8,128)(2,1)S(1)} collective-permute-done((bf16[4,64,512]{2,1,0:T(8,128)(2,1)S(1)}, bf16[4,64,512]{2,1,0:T(8,128)(2,1)S(1)}, u32[]{:S(2)}, u32[]{:S(2)}) %collective-permute-start.8) | collective-permute-done | bytes 262176 | tf_op jit(solution)/shard_map/ppermute | solution.py:352
  37.6 5.9 %collective-permute-start.11 = (bf16[128,2048]{1,0:T(8,128)(2,1)}, bf16[128,2048]{1,0:T(8,128)(2,1)S(1)}, u32[]{:S(2)}, u32[]{:S(2)}) collective-permute-start(bf16[128,2048]{1,0:T(8,128)(2,1)} %shard_map.85.refs_0_), channel_id=1, source_target_pairs={{0,1},{1,0},{2,3},{3,2},{4,5},{5,4},{6,7},{7,6},{8,9},{9,8},{10,11... | collective-permute-start | bytes 1572872 | tf_op jit(solution)/shard_map/ppermute | solution.py:331
  45.1 3.4 %collective-permute-start.10 = (bf16[64,2048]{1,0:T(8,128)(2,1)S(1)}, bf16[64,2048]{1,0:T(8,128)(2,1)S(1)}, u32[]{:S(2)}, u32[]{:S(2)}) collective-permute-start(bf16[64,2048]{1,0:T(8,128)(2,1)S(1)} %slice.22), channel_id=1, source_target_pairs={{0,6},{1,7},{2,0},{3,1},{4,2},{5,3},{6,4},{7,5},{8,14},{9,15},{10,... | collective-permute-start | bytes 786440 | tf_op jit(solution)/shard_map/ppermute | solution.py:327
  50.3 9.8 %collective-permute-done.10.refs_3_ = bf16[64,2048]{1,0:T(8,128)(2,1)S(1)} collective-permute-done((bf16[64,2048]{1,0:T(8,128)(2,1)S(1)}, bf16[64,2048]{1,0:T(8,128)(2,1)S(1)}, u32[]{:S(2)}, u32[]{:S(2)}) %collective-permute-start.10) | collective-permute-done | bytes 262176 | tf_op jit(solution)/shard_map/ppermute | solution.py:327
  60.7 3.3 %collective-permute-start.13 = (bf16[64,2048]{1,0:T(8,128)(2,1)S(1)}, bf16[64,2048]{1,0:T(8,128)(2,1)S(1)}, u32[]{:S(2)}, u32[]{:S(2)}) collective-permute-start(bf16[64,2048]{1,0:T(8,128)(2,1)S(1)} %collective-permute-done.9.refs_2_), channel_id=1, source_target_pairs={{0,1},{1,0},{2,3},{3,2},{4,5},{5,4},{6,7},{7,6},{8,9},{9,8},{10,11... | collective-permute-start | bytes 786440 | tf_op jit(solution)/shard_map/ppermute | solution.py:331
  66.9 15.5 %shard_map.89 = (bf16[16,64,512]{2,1,0:T(8,128)(2,1)}, bf16[128,1024]{1,0:T(8,128)(2,1)}, bf16[384,1024]{1,0:T(8,128)(2,1)}, bf16[128,1024]{1,0:T(8,128)(2,1)}, ...) custom-call(s32[4]{0:T(128)} %copy-done.4, bf16[128,2048]{1,0:T(8,128)(2,1)} %shard_map.85.refs_0_, ...), custom_call_target="tpu_custom_call" | custom-call | flops 17179869184 | bytes 8388608 | tf_op jit(solution)/shard_map/pallas_call | solution.py:136
  82.5 5.1 %all-to-all-start = ((bf16[16,64,512]{2,1,0:T(8,128)(2,1)}), bf16[16,64,512]{2,1,0:T(8,128)(2,1)S(1)}, u32[]{:S(2)}, u32[]{:S(2)}) async-start(bf16[16,64,512]{2,1,0:T(8,128)(2,1)} %get-tuple-element.33), calls=%async_computation | async-start | bytes 2097152 | tf_op jit(solution)/shard_map/all_to_all | solution.py:357
  88.7 2.4 %collective-permute-done.18 = bf16[128,1024]{1,0:T(8,128)(2,1)S(1)} collective-permute-done((bf16[128,1024]{1,0:T(8,128)(2,1)}, bf16[128,1024]{1,0:T(8,128)(2,1)S(1)}, u32[]{:S(2)}, u32[]{:S(2)}) %collective-permute-start.18) | collective-permute-done | bytes 262176 | tf_op jit(solution)/shard_map/ppermute | solution.py:331
  92.1 2.4 %collective-permute-start.19 = (bf16[128,1024]{1,0:T(8,128)(2,1)S(1)}, bf16[128,1024]{1,0:T(8,128)(2,1)S(1)}, u32[]{:S(2)}, u32[]{:S(2)}) collective-permute-start(bf16[128,1024]{1,0:T(8,128)(2,1)S(1)} %add_convert_fusion.1), channel_id=1, source_target_pairs={{0,4},{1,5},{2,6},{3,7},{4,0},{5,1},{6,2},{7,3},{8,12},{9,13},{10,... | collective-permute-start | bytes 786440 | tf_op jit(solution)/shard_map/ppermute | solution.py:327
  94.5 15.3 %collective-permute-done.19.refs_2_ = bf16[128,1024]{1,0:T(8,128)(2,1)S(1)} collective-permute-done((bf16[128,1024]{1,0:T(8,128)(2,1)S(1)}, bf16[128,1024]{1,0:T(8,128)(2,1)S(1)}, u32[]{:S(2)}, u32[]{:S(2)}) %collective-permute-start.19) | collective-permute-done | bytes 262176 | tf_op jit(solution)/shard_map/ppermute | solution.py:327
  111.1 3.7 %collective-permute-start.21 = (bf16[64,128]{1,0:T(8,128)(2,1)S(1)}, bf16[64,128]{1,0:T(8,128)(2,1)S(1)}, u32[]{:S(2)}, u32[]{:S(2)}) collective-permute-start(bf16[64,128]{1,0:T(8,128)(2,1)S(1)} %get-tuple-element.39), channel_id=1, source_target_pairs={{0,0},{1,32},{2,64},{3,96},{4,128},{5,160},{6,192},{7,224},{8,8},{... | collective-permute-start | bytes 49160 | tf_op jit(solution)/shard_map/ppermute | solution.py:341
  115.2 2.2 %collective-permute-start.20 = (bf16[32,384]{1,0:T(8,128)(2,1)S(1)}, bf16[32,384]{1,0:T(8,128)(2,1)S(1)}, u32[]{:S(2)}, u32[]{:S(2)}) collective-permute-start(bf16[32,384]{1,0:T(8,128)(2,1)S(1)} %get-tuple-element.38), channel_id=1, source_target_pairs={{0,128},{8,136},{16,144},{24,152},{32,160},{40,168},{48,176},{56,1... | collective-permute-start | bytes 73736 | tf_op jit(solution)/shard_map/ppermute | solution.py:335
  118.6 3.5 %collective-permute-start.22 = (bf16[128,1024]{1,0:T(8,128)(2,1)S(1)}, bf16[128,1024]{1,0:T(8,128)(2,1)S(1)}, u32[]{:S(2)}, u32[]{:S(2)}) collective-permute-start(bf16[128,1024]{1,0:T(8,128)(2,1)S(1)} %get-tuple-element.40), channel_id=1, source_target_pairs={{0,6},{1,7},{2,0},{3,1},{4,2},{5,3},{6,4},{7,5},{8,14},{9,15},{10,... | collective-permute-start | bytes 786440 | tf_op jit(solution)/shard_map/ppermute | solution.py:327
  122.1 2.1 %collective-permute-start.27 = (bf16[32,640]{1,0:T(8,128)(2,1)S(1)}, bf16[32,640]{1,0:T(8,128)(2,1)S(1)}, u32[]{:S(2)}, u32[]{:S(2)}) collective-permute-start(bf16[32,640]{1,0:T(8,128)(2,1)S(1)} %pad_maximum_fusion.refs_0_), channel_id=1, source_target_pairs={{0,1},{1,0},{2,3},{3,2},{4,5},{5,4},{6,7},{7,6},{8,9},{9,8},{10,11... | collective-permute-start | bytes 122888 | tf_op jit(solution)/shard_map/ppermute | solution.py:331
  124.2 3.9 %collective-permute-start.26 = (bf16[32,640]{1,0:T(8,128)(2,1)S(1)}, bf16[32,640]{1,0:T(8,128)(2,1)S(1)}, u32[]{:S(2)}, u32[]{:S(2)}) collective-permute-start(bf16[32,640]{1,0:T(8,128)(2,1)S(1)} %pad_maximum_fusion.refs_0_), channel_id=1, source_target_pairs={{0,6},{1,7},{2,0},{3,1},{4,2},{5,3},{6,4},{7,5},{8,14},{9,15},{10,... | collective-permute-start | bytes 122888 | tf_op jit(solution)/shard_map/ppermute | solution.py:327
  128.0 2.6 %collective-permute-start.25 = (bf16[32,640]{1,0:T(8,128)(2,1)S(1)}, bf16[32,640]{1,0:T(8,128)(2,1)S(1)}, u32[]{:S(2)}, u32[]{:S(2)}) collective-permute-start(bf16[32,640]{1,0:T(8,128)(2,1)S(1)} %pad_maximum_fusion.refs_0_), channel_id=1, source_target_pairs={{0,4},{1,5},{2,6},{3,7},{4,0},{5,1},{6,2},{7,3},{8,12},{9,13},{10,... | collective-permute-start | bytes 122888 | tf_op jit(solution)/shard_map/ppermute | solution.py:327
  130.6 6.3 %collective-permute-done.26.refs_3_ = bf16[32,640]{1,0:T(8,128)(2,1)S(1)} collective-permute-done((bf16[32,640]{1,0:T(8,128)(2,1)S(1)}, bf16[32,640]{1,0:T(8,128)(2,1)S(1)}, u32[]{:S(2)}, u32[]{:S(2)}) %collective-permute-start.26) | collective-permute-done | bytes 40992 | tf_op jit(solution)/shard_map/ppermute | solution.py:327
  138.2 2.9 %collective-permute-start.28 = (bf16[32,640]{1,0:T(8,128)(2,1)S(1)}, bf16[32,640]{1,0:T(8,128)(2,1)S(1)}, u32[]{:S(2)}, u32[]{:S(2)}) collective-permute-start(bf16[32,640]{1,0:T(8,128)(2,1)S(1)} %collective-permute-done.24.refs_1_), channel_id=1, source_target_pairs={{0,1},{1,0},{2,3},{3,2},{4,5},{5,4},{6,7},{7,6},{8,9},{9,8},{10,11... | collective-permute-start | bytes 122888 | tf_op jit(solution)/shard_map/ppermute | solution.py:331
  (101 shorter events, 28.2 us)
Async XLA Ops:
  2.1 15.6 %collective-permute-start.1 = (bf16[64,128]{1,0:T(8,128)(2,1)}, bf16[64,128]{1,0:T(8,128)(2,1)S(1)}, u32[]{:S(2)}, u32[]{:S(2)}) collective-permute-start(bf16[64,128]{1,0:T(8,128)(2,1)} %get-tuple-element.25), channel_id=1, source_target_pairs={{0,0},{1,32},{2,64},{3,96},{4,128},{5,160},{6,192},{7,224},{8,8},{... | collective-permute-start | bytes 49160 | tf_op jit(solution)/shard_map/ppermute | solution.py:341
  6.6 11.1 %collective-permute-start = (bf16[32,384]{1,0:T(8,128)(2,1)}, bf16[32,384]{1,0:T(8,128)(2,1)S(1)}, u32[]{:S(2)}, u32[]{:S(2)}) collective-permute-start(bf16[32,384]{1,0:T(8,128)(2,1)} %get-tuple-element.24.w_part), channel_id=1, source_target_pairs={{0,128},{8,136},{16,144},{24,152},{32,160},{40,168},{48,176},{56,1... | collective-permute-start | bytes 73736 | tf_op jit(solution)/shard_map/ppermute | solution.py:335
  17.7 27.4 %collective-permute-start.6 = (bf16[128,2048]{1,0:T(8,128)(2,1)}, bf16[128,2048]{1,0:T(8,128)(2,1)S(1)}, u32[]{:S(2)}, u32[]{:S(2)}) collective-permute-start(bf16[128,2048]{1,0:T(8,128)(2,1)} %shard_map.85.refs_0_), channel_id=1, source_target_pairs={{0,6},{1,7},{2,0},{3,1},{4,2},{5,3},{6,4},{7,5},{8,14},{9,15},{10,... | collective-permute-start | bytes 1572872 | tf_op jit(solution)/shard_map/ppermute | solution.py:327
  19.7 25.4 %collective-permute-start.5 = (bf16[128,2048]{1,0:T(8,128)(2,1)}, bf16[128,2048]{1,0:T(8,128)(2,1)S(1)}, u32[]{:S(2)}, u32[]{:S(2)}) collective-permute-start(bf16[128,2048]{1,0:T(8,128)(2,1)} %shard_map.85.refs_0_), channel_id=1, source_target_pairs={{0,2},{1,3},{2,4},{3,5},{4,6},{5,7},{6,0},{7,1},{8,10},{9,11},{10,... | collective-permute-start | bytes 1572872 | tf_op jit(solution)/shard_map/ppermute | solution.py:327
  24.3 4.9 %collective-permute-start.3 = (bf16[64,512]{1,0:T(8,128)(2,1)S(1)}, bf16[64,512]{1,0:T(8,128)(2,1)S(1)}, u32[]{:S(2)}, u32[]{:S(2)}) collective-permute-start(bf16[64,512]{1,0:T(8,128)(2,1)S(1)} %shard_map.87.refs_0_), channel_id=1, source_target_pairs={{0,16},{8,24},{16,0},{24,8},{32,48},{40,56},{48,32},{56,40},{64,80... | collective-permute-start | bytes 196616 | tf_op jit(solution)/shard_map/ppermute | solution.py:352
  24.6 5.3 %collective-permute-start.2 = (bf16[64,512]{1,0:T(8,128)(2,1)S(1)}, bf16[64,512]{1,0:T(8,128)(2,1)S(1)}, u32[]{:S(2)}, u32[]{:S(2)}) collective-permute-start(bf16[64,512]{1,0:T(8,128)(2,1)S(1)} %shard_map.87.refs_0_), channel_id=1, source_target_pairs={{0,8},{8,16},{16,24},{24,0},{32,40},{40,48},{48,56},{56,32},{64,72... | collective-permute-start | bytes 196616 | tf_op jit(solution)/shard_map/ppermute | solution.py:352
  30.5 7.2 %collective-permute-start.8 = (bf16[4,64,512]{2,1,0:T(8,128)(2,1)S(1)}, bf16[4,64,512]{2,1,0:T(8,128)(2,1)S(1)}, u32[]{:S(2)}, u32[]{:S(2)}) collective-permute-start(bf16[4,64,512]{2,1,0:T(8,128)(2,1)S(1)} %shard_map.88.refs_10_), channel_id=1, source_target_pairs={{0,64},{8,72},{16,80},{24,88},{32,96},{40,104},{48,112},{56,120},{... | collective-permute-start | bytes 786440 | tf_op jit(solution)/shard_map/ppermute | solution.py:352
  32.4 12.7 %collective-permute-start.7 = (bf16[4,64,512]{2,1,0:T(8,128)(2,1)S(1)}, bf16[4,64,512]{2,1,0:T(8,128)(2,1)S(1)}, u32[]{:S(2)}, u32[]{:S(2)}) collective-permute-start(bf16[4,64,512]{2,1,0:T(8,128)(2,1)S(1)} %shard_map.88.refs_10_), channel_id=1, source_target_pairs={{0,32},{8,40},{16,48},{24,56},{32,64},{40,72},{48,80},{56,88},{64,... | collective-permute-start | bytes 786440 | tf_op jit(solution)/shard_map/ppermute | solution.py:352
  33.8 16.4 %collective-permute-start.16 = (bf16[4,64,512]{2,1,0:T(8,128)(2,1)S(1)}, bf16[4,64,512]{2,1,0:T(8,128)(2,1)S(1)}, u32[]{:S(2)}, u32[]{:S(2)}) collective-permute-start(bf16[4,64,512]{2,1,0:T(8,128)(2,1)S(1)} %shard_map.88.refs_10_), channel_id=1, source_target_pairs={{0,96},{8,104},{16,112},{24,120},{32,0},{40,8},{48,16},{56,24},{64... | collective-permute-start | bytes 786440 | tf_op jit(solution)/shard_map/ppermute | solution.py:352
  37.6 26.4 %collective-permute-start.11 = (bf16[128,2048]{1,0:T(8,128)(2,1)}, bf16[128,2048]{1,0:T(8,128)(2,1)S(1)}, u32[]{:S(2)}, u32[]{:S(2)}) collective-permute-start(bf16[128,2048]{1,0:T(8,128)(2,1)} %shard_map.85.refs_0_), channel_id=1, source_target_pairs={{0,1},{1,0},{2,3},{3,2},{4,5},{5,4},{6,7},{7,6},{8,9},{9,8},{10,11... | collective-permute-start | bytes 1572872 | tf_op jit(solution)/shard_map/ppermute | solution.py:331
  45.1 15.0 %collective-permute-start.10 = (bf16[64,2048]{1,0:T(8,128)(2,1)S(1)}, bf16[64,2048]{1,0:T(8,128)(2,1)S(1)}, u32[]{:S(2)}, u32[]{:S(2)}) collective-permute-start(bf16[64,2048]{1,0:T(8,128)(2,1)S(1)} %slice.22), channel_id=1, source_target_pairs={{0,6},{1,7},{2,0},{3,1},{4,2},{5,3},{6,4},{7,5},{8,14},{9,15},{10,... | collective-permute-start | bytes 786440 | tf_op jit(solution)/shard_map/ppermute | solution.py:327
  48.6 12.2 %collective-permute-start.9 = (bf16[64,2048]{1,0:T(8,128)(2,1)S(1)}, bf16[64,2048]{1,0:T(8,128)(2,1)S(1)}, u32[]{:S(2)}, u32[]{:S(2)}) collective-permute-start(bf16[64,2048]{1,0:T(8,128)(2,1)S(1)} %slice.21), channel_id=1, source_target_pairs={{0,2},{1,3},{2,4},{3,5},{4,6},{5,7},{6,0},{7,1},{8,10},{9,11},{10,... | collective-permute-start | bytes 786440 | tf_op jit(solution)/shard_map/ppermute | solution.py:327
  48.6 16.6 %collective-permute-start.12 = (bf16[128,2048]{1,0:T(8,128)(2,1)S(1)}, bf16[128,2048]{1,0:T(8,128)(2,1)S(1)}, u32[]{:S(2)}, u32[]{:S(2)}) collective-permute-start(bf16[128,2048]{1,0:T(8,128)(2,1)S(1)} %collective-permute-done.5.refs_1_), channel_id=1, source_target_pairs={{0,1},{1,0},{2,3},{3,2},{4,5},{5,4},{6,7},{7,6},{8,9},{9,8},{10,11... | collective-permute-start | bytes 1572872 | tf_op jit(solution)/shard_map/ppermute | solution.py:331
  50.2 15.0 %collective-permute-start.15 = (bf16[128,2048]{1,0:T(8,128)(2,1)S(1)}, bf16[128,2048]{1,0:T(8,128)(2,1)S(1)}, u32[]{:S(2)}, u32[]{:S(2)}) collective-permute-start(bf16[128,2048]{1,0:T(8,128)(2,1)S(1)} %collective-permute-done.6.refs_4_), channel_id=1, source_target_pairs={{0,1},{1,0},{2,3},{3,2},{4,5},{5,4},{6,7},{7,6},{8,9},{9,8},{10,11... | collective-permute-start | bytes 1572872 | tf_op jit(solution)/shard_map/ppermute | solution.py:331
  82.5 27.2 %all-to-all-start = ((bf16[16,64,512]{2,1,0:T(8,128)(2,1)}), bf16[16,64,512]{2,1,0:T(8,128)(2,1)S(1)}, u32[]{:S(2)}, u32[]{:S(2)}) async-start(bf16[16,64,512]{2,1,0:T(8,128)(2,1)} %get-tuple-element.33), calls=%async_computation | async-start | bytes 2097152 | tf_op jit(solution)/shard_map/all_to_all | solution.py:357
  87.6 27.2 %collective-permute-start.17 = (bf16[384,1024]{1,0:T(8,128)(2,1)}, bf16[384,1024]{1,0:T(8,128)(2,1)S(1)}, u32[]{:S(2)}, u32[]{:S(2)}) collective-permute-start(bf16[384,1024]{1,0:T(8,128)(2,1)} %get-tuple-element.31), channel_id=1, source_target_pairs={{0,1},{1,0},{2,3},{3,2},{4,5},{5,4},{6,7},{7,6},{8,9},{9,8},{10,11... | collective-permute-start | bytes 2359304 | tf_op jit(solution)/shard_map/ppermute | solution.py:331
  92.1 17.7 %collective-permute-start.19 = (bf16[128,1024]{1,0:T(8,128)(2,1)S(1)}, bf16[128,1024]{1,0:T(8,128)(2,1)S(1)}, u32[]{:S(2)}, u32[]{:S(2)}) collective-permute-start(bf16[128,1024]{1,0:T(8,128)(2,1)S(1)} %add_convert_fusion.1), channel_id=1, source_target_pairs={{0,4},{1,5},{2,6},{3,7},{4,0},{5,1},{6,2},{7,3},{8,12},{9,13},{10,... | collective-permute-start | bytes 786440 | tf_op jit(solution)/shard_map/ppermute | solution.py:327
  111.1 6.2 %collective-permute-start.21 = (bf16[64,128]{1,0:T(8,128)(2,1)S(1)}, bf16[64,128]{1,0:T(8,128)(2,1)S(1)}, u32[]{:S(2)}, u32[]{:S(2)}) collective-permute-start(bf16[64,128]{1,0:T(8,128)(2,1)S(1)} %get-tuple-element.39), channel_id=1, source_target_pairs={{0,0},{1,32},{2,64},{3,96},{4,128},{5,160},{6,192},{7,224},{8,8},{... | collective-permute-start | bytes 49160 | tf_op jit(solution)/shard_map/ppermute | solution.py:341
  118.6 24.8 %collective-permute-start.22 = (bf16[128,1024]{1,0:T(8,128)(2,1)S(1)}, bf16[128,1024]{1,0:T(8,128)(2,1)S(1)}, u32[]{:S(2)}, u32[]{:S(2)}) collective-permute-start(bf16[128,1024]{1,0:T(8,128)(2,1)S(1)} %get-tuple-element.40), channel_id=1, source_target_pairs={{0,6},{1,7},{2,0},{3,1},{4,2},{5,3},{6,4},{7,5},{8,14},{9,15},{10,... | collective-permute-start | bytes 786440 | tf_op jit(solution)/shard_map/ppermute | solution.py:327
  122.1 21.3 %collective-permute-start.23 = (bf16[128,1024]{1,0:T(8,128)(2,1)S(1)}, bf16[128,1024]{1,0:T(8,128)(2,1)S(1)}, u32[]{:S(2)}, u32[]{:S(2)}) collective-permute-start(bf16[128,1024]{1,0:T(8,128)(2,1)S(1)} %get-tuple-element.42), channel_id=1, source_target_pairs={{0,2},{1,3},{2,4},{3,5},{4,6},{5,7},{6,0},{7,1},{8,10},{9,11},{10,... | collective-permute-start | bytes 786440 | tf_op jit(solution)/shard_map/ppermute | solution.py:327
  122.1 8.5 %collective-permute-start.27 = (bf16[32,640]{1,0:T(8,128)(2,1)S(1)}, bf16[32,640]{1,0:T(8,128)(2,1)S(1)}, u32[]{:S(2)}, u32[]{:S(2)}) collective-permute-start(bf16[32,640]{1,0:T(8,128)(2,1)S(1)} %pad_maximum_fusion.refs_0_), channel_id=1, source_target_pairs={{0,1},{1,0},{2,3},{3,2},{4,5},{5,4},{6,7},{7,6},{8,9},{9,8},{10,11... | collective-permute-start | bytes 122888 | tf_op jit(solution)/shard_map/ppermute | solution.py:331
  124.2 12.7 %collective-permute-start.26 = (bf16[32,640]{1,0:T(8,128)(2,1)S(1)}, bf16[32,640]{1,0:T(8,128)(2,1)S(1)}, u32[]{:S(2)}, u32[]{:S(2)}) collective-permute-start(bf16[32,640]{1,0:T(8,128)(2,1)S(1)} %pad_maximum_fusion.refs_0_), channel_id=1, source_target_pairs={{0,6},{1,7},{2,0},{3,1},{4,2},{5,3},{6,4},{7,5},{8,14},{9,15},{10,... | collective-permute-start | bytes 122888 | tf_op jit(solution)/shard_map/ppermute | solution.py:327
  128.0 9.7 %collective-permute-start.25 = (bf16[32,640]{1,0:T(8,128)(2,1)S(1)}, bf16[32,640]{1,0:T(8,128)(2,1)S(1)}, u32[]{:S(2)}, u32[]{:S(2)}) collective-permute-start(bf16[32,640]{1,0:T(8,128)(2,1)S(1)} %pad_maximum_fusion.refs_0_), channel_id=1, source_target_pairs={{0,4},{1,5},{2,6},{3,7},{4,0},{5,1},{6,2},{7,3},{8,12},{9,13},{10,... | collective-permute-start | bytes 122888 | tf_op jit(solution)/shard_map/ppermute | solution.py:327
  130.6 7.6 %collective-permute-start.24 = (bf16[32,640]{1,0:T(8,128)(2,1)S(1)}, bf16[32,640]{1,0:T(8,128)(2,1)S(1)}, u32[]{:S(2)}, u32[]{:S(2)}) collective-permute-start(bf16[32,640]{1,0:T(8,128)(2,1)S(1)} %pad_maximum_fusion.refs_0_), channel_id=1, source_target_pairs={{0,2},{1,3},{2,4},{3,5},{4,6},{5,7},{6,0},{7,1},{8,10},{9,11},{10,... | collective-permute-start | bytes 122888 | tf_op jit(solution)/shard_map/ppermute | solution.py:327
  (30 other events, 506.5 us)

commit v4 on v3

--- a/solution.py
+++ b/solution.py
@@ -44,40 +44,70 @@
     return lane < PAIR // 2, lane >= PAIR // 2
 
 
-def attention_kernel(where, *refs):
-    pieces, parts, rest = refs[:PIECES], refs[PIECES : PIECES + 4], refs[PIECES + 4 :]
-    grads, *results = rest[:7]
-    x, weights, wq, wo, qkv, att, d_att, dqkv, turned, sent, terms, sems = rest[7:]
-    copies, at = [], 0
-    for i, part in enumerate(parts):
-        copies.append(pltpu.make_async_copy(part, weights.at[i], sems.at[PIECES + i]))
-    for i, piece in enumerate(pieces):
-        to = x.at[at : at + piece.shape[0], :]
-        copies.append(pltpu.make_async_copy(piece, to, sems.at[i]))
-        at += piece.shape[0]
-    for copy in copies:
-        copy.start()
-    for far in range(4):
-        copies[far].wait()
+def project_kernel(where, *refs):
+    pieces, parts, (qkvd, wq, wo, x) = refs[:6], refs[6:10], refs[10:]
+    for far, part in enumerate(parts):
         col = lax.rem(where[2] - far + 4, 4)
         for lo in range(2):
             half = slice(lo * ROWS, (lo + 1) * ROWS)
             columns = pl.ds(pl.multiple_of((lo * 4 + col) * PAIR, PAIR), PAIR)
             for y in range(4):
                 at = pl.multiple_of(((lo * 4 + col) * 4 + y) * ROWS, ROWS)
-                wq[pl.ds(at, ROWS), :] = weights[far, y, half, :QKV]
-                wo[y * ROWS : (y + 1) * ROWS, columns] = weights[far, y, half, QKV:]
+                wq[pl.ds(at, ROWS), :] = part[y, half, :QKV]
+                wo[y * ROWS : (y + 1) * ROWS, columns] = part[y, half, QKV:]
+    for i, piece in enumerate(pieces):
+        x[i * CELLS : (i + 1) * CELLS, :] = piece[...]
+    qkvd[:, :QKV] = nn(x[:, :C], wq[...]).astype(BF16)
+    qkvd[:, QKV:] = nt(x[:, C:], wo[...]).astype(BF16)
+
+
+def project(where, pieces, parts):
+    return pl.pallas_call(
+        project_kernel,
+        in_specs=[SCALARS] + [WHOLE] * 10,
+        out_shape=(struct((6 * CELLS, QKV + PAIR)), struct((C, QKV)), struct((PAIR, C))),
+        scratch_shapes=[pltpu.VMEM((6 * CELLS, 2 * C), BF16)],
+        compiler_params=PARAMS,
+        cost_estimate=CHEAP,
+    )(where, *pieces, *parts)
+
+
+def attention_kernel(*refs):
+    pieces, rest = refs[:PIECES], refs[PIECES:]
+    first, wq_far, wo_far, grads, *results = rest[:10]
+    x, wq, wo, qkv, att, dqkv, turned, sent, terms, sems = rest[10:]
+    starts = (0, 128, 256, 320, 384, 512, 640, 768, 832, 896)
+    late = (2, 3, 7, 8)
+    copies = [pltpu.make_async_copy(wq_far, wq, sems.at[PIECES])]
+    copies.append(pltpu.make_async_copy(wo_far, wo, sems.at[PIECES + 1]))
+    for i in late:
+        to = x.at[starts[i] : starts[i] + pieces[i].shape[0], :]
+        copies.append(pltpu.make_async_copy(pieces[i], to, sems.at[i]))
+    for i, (at, to, size) in enumerate(
+        ((0, 0, 256), (256, 384, 128), (384, 512, 256), (640, 896, 128))
+    ):
+        source = first.at[at : at + size, :]
+        copies.append(
+            pltpu.make_async_copy(source, qkv.at[to : to + size, :], sems.at[PIECES + 2 + i])
+        )
+    rest_of_x = []
+    for i in range(PIECES):
+        if i not in late:
+            to = x.at[starts[i] : starts[i] + pieces[i].shape[0], :]
+            rest_of_x.append(pltpu.make_async_copy(pieces[i], to, sems.at[i]))
+    for copy in copies + rest_of_x:
+        copy.start()
+    for copy in copies:
+        copy.wait()
     cells = Z * CELLS
-    for core in range(2):
-        rows = slice(core * cells, (core + 1) * cells)
-        for copy in copies[4 + core * PIECES // 2 : 4 + (core + 1) * PIECES // 2]:
-            copy.wait()
-        qkv[rows, :] = nn(x[rows, :C], wq[...]).astype(BF16)
-        d_att[rows, :] = nt(x[rows, C:], wo[...]).astype(BF16)
+    for at in (256, 768):
+        rows = slice(at, at + CELLS)
+        qkv[rows, :QKV] = nn(x[rows, :C], wq[...]).astype(BF16)
+        qkv[rows, QKV:] = nt(x[rows, C:], wo[...]).astype(BF16)
     q = qkv[:, :PAIR] * jnp.bfloat16(0.125)
     k = qkv[:, PAIR : 2 * PAIR]
-    v = qkv[:, 2 * PAIR :]
-    d = d_att[...]
+    v = qkv[:, 2 * PAIR : QKV]
+    d = qkv[:, QKV:]
     zero = jnp.zeros_like(q)
     for head, mine_head in enumerate(heads()):
         qh = jnp.where(mine_head, q, zero)
@@ -103,6 +133,8 @@
             turned[PAIR:, :] += dv
 
     dqkv[:, PAIR:] = turned[...].T.astype(BF16)
+    for copy in rest_of_x:
+        copy.wait()
     grad = tn(dqkv[...], x[:, :C]).T.astype(BF16)
     for lo in range(2):
         for xy in range(XY):
@@ -131,11 +163,11 @@
         copy.wait()
 
 
-def attention(where, pieces, parts):
+def attention(pieces, first, wq, wo):
     cells = 8 * CELLS
     return pl.pallas_call(
         attention_kernel,
-        in_specs=[SCALARS] + [FAR] * (PIECES + 4),
+        in_specs=[FAR] * (PIECES + 3),
         out_specs=[FAR] * 7,
         out_shape=(
             struct((XY, 2 * ROWS, QKV + PAIR)),
@@ -145,23 +177,21 @@
         ),
         scratch_shapes=[
             pltpu.VMEM((cells, 2 * C), BF16),
-            pltpu.VMEM((4, 4, 2 * ROWS, QKV + PAIR), BF16),
             pltpu.VMEM((C, QKV), BF16),
             pltpu.VMEM((PAIR, C), BF16),
-            pltpu.VMEM((cells, QKV), BF16),
-            pltpu.VMEM((cells, PAIR), BF16),
+            pltpu.VMEM((cells, QKV + PAIR), BF16),
             pltpu.VMEM((cells, PAIR), BF16),
             pltpu.VMEM((cells, QKV), BF16),
             pltpu.VMEM((2 * PAIR, cells), F32),
             pltpu.VMEM((XY, 2 * ROWS, QKV + PAIR), BF16),
             pltpu.VMEM((cells, C), BF16),
-            pltpu.SemaphoreType.DMA((PIECES + 4,)),
+            pltpu.SemaphoreType.DMA((PIECES + 6,)),
         ],
         compiler_params=PARAMS,
         cost_estimate=pl.CostEstimate(
             flops=2**34, bytes_accessed=2**23, transcendentals=2 * cells * cells
         ),
-    )(where, *pieces, *parts)
+    )(*pieces, first, wq, wo)
 
 
 def normalize(image, row):
@@ -380,28 +410,32 @@
     parts = join(where, packed)
     x = after(x, *packed)
     parts = [parts] + [turn_dp(parts, by, 0) for by in range(1, 4)]
-    one, three = after((one, three), parts[1], parts[2])
+    one, three = after((one, three), *parts)
     half = CELLS // 2
-    pieces = [x, one, turn(one[:half], 1), turn(three[half:], 3), three]
-    pieces += [swap(piece) for piece in pieces]
-    grads, far, near, two, own, one, three = attention(where, pieces, parts)
+    two = turn(one[:half], 1), turn(three[half:], 3)
+    others = [swap(piece) for piece in (x, one, three)]
+    first, wq, wo = project(where, [x, one, three, *others], parts)
+    two = after(two, first)
+    pieces = [x, one, *two, three]
+    pieces += [others[0], others[1], *[swap(piece) for piece in two], others[2]]
+    grads, far, near, two, own, one, three = attention(pieces, first, wq, wo)
     grads = over_xy(grads)
 
-    two = add(two, swap(far))
+    two = turn(add(two, swap(far)), 2)
     near = swap(near)
     own, one, three = (
         add(piece, near[i * CELLS : (i + 1) * CELLS]) for i, piece in enumerate((own, one, three))
     )
-    two = turn(two, 2)
-
-    near, far, go = add_up(where, after(grads, two))
+    one, three = turn(one, 3), turn(three, 1)
+    branch = finish(image, row, (own, one, two, three))
+
+    near, far, go = add_up(where, grads)
     go = transpose_devices(go)
     gq = (near + swap_lo(far).astype(F32)).astype(BF16)
     mine = jnp.concatenate([gq, go[:ROWS], go[ROWS:]], 1)
-    one, three = turn(after(one, mine), 3), turn(after(three, mine), 1)
+    mine = after(mine, two)
     every = [mine] + [turn(mine, by) for by in range(1, Z)]
     grad_q, grad_o = place(every + [swap(piece) for piece in every], where)
-    branch = finish(image, row, (own, one, two, three))
     return branch[None], grad_q, grad_o
 
 

time: 145 us -> 141 us (0.972)
  waiting for transfers between devices: 45.9 us -> 41.5 us
  Pallas kernels: 23.5 us -> 26.1 us
  starting transfers between devices: 67.7 us -> 65.3 us
    ppermute x10, waiting for transfers between devices: 31.5 us -> 6.73 us  [turn(): return lax.ppermute(x, 'space', pairs)]
    ppermute x2, waiting for transfers between devices: 1.21 us -> 10.5 us  [swap_lo(): return lax.ppermute(x, 'dp', [(i, i ^ XY) for i in range(2 * XY)])]
    all_to_all x1, waiting for transfers between devices: 0.01 us -> 6.9 us  [over_xy(): return lax.all_to_all(x, 'dp', 0, 0, axis_index_groups=groups, tiled=True)]
    ppermute x6, waiting for transfers between devices: 8.75 us -> 13.5 us  [turn_dp(): return lax.ppermute(x, 'dp', pairs)]
    ppermute x11, starting transfers between devices: 18.7 us -> 15.6 us  [swap(): return lax.ppermute(x, 'space', [(i, i ^ 1) for i in range(2 * Z)])]
    pallas_call x1 -> x2, Pallas kernels: 15.5 us -> 18.1 us  [the longest x1 13.6 us: attention(): pl.pallas_call(attention_kernel, in_specs=[FAR] * (PIECES + 3), out_specs...]
    ppermute x10, starting transfers between devices: 18.1 us -> 19.7 us  [turn(): return lax.ppermute(x, 'space', pairs)]
    unnamed x44 -> x42, local copies, waits for them, and re-layouts: 3.09 us -> 3.21 us
  transfers between devices with their start and end apart: 32 -> 32, of which waited for: 13 -> 13; matrix products, arithmetic and copies ran while one was open for 2% -> 2% of each run, Pallas kernels for 4% -> 7%
where the time goes in v4:
time: 141 us; the launch traced here: 140 us
  starting transfers between devices  65.3 us (46%)
  waiting for transfers between devices  41.5 us (29%)
  Pallas kernels  26.1 us (19%)
  local copies, waits for them, and re-layouts  4.61 us (3%)
  between operations  1.62 us (1%)
  other arithmetic  1.41 us (1%)
    ppermute x10, starting transfers between devices, turn(): return lax.ppermute(x, 'space', pairs)  19.7 us
    ppermute x11, starting transfers between devices, swap(): return lax.ppermute(x, 'space', [(i, i ^ 1) for i in range(2 * Z)])  15.6 us
    pallas_call x1, Pallas kernels, attention(): pl.pallas_call(attention_kernel, in_specs=[FAR] * (PIECES + 3), out_specs...  13.6 us
    ppermute x6, waiting for transfers between devices, turn_dp(): return lax.ppermute(x, 'dp', pairs)  13.5 us
    ppermute x2, waiting for transfers between devices, swap_lo(): return lax.ppermute(x, 'dp', [(i, i ^ XY) for i in range(2 * XY)])  10.5 us
    ppermute x2, starting transfers between devices, swap_lo(): return lax.ppermute(x, 'dp', [(i, i ^ XY) for i in range(2 * XY)])  9.43 us
    ppermute x2, starting transfers between devices, transpose_devices(): return lax.ppermute(x, ('dp', 'space'), pairs)  8.93 us
    ppermute x6, starting transfers between devices, turn_dp(): return lax.ppermute(x, 'dp', pairs)  7.29 us
  transfers between devices with their start and end apart: 32, of which 13 were waited for; matrix products, arithmetic and copies ran while one was open for 2% of the time, Pallas kernels for 7%

profile of v4, /device:TPU:1, one launch (start us, length us, event | category | flops | bytes accessed | tf_op | source)
XLA Modules:
  0.0 140.5 jit_solution(1380164441425671205)
XLA Ops:
  2.1 4.5 %collective-permute-start.1 = (bf16[64,128]{1,0:T(8,128)(2,1)}, bf16[64,128]{1,0:T(8,128)(2,1)S(1)}, u32[]{:S(2)}, u32[]{:S(2)}) collective-permute-start(bf16[64,128]{1,0:T(8,128)(2,1)} %get-tuple-element.28), channel_id=1, source_target_pairs={{0,0},{1,32},{2,64},{3,96},{4,128},{5,160},{6,192},{7,224},{8,8},{... | collective-permute-start | bytes 49160 | tf_op jit(solution)/shard_map/ppermute | solution.py:371
  6.6 7.0 %collective-permute-start = (bf16[32,384]{1,0:T(8,128)(2,1)}, bf16[32,384]{1,0:T(8,128)(2,1)S(1)}, u32[]{:S(2)}, u32[]{:S(2)}) collective-permute-start(bf16[32,384]{1,0:T(8,128)(2,1)} %get-tuple-element.27.w_part), channel_id=1, source_target_pairs={{0,128},{8,136},{16,144},{24,152},{32,160},{40,168},{48,176},{56,1... | collective-permute-start | bytes 73736 | tf_op jit(solution)/shard_map/ppermute | solution.py:365
  15.6 2.1 %shard_map.85.refs_0_ = bf16[128,2048]{1,0:T(8,128)(2,1)} custom-call(bf16[128,1024]{1,0:T(8,128)(2,1)} %bitcast.11, bf16[128,1024]{1,0:T(8,128)(2,1)} %bitcast.13, bf16[1,2048]{1,0:T(2,128)(2,1)} %constant_dynamic-slice_fusion.row), custom_call_target="tpu_custom_call" | custom-call | tf_op jit(solution)/shard_map/pallas_call | solution.py:211
  17.7 2.0 %collective-permute-start.6 = (bf16[128,2048]{1,0:T(8,128)(2,1)}, bf16[128,2048]{1,0:T(8,128)(2,1)S(1)}, u32[]{:S(2)}, u32[]{:S(2)}) collective-permute-start(bf16[128,2048]{1,0:T(8,128)(2,1)} %shard_map.85.refs_0_), channel_id=1, source_target_pairs={{0,6},{1,7},{2,0},{3,1},{4,2},{5,3},{6,4},{7,5},{8,14},{9,15},{10,... | collective-permute-start | bytes 1572872 | tf_op jit(solution)/shard_map/ppermute | solution.py:357
  21.4 2.8 %collective-permute-start.4 = (bf16[64,512]{1,0:T(8,128)(2,1)S(1)}, bf16[64,512]{1,0:T(8,128)(2,1)S(1)}, u32[]{:S(2)}, u32[]{:S(2)}) collective-permute-start(bf16[64,512]{1,0:T(8,128)(2,1)S(1)} %shard_map.87.refs_0_), channel_id=1, source_target_pairs={{0,24},{8,0},{16,8},{24,16},{32,56},{40,32},{48,40},{56,48},{64,88... | collective-permute-start | bytes 196616 | tf_op jit(solution)/shard_map/ppermute | solution.py:382
  25.6 3.6 %collective-permute-done.3.refs_2_ = bf16[64,512]{1,0:T(8,128)(2,1)S(1)} collective-permute-done((bf16[64,512]{1,0:T(8,128)(2,1)S(1)}, bf16[64,512]{1,0:T(8,128)(2,1)S(1)}, u32[]{:S(2)}, u32[]{:S(2)}) %collective-permute-start.3) | collective-permute-done | bytes 65568 | tf_op jit(solution)/shard_map/ppermute | solution.py:382
  30.5 2.8 %collective-permute-start.9 = (bf16[4,64,512]{2,1,0:T(8,128)(2,1)S(1)}, bf16[4,64,512]{2,1,0:T(8,128)(2,1)S(1)}, u32[]{:S(2)}, u32[]{:S(2)}) collective-permute-start(bf16[4,64,512]{2,1,0:T(8,128)(2,1)S(1)} %shard_map.88.refs_6_), channel_id=1, source_target_pairs={{0,96},{8,104},{16,112},{24,120},{32,0},{40,8},{48,16},{56,24},{64... | collective-permute-start | bytes 786440 | tf_op jit(solution)/shard_map/ppermute | solution.py:382
  33.9 6.3 %collective-permute-done.9.refs_9_ = bf16[4,64,512]{2,1,0:T(8,128)(2,1)S(1)} collective-permute-done((bf16[4,64,512]{2,1,0:T(8,128)(2,1)S(1)}, bf16[4,64,512]{2,1,0:T(8,128)(2,1)S(1)}, u32[]{:S(2)}, u32[]{:S(2)}) %collective-permute-start.9) | collective-permute-done | bytes 262176 | tf_op jit(solution)/shard_map/ppermute | solution.py:382
  40.2 5.1 %collective-permute-start.12 = (bf16[128,2048]{1,0:T(8,128)(2,1)}, bf16[128,2048]{1,0:T(8,128)(2,1)S(1)}, u32[]{:S(2)}, u32[]{:S(2)}) collective-permute-start(bf16[128,2048]{1,0:T(8,128)(2,1)} %shard_map.85.refs_0_), channel_id=1, source_target_pairs={{0,1},{1,0},{2,3},{3,2},{4,5},{5,4},{6,7},{7,6},{8,9},{9,8},{10,11... | collective-permute-start | bytes 1572872 | tf_op jit(solution)/shard_map/ppermute | solution.py:361
  45.4 2.6 %collective-permute-done.7.refs_7_ = bf16[4,64,512]{2,1,0:T(8,128)(2,1)S(1)} collective-permute-done((bf16[4,64,512]{2,1,0:T(8,128)(2,1)S(1)}, bf16[4,64,512]{2,1,0:T(8,128)(2,1)S(1)}, u32[]{:S(2)}, u32[]{:S(2)}) %collective-permute-start.7) | collective-permute-done | bytes 262176 | tf_op jit(solution)/shard_map/ppermute | solution.py:382
  53.3 4.5 %shard_map.89 = (bf16[768,512]{1,0:T(8,128)(2,1)}, bf16[1024,384]{1,0:T(8,128)(2,1)}, bf16[128,1024]{1,0:T(8,128)(2,1)}) custom-call(s32[4]{0:T(128)} %copy-done.4, bf16[128,2048]{1,0:T(8,128)(2,1)} %shard_map.85.refs_0_, bf16[128,2048]{1,0:T(8,128)(2,1)} %copy-done.7, bf16[128,2048]{1,0:T(8,128)(2,1)} %copy-done.6, bf16[128,2048]{1,0:T(8,128)(2,1)} %copy-done.8, ...), custom_call_target="tpu_custom_call" | custom-call | tf_op jit(solution)/shard_map/pallas_call | solution.py:65
  57.8 6.0 %collective-permute-done.11.refs_3_ = bf16[64,2048]{1,0:T(8,128)(2,1)S(1)} collective-permute-done((bf16[64,2048]{1,0:T(8,128)(2,1)S(1)}, bf16[64,2048]{1,0:T(8,128)(2,1)S(1)}, u32[]{:S(2)}, u32[]{:S(2)}) %collective-permute-start.11) | collective-permute-done | bytes 262176 | tf_op jit(solution)/shard_map/ppermute | solution.py:357
  68.0 13.6 %shard_map.90 = (bf16[16,64,512]{2,1,0:T(8,128)(2,1)}, bf16[128,1024]{1,0:T(8,128)(2,1)}, bf16[384,1024]{1,0:T(8,128)(2,1)}, bf16[128,1024]{1,0:T(8,128)(2,1)}, ...) custom-call(bf16[128,2048]{1,0:T(8,128)(2,1)} %shard_map.85.refs_0_, ...), custom_call_target="tpu_custom_call" | custom-call | flops 17179869184 | bytes 8388608 | tf_op jit(solution)/shard_map/pallas_call | solution.py:168
  81.7 4.3 %all-to-all-start = ((bf16[16,64,512]{2,1,0:T(8,128)(2,1)}), bf16[16,64,512]{2,1,0:T(8,128)(2,1)S(1)}, u32[]{:S(2)}, u32[]{:S(2)}) async-start(bf16[16,64,512]{2,1,0:T(8,128)(2,1)} %get-tuple-element.44), calls=%async_computation | async-start | bytes 2097152 | tf_op jit(solution)/shard_map/all_to_all | solution.py:387
  86.8 2.4 %collective-permute-done.19 = bf16[128,1024]{1,0:T(8,128)(2,1)S(1)} collective-permute-done((bf16[128,1024]{1,0:T(8,128)(2,1)}, bf16[128,1024]{1,0:T(8,128)(2,1)S(1)}, u32[]{:S(2)}, u32[]{:S(2)}) %collective-permute-start.19) | collective-permute-done | bytes 262176 | tf_op jit(solution)/shard_map/ppermute | solution.py:361
  90.3 3.8 %collective-permute-start.20 = (bf16[128,1024]{1,0:T(8,128)(2,1)S(1)}, bf16[128,1024]{1,0:T(8,128)(2,1)S(1)}, u32[]{:S(2)}, u32[]{:S(2)}) collective-permute-start(bf16[128,1024]{1,0:T(8,128)(2,1)S(1)} %add_convert_fusion.1), channel_id=1, source_target_pairs={{0,4},{1,5},{2,6},{3,7},{4,0},{5,1},{6,2},{7,3},{8,12},{9,13},{10,... | collective-permute-start | bytes 786440 | tf_op jit(solution)/shard_map/ppermute | solution.py:357
  94.1 6.9 %all-to-all-done.sent = bf16[16,64,512]{2,1,0:T(8,128)(2,1)S(1)} async-done(((bf16[16,64,512]{2,1,0:T(8,128)(2,1)}), bf16[16,64,512]{2,1,0:T(8,128)(2,1)S(1)}, u32[]{:S(2)}, u32[]{:S(2)}) %all-to-all-start) | async-done | bytes 1048608 | tf_op jit(solution)/shard_map/all_to_all | solution.py:387
  101.7 4.4 %collective-permute-start.23 = (bf16[64,128]{1,0:T(8,128)(2,1)S(1)}, bf16[64,128]{1,0:T(8,128)(2,1)S(1)}, u32[]{:S(2)}, u32[]{:S(2)}) collective-permute-start(bf16[64,128]{1,0:T(8,128)(2,1)S(1)} %get-tuple-element.47), channel_id=1, source_target_pairs={{0,0},{1,32},{2,64},{3,96},{4,128},{5,160},{6,192},{7,224},{8,8},{... | collective-permute-start | bytes 49160 | tf_op jit(solution)/shard_map/ppermute | solution.py:371
  106.5 3.7 %collective-permute-start.21 = (bf16[128,1024]{1,0:T(8,128)(2,1)S(1)}, bf16[128,1024]{1,0:T(8,128)(2,1)S(1)}, u32[]{:S(2)}, u32[]{:S(2)}) collective-permute-start(bf16[128,1024]{1,0:T(8,128)(2,1)S(1)} %get-tuple-element.51), channel_id=1, source_target_pairs={{0,2},{1,3},{2,4},{3,5},{4,6},{5,7},{6,0},{7,1},{8,10},{9,11},{10,... | collective-permute-start | bytes 786440 | tf_op jit(solution)/shard_map/ppermute | solution.py:357
  111.2 2.4 %collective-permute-start.22 = (bf16[32,384]{1,0:T(8,128)(2,1)S(1)}, bf16[32,384]{1,0:T(8,128)(2,1)S(1)}, u32[]{:S(2)}, u32[]{:S(2)}) collective-permute-start(bf16[32,384]{1,0:T(8,128)(2,1)S(1)} %get-tuple-element.46), channel_id=1, source_target_pairs={{0,128},{8,136},{16,144},{24,152},{32,160},{40,168},{48,176},{56,1... | collective-permute-start | bytes 73736 | tf_op jit(solution)/shard_map/ppermute | solution.py:365
  113.7 10.5 %collective-permute-done.22 = bf16[32,384]{1,0:T(8,128)(2,1)S(1)} collective-permute-done((bf16[32,384]{1,0:T(8,128)(2,1)S(1)}, bf16[32,384]{1,0:T(8,128)(2,1)S(1)}, u32[]{:S(2)}, u32[]{:S(2)}) %collective-permute-start.22) | collective-permute-done | bytes 24608 | tf_op jit(solution)/shard_map/ppermute | solution.py:365
  125.3 5.2 %collective-permute-start.25 = (bf16[32,640]{1,0:T(8,128)(2,1)S(1)}, bf16[32,640]{1,0:T(8,128)(2,1)S(1)}, u32[]{:S(2)}, u32[]{:S(2)}) collective-permute-start(bf16[32,640]{1,0:T(8,128)(2,1)S(1)} %pad_maximum_fusion.refs_0_), channel_id=1, source_target_pairs={{0,4},{1,5},{2,6},{3,7},{4,0},{5,1},{6,2},{7,3},{8,12},{9,13},{10,... | collective-permute-start | bytes 122888 | tf_op jit(solution)/shard_map/ppermute | solution.py:357
  132.2 3.5 %collective-permute-start.30 = (bf16[32,640]{1,0:T(8,128)(2,1)S(1)}, bf16[32,640]{1,0:T(8,128)(2,1)S(1)}, u32[]{:S(2)}, u32[]{:S(2)}) collective-permute-start(bf16[32,640]{1,0:T(8,128)(2,1)S(1)} %collective-permute-done.26.refs_3_), channel_id=1, source_target_pairs={{0,1},{1,0},{2,3},{3,2},{4,5},{5,4},{6,7},{7,6},{8,9},{9,8},{10,11... | collective-permute-start | bytes 122888 | tf_op jit(solution)/shard_map/ppermute | solution.py:361
  135.8 2.0 %collective-permute-start.29 = (bf16[32,640]{1,0:T(8,128)(2,1)S(1)}, bf16[32,640]{1,0:T(8,128)(2,1)S(1)}, u32[]{:S(2)}, u32[]{:S(2)}) collective-permute-start(bf16[32,640]{1,0:T(8,128)(2,1)S(1)} %collective-permute-done.25.refs_2_), channel_id=1, source_target_pairs={{0,1},{1,0},{2,3},{3,2},{4,5},{5,4},{6,7},{7,6},{8,9},{9,8},{10,11... | collective-permute-start | bytes 122888 | tf_op jit(solution)/shard_map/ppermute | solution.py:361
  (100 shorter events, 26.7 us)
Async XLA Ops:
  2.1 15.6 %collective-permute-start.1 = (bf16[64,128]{1,0:T(8,128)(2,1)}, bf16[64,128]{1,0:T(8,128)(2,1)S(1)}, u32[]{:S(2)}, u32[]{:S(2)}) collective-permute-start(bf16[64,128]{1,0:T(8,128)(2,1)} %get-tuple-element.28), channel_id=1, source_target_pairs={{0,0},{1,32},{2,64},{3,96},{4,128},{5,160},{6,192},{7,224},{8,8},{... | collective-permute-start | bytes 49160 | tf_op jit(solution)/shard_map/ppermute | solution.py:371
  6.6 11.1 %collective-permute-start = (bf16[32,384]{1,0:T(8,128)(2,1)}, bf16[32,384]{1,0:T(8,128)(2,1)S(1)}, u32[]{:S(2)}, u32[]{:S(2)}) collective-permute-start(bf16[32,384]{1,0:T(8,128)(2,1)} %get-tuple-element.27.w_part), channel_id=1, source_target_pairs={{0,128},{8,136},{16,144},{24,152},{32,160},{40,168},{48,176},{56,1... | collective-permute-start | bytes 73736 | tf_op jit(solution)/shard_map/ppermute | solution.py:365
  17.7 30.2 %collective-permute-start.6 = (bf16[128,2048]{1,0:T(8,128)(2,1)}, bf16[128,2048]{1,0:T(8,128)(2,1)S(1)}, u32[]{:S(2)}, u32[]{:S(2)}) collective-permute-start(bf16[128,2048]{1,0:T(8,128)(2,1)} %shard_map.85.refs_0_), channel_id=1, source_target_pairs={{0,6},{1,7},{2,0},{3,1},{4,2},{5,3},{6,4},{7,5},{8,14},{9,15},{10,... | collective-permute-start | bytes 1572872 | tf_op jit(solution)/shard_map/ppermute | solution.py:357
  19.7 28.2 %collective-permute-start.5 = (bf16[128,2048]{1,0:T(8,128)(2,1)}, bf16[128,2048]{1,0:T(8,128)(2,1)S(1)}, u32[]{:S(2)}, u32[]{:S(2)}) collective-permute-start(bf16[128,2048]{1,0:T(8,128)(2,1)} %shard_map.85.refs_0_), channel_id=1, source_target_pairs={{0,2},{1,3},{2,4},{3,5},{4,6},{5,7},{6,0},{7,1},{8,10},{9,11},{10,... | collective-permute-start | bytes 1572872 | tf_op jit(solution)/shard_map/ppermute | solution.py:357
  24.3 4.9 %collective-permute-start.3 = (bf16[64,512]{1,0:T(8,128)(2,1)S(1)}, bf16[64,512]{1,0:T(8,128)(2,1)S(1)}, u32[]{:S(2)}, u32[]{:S(2)}) collective-permute-start(bf16[64,512]{1,0:T(8,128)(2,1)S(1)} %shard_map.87.refs_0_), channel_id=1, source_target_pairs={{0,16},{8,24},{16,0},{24,8},{32,48},{40,56},{48,32},{56,40},{64,80... | collective-permute-start | bytes 196616 | tf_op jit(solution)/shard_map/ppermute | solution.py:382
  24.6 5.3 %collective-permute-start.2 = (bf16[64,512]{1,0:T(8,128)(2,1)S(1)}, bf16[64,512]{1,0:T(8,128)(2,1)S(1)}, u32[]{:S(2)}, u32[]{:S(2)}) collective-permute-start(bf16[64,512]{1,0:T(8,128)(2,1)S(1)} %shard_map.87.refs_0_), channel_id=1, source_target_pairs={{0,8},{8,16},{16,24},{24,0},{32,40},{40,48},{48,56},{56,32},{64,72... | collective-permute-start | bytes 196616 | tf_op jit(solution)/shard_map/ppermute | solution.py:382
  30.5 9.8 %collective-permute-start.9 = (bf16[4,64,512]{2,1,0:T(8,128)(2,1)S(1)}, bf16[4,64,512]{2,1,0:T(8,128)(2,1)S(1)}, u32[]{:S(2)}, u32[]{:S(2)}) collective-permute-start(bf16[4,64,512]{2,1,0:T(8,128)(2,1)S(1)} %shard_map.88.refs_6_), channel_id=1, source_target_pairs={{0,96},{8,104},{16,112},{24,120},{32,0},{40,8},{48,16},{56,24},{64... | collective-permute-start | bytes 786440 | tf_op jit(solution)/shard_map/ppermute | solution.py:382
  33.2 12.1 %collective-permute-start.8 = (bf16[4,64,512]{2,1,0:T(8,128)(2,1)S(1)}, bf16[4,64,512]{2,1,0:T(8,128)(2,1)S(1)}, u32[]{:S(2)}, u32[]{:S(2)}) collective-permute-start(bf16[4,64,512]{2,1,0:T(8,128)(2,1)S(1)} %shard_map.88.refs_6_), channel_id=1, source_target_pairs={{0,64},{8,72},{16,80},{24,88},{32,96},{40,104},{48,112},{56,120},{... | collective-permute-start | bytes 786440 | tf_op jit(solution)/shard_map/ppermute | solution.py:382
  33.2 14.7 %collective-permute-start.7 = (bf16[4,64,512]{2,1,0:T(8,128)(2,1)S(1)}, bf16[4,64,512]{2,1,0:T(8,128)(2,1)S(1)}, u32[]{:S(2)}, u32[]{:S(2)}) collective-permute-start(bf16[4,64,512]{2,1,0:T(8,128)(2,1)S(1)} %shard_map.88.refs_6_), channel_id=1, source_target_pairs={{0,32},{8,40},{16,48},{24,56},{32,64},{40,72},{48,80},{56,88},{64,... | collective-permute-start | bytes 786440 | tf_op jit(solution)/shard_map/ppermute | solution.py:382
  40.2 11.3 %collective-permute-start.12 = (bf16[128,2048]{1,0:T(8,128)(2,1)}, bf16[128,2048]{1,0:T(8,128)(2,1)S(1)}, u32[]{:S(2)}, u32[]{:S(2)}) collective-permute-start(bf16[128,2048]{1,0:T(8,128)(2,1)} %shard_map.85.refs_0_), channel_id=1, source_target_pairs={{0,1},{1,0},{2,3},{3,2},{4,5},{5,4},{6,7},{7,6},{8,9},{9,8},{10,11... | collective-permute-start | bytes 1572872 | tf_op jit(solution)/shard_map/ppermute | solution.py:361
  49.0 14.8 %collective-permute-start.11 = (bf16[64,2048]{1,0:T(8,128)(2,1)S(1)}, bf16[64,2048]{1,0:T(8,128)(2,1)S(1)}, u32[]{:S(2)}, u32[]{:S(2)}) collective-permute-start(bf16[64,2048]{1,0:T(8,128)(2,1)S(1)} %slice.22), channel_id=1, source_target_pairs={{0,6},{1,7},{2,0},{3,1},{4,2},{5,3},{6,4},{7,5},{8,14},{9,15},{10,... | collective-permute-start | bytes 786440 | tf_op jit(solution)/shard_map/ppermute | solution.py:357
  50.5 13.7 %collective-permute-start.10 = (bf16[64,2048]{1,0:T(8,128)(2,1)S(1)}, bf16[64,2048]{1,0:T(8,128)(2,1)S(1)}, u32[]{:S(2)}, u32[]{:S(2)}) collective-permute-start(bf16[64,2048]{1,0:T(8,128)(2,1)S(1)} %slice.21), channel_id=1, source_target_pairs={{0,2},{1,3},{2,4},{3,5},{4,6},{5,7},{6,0},{7,1},{8,10},{9,11},{10,... | collective-permute-start | bytes 786440 | tf_op jit(solution)/shard_map/ppermute | solution.py:357
  81.7 19.3 %all-to-all-start = ((bf16[16,64,512]{2,1,0:T(8,128)(2,1)}), bf16[16,64,512]{2,1,0:T(8,128)(2,1)S(1)}, u32[]{:S(2)}, u32[]{:S(2)}) async-start(bf16[16,64,512]{2,1,0:T(8,128)(2,1)} %get-tuple-element.44), calls=%async_computation | async-start | bytes 2097152 | tf_op jit(solution)/shard_map/all_to_all | solution.py:387
  86.0 20.1 %collective-permute-start.17 = (bf16[384,1024]{1,0:T(8,128)(2,1)}, bf16[384,1024]{1,0:T(8,128)(2,1)S(1)}, u32[]{:S(2)}, u32[]{:S(2)}) collective-permute-start(bf16[384,1024]{1,0:T(8,128)(2,1)} %get-tuple-element.39), channel_id=1, source_target_pairs={{0,1},{1,0},{2,3},{3,2},{4,5},{5,4},{6,7},{7,6},{8,9},{9,8},{10,11... | collective-permute-start | bytes 2359304 | tf_op jit(solution)/shard_map/ppermute | solution.py:361
  90.3 33.9 %collective-permute-start.20 = (bf16[128,1024]{1,0:T(8,128)(2,1)S(1)}, bf16[128,1024]{1,0:T(8,128)(2,1)S(1)}, u32[]{:S(2)}, u32[]{:S(2)}) collective-permute-start(bf16[128,1024]{1,0:T(8,128)(2,1)S(1)} %add_convert_fusion.1), channel_id=1, source_target_pairs={{0,4},{1,5},{2,6},{3,7},{4,0},{5,1},{6,2},{7,3},{8,12},{9,13},{10,... | collective-permute-start | bytes 786440 | tf_op jit(solution)/shard_map/ppermute | solution.py:357
  101.7 12.0 %collective-permute-start.23 = (bf16[64,128]{1,0:T(8,128)(2,1)S(1)}, bf16[64,128]{1,0:T(8,128)(2,1)S(1)}, u32[]{:S(2)}, u32[]{:S(2)}) collective-permute-start(bf16[64,128]{1,0:T(8,128)(2,1)S(1)} %get-tuple-element.47), channel_id=1, source_target_pairs={{0,0},{1,32},{2,64},{3,96},{4,128},{5,160},{6,192},{7,224},{8,8},{... | collective-permute-start | bytes 49160 | tf_op jit(solution)/shard_map/ppermute | solution.py:371
  106.5 31.3 %collective-permute-start.21 = (bf16[128,1024]{1,0:T(8,128)(2,1)S(1)}, bf16[128,1024]{1,0:T(8,128)(2,1)S(1)}, u32[]{:S(2)}, u32[]{:S(2)}) collective-permute-start(bf16[128,1024]{1,0:T(8,128)(2,1)S(1)} %get-tuple-element.51), channel_id=1, source_target_pairs={{0,2},{1,3},{2,4},{3,5},{4,6},{5,7},{6,0},{7,1},{8,10},{9,11},{10,... | collective-permute-start | bytes 786440 | tf_op jit(solution)/shard_map/ppermute | solution.py:357
  110.2 27.6 %collective-permute-start.18 = (bf16[128,1024]{1,0:T(8,128)(2,1)S(1)}, bf16[128,1024]{1,0:T(8,128)(2,1)S(1)}, u32[]{:S(2)}, u32[]{:S(2)}) collective-permute-start(bf16[128,1024]{1,0:T(8,128)(2,1)S(1)} %get-tuple-element.52), channel_id=1, source_target_pairs={{0,6},{1,7},{2,0},{3,1},{4,2},{5,3},{6,4},{7,5},{8,14},{9,15},{10,... | collective-permute-start | bytes 786440 | tf_op jit(solution)/shard_map/ppermute | solution.py:357
  111.2 12.9 %collective-permute-start.22 = (bf16[32,384]{1,0:T(8,128)(2,1)S(1)}, bf16[32,384]{1,0:T(8,128)(2,1)S(1)}, u32[]{:S(2)}, u32[]{:S(2)}) collective-permute-start(bf16[32,384]{1,0:T(8,128)(2,1)S(1)} %get-tuple-element.46), channel_id=1, source_target_pairs={{0,128},{8,136},{16,144},{24,152},{32,160},{40,168},{48,176},{56,1... | collective-permute-start | bytes 73736 | tf_op jit(solution)/shard_map/ppermute | solution.py:365
  124.2 6.3 %collective-permute-start.26 = (bf16[32,640]{1,0:T(8,128)(2,1)S(1)}, bf16[32,640]{1,0:T(8,128)(2,1)S(1)}, u32[]{:S(2)}, u32[]{:S(2)}) collective-permute-start(bf16[32,640]{1,0:T(8,128)(2,1)S(1)} %pad_maximum_fusion.refs_0_), channel_id=1, source_target_pairs={{0,6},{1,7},{2,0},{3,1},{4,2},{5,3},{6,4},{7,5},{8,14},{9,15},{10,... | collective-permute-start | bytes 122888 | tf_op jit(solution)/shard_map/ppermute | solution.py:357
  125.3 6.9 %collective-permute-start.25 = (bf16[32,640]{1,0:T(8,128)(2,1)S(1)}, bf16[32,640]{1,0:T(8,128)(2,1)S(1)}, u32[]{:S(2)}, u32[]{:S(2)}) collective-permute-start(bf16[32,640]{1,0:T(8,128)(2,1)S(1)} %pad_maximum_fusion.refs_0_), channel_id=1, source_target_pairs={{0,4},{1,5},{2,6},{3,7},{4,0},{5,1},{6,2},{7,3},{8,12},{9,13},{10,... | collective-permute-start | bytes 122888 | tf_op jit(solution)/shard_map/ppermute | solution.py:357
  130.5 5.3 %collective-permute-start.24 = (bf16[32,640]{1,0:T(8,128)(2,1)S(1)}, bf16[32,640]{1,0:T(8,128)(2,1)S(1)}, u32[]{:S(2)}, u32[]{:S(2)}) collective-permute-start(bf16[32,640]{1,0:T(8,128)(2,1)S(1)} %pad_maximum_fusion.refs_0_), channel_id=1, source_target_pairs={{0,2},{1,3},{2,4},{3,5},{4,6},{5,7},{6,0},{7,1},{8,10},{9,11},{10,... | collective-permute-start | bytes 122888 | tf_op jit(solution)/shard_map/ppermute | solution.py:357
  130.5 8.5 %collective-permute-start.27 = (bf16[32,640]{1,0:T(8,128)(2,1)S(1)}, bf16[32,640]{1,0:T(8,128)(2,1)S(1)}, u32[]{:S(2)}, u32[]{:S(2)}) collective-permute-start(bf16[32,640]{1,0:T(8,128)(2,1)S(1)} %pad_maximum_fusion.refs_0_), channel_id=1, source_target_pairs={{0,1},{1,0},{2,3},{3,2},{4,5},{5,4},{6,7},{7,6},{8,9},{9,8},{10,11... | collective-permute-start | bytes 122888 | tf_op jit(solution)/shard_map/ppermute | solution.py:361
  132.2 6.8 %collective-permute-start.30 = (bf16[32,640]{1,0:T(8,128)(2,1)S(1)}, bf16[32,640]{1,0:T(8,128)(2,1)S(1)}, u32[]{:S(2)}, u32[]{:S(2)}) collective-permute-start(bf16[32,640]{1,0:T(8,128)(2,1)S(1)} %collective-permute-done.26.refs_3_), channel_id=1, source_target_pairs={{0,1},{1,0},{2,3},{3,2},{4,5},{5,4},{6,7},{7,6},{8,9},{9,8},{10,11... | collective-permute-start | bytes 122888 | tf_op jit(solution)/shard_map/ppermute | solution.py:361
  (29 other events, 331.7 us)

commit v5 on v4

--- a/solution.py
+++ b/solution.py
@@ -426,16 +426,16 @@
     own, one, three = (
         add(piece, near[i * CELLS : (i + 1) * CELLS]) for i, piece in enumerate((own, one, three))
     )
-    one, three = turn(one, 3), turn(three, 1)
-    branch = finish(image, row, (own, one, two, three))
 
     near, far, go = add_up(where, grads)
     go = transpose_devices(go)
     gq = (near + swap_lo(far).astype(F32)).astype(BF16)
     mine = jnp.concatenate([gq, go[:ROWS], go[ROWS:]], 1)
     mine = after(mine, two)
+    one, three = turn(after(one, mine), 3), turn(after(three, mine), 1)
     every = [mine] + [turn(mine, by) for by in range(1, Z)]
     grad_q, grad_o = place(every + [swap(piece) for piece in every], where)
+    branch = finish(image, row, (own, one, two, three))
     return branch[None], grad_q, grad_o
 
 

time: 141 us -> 139 us (0.986)
  waiting for transfers between devices: 41.5 us -> 35.5 us
  starting transfers between devices: 65.3 us -> 68.9 us
    ppermute x2, waiting for transfers between devices: 10.5 us -> 1.21 us  [swap_lo(): return lax.ppermute(x, 'dp', [(i, i ^ XY) for i in range(2 * XY)])]
    ppermute x11, starting transfers between devices: 15.6 us -> 20.6 us  [swap(): return lax.ppermute(x, 'space', [(i, i ^ 1) for i in range(2 * Z)])]
    ppermute x10, starting transfers between devices: 19.7 us -> 17.2 us  [turn(): return lax.ppermute(x, 'space', pairs)]
    ppermute x10, waiting for transfers between devices: 6.73 us -> 9.11 us  [turn(): return lax.ppermute(x, 'space', pairs)]
  transfers between devices with their start and end apart: 32 -> 32, of which waited for: 13 -> 16; matrix products, arithmetic and copies ran while one was open for 2% -> 2% of each run, Pallas kernels for 7% -> 7%
where the time goes in v5:
time: 139 us; the launch traced here: 138 us
  starting transfers between devices  68.9 us (50%)
  waiting for transfers between devices  35.5 us (26%)
  Pallas kernels  26 us (19%)
  local copies, waits for them, and re-layouts  4.61 us (3%)
  between operations  1.6 us (1%)
  other arithmetic  1.41 us (1%)
    ppermute x11, starting transfers between devices, swap(): return lax.ppermute(x, 'space', [(i, i ^ 1) for i in range(2 * Z)])  20.6 us
    ppermute x10, starting transfers between devices, turn(): return lax.ppermute(x, 'space', pairs)  17.2 us
    pallas_call x1, Pallas kernels, attention(): pl.pallas_call(attention_kernel, in_specs=[FAR] * (PIECES + 3), out_specs...  13.6 us
    ppermute x6, waiting for transfers between devices, turn_dp(): return lax.ppermute(x, 'dp', pairs)  13.5 us
    ppermute x2, starting transfers between devices, swap_lo(): return lax.ppermute(x, 'dp', [(i, i ^ XY) for i in range(2 * XY)])  10.6 us
    ppermute x10, waiting for transfers between devices, turn(): return lax.ppermute(x, 'space', pairs)  9.11 us
    ppermute x2, starting transfers between devices, transpose_devices(): return lax.ppermute(x, ('dp', 'space'), pairs)  8.93 us
    ppermute x6, starting transfers between devices, turn_dp(): return lax.ppermute(x, 'dp', pairs)  7.29 us
  transfers between devices with their start and end apart: 32, of which 16 were waited for; matrix products, arithmetic and copies ran while one was open for 2% of the time, Pallas kernels for 7%

profile of v5, /device:TPU:1, one launch (start us, length us, event | category | flops | bytes accessed | tf_op | source)
XLA Modules:
  0.0 138.1 jit_solution(8403717719700962254)
XLA Ops:
  2.1 4.5 %collective-permute-start.1 = (bf16[64,128]{1,0:T(8,128)(2,1)}, bf16[64,128]{1,0:T(8,128)(2,1)S(1)}, u32[]{:S(2)}, u32[]{:S(2)}) collective-permute-start(bf16[64,128]{1,0:T(8,128)(2,1)} %get-tuple-element.30), channel_id=1, source_target_pairs={{0,0},{1,32},{2,64},{3,96},{4,128},{5,160},{6,192},{7,224},{8,8},{... | collective-permute-start | bytes 49160 | tf_op jit(solution)/shard_map/ppermute | solution.py:371
  6.6 7.0 %collective-permute-start = (bf16[32,384]{1,0:T(8,128)(2,1)}, bf16[32,384]{1,0:T(8,128)(2,1)S(1)}, u32[]{:S(2)}, u32[]{:S(2)}) collective-permute-start(bf16[32,384]{1,0:T(8,128)(2,1)} %get-tuple-element.29.w_part), channel_id=1, source_target_pairs={{0,128},{8,136},{16,144},{24,152},{32,160},{40,168},{48,176},{56,1... | collective-permute-start | bytes 73736 | tf_op jit(solution)/shard_map/ppermute | solution.py:365
  15.6 2.1 %shard_map.85.refs_0_ = bf16[128,2048]{1,0:T(8,128)(2,1)} custom-call(bf16[128,1024]{1,0:T(8,128)(2,1)} %bitcast.11, bf16[128,1024]{1,0:T(8,128)(2,1)} %bitcast.13, bf16[1,2048]{1,0:T(2,128)(2,1)} %constant_dynamic-slice_fusion.row), custom_call_target="tpu_custom_call" | custom-call | tf_op jit(solution)/shard_map/pallas_call | solution.py:211
  21.4 2.8 %collective-permute-start.4 = (bf16[64,512]{1,0:T(8,128)(2,1)S(1)}, bf16[64,512]{1,0:T(8,128)(2,1)S(1)}, u32[]{:S(2)}, u32[]{:S(2)}) collective-permute-start(bf16[64,512]{1,0:T(8,128)(2,1)S(1)} %shard_map.87.refs_0_), channel_id=1, source_target_pairs={{0,24},{8,0},{16,8},{24,16},{32,56},{40,32},{48,40},{56,48},{64,88... | collective-permute-start | bytes 196616 | tf_op jit(solution)/shard_map/ppermute | solution.py:382
  25.6 3.6 %collective-permute-done.3.refs_2_ = bf16[64,512]{1,0:T(8,128)(2,1)S(1)} collective-permute-done((bf16[64,512]{1,0:T(8,128)(2,1)S(1)}, bf16[64,512]{1,0:T(8,128)(2,1)S(1)}, u32[]{:S(2)}, u32[]{:S(2)}) %collective-permute-start.3) | collective-permute-done | bytes 65568 | tf_op jit(solution)/shard_map/ppermute | solution.py:382
  30.5 2.8 %collective-permute-start.9 = (bf16[4,64,512]{2,1,0:T(8,128)(2,1)S(1)}, bf16[4,64,512]{2,1,0:T(8,128)(2,1)S(1)}, u32[]{:S(2)}, u32[]{:S(2)}) collective-permute-start(bf16[4,64,512]{2,1,0:T(8,128)(2,1)S(1)} %shard_map.88.refs_6_), channel_id=1, source_target_pairs={{0,96},{8,104},{16,112},{24,120},{32,0},{40,8},{48,16},{56,24},{64... | collective-permute-start | bytes 786440 | tf_op jit(solution)/shard_map/ppermute | solution.py:382
  33.9 6.3 %collective-permute-done.9.refs_9_ = bf16[4,64,512]{2,1,0:T(8,128)(2,1)S(1)} collective-permute-done((bf16[4,64,512]{2,1,0:T(8,128)(2,1)S(1)}, bf16[4,64,512]{2,1,0:T(8,128)(2,1)S(1)}, u32[]{:S(2)}, u32[]{:S(2)}) %collective-permute-start.9) | collective-permute-done | bytes 262176 | tf_op jit(solution)/shard_map/ppermute | solution.py:382
  40.2 5.1 %collective-permute-start.12 = (bf16[128,2048]{1,0:T(8,128)(2,1)}, bf16[128,2048]{1,0:T(8,128)(2,1)S(1)}, u32[]{:S(2)}, u32[]{:S(2)}) collective-permute-start(bf16[128,2048]{1,0:T(8,128)(2,1)} %shard_map.85.refs_0_), channel_id=1, source_target_pairs={{0,1},{1,0},{2,3},{3,2},{4,5},{5,4},{6,7},{7,6},{8,9},{9,8},{10,11... | collective-permute-start | bytes 1572872 | tf_op jit(solution)/shard_map/ppermute | solution.py:361
  45.4 2.6 %collective-permute-done.7.refs_7_ = bf16[4,64,512]{2,1,0:T(8,128)(2,1)S(1)} collective-permute-done((bf16[4,64,512]{2,1,0:T(8,128)(2,1)S(1)}, bf16[4,64,512]{2,1,0:T(8,128)(2,1)S(1)}, u32[]{:S(2)}, u32[]{:S(2)}) %collective-permute-start.7) | collective-permute-done | bytes 262176 | tf_op jit(solution)/shard_map/ppermute | solution.py:382
  53.3 4.5 %shard_map.89 = (bf16[768,512]{1,0:T(8,128)(2,1)}, bf16[1024,384]{1,0:T(8,128)(2,1)}, bf16[128,1024]{1,0:T(8,128)(2,1)}) custom-call(s32[4]{0:T(128)} %copy-done.4, bf16[128,2048]{1,0:T(8,128)(2,1)} %shard_map.85.refs_0_, bf16[128,2048]{1,0:T(8,128)(2,1)} %copy-done.7, bf16[128,2048]{1,0:T(8,128)(2,1)} %copy-done.6, bf16[128,2048]{1,0:T(8,128)(2,1)} %copy-done.8, ...), custom_call_target="tpu_custom_call" | custom-call | tf_op jit(solution)/shard_map/pallas_call | solution.py:65
  57.8 6.0 %collective-permute-done.11.refs_3_ = bf16[64,2048]{1,0:T(8,128)(2,1)S(1)} collective-permute-done((bf16[64,2048]{1,0:T(8,128)(2,1)S(1)}, bf16[64,2048]{1,0:T(8,128)(2,1)S(1)}, u32[]{:S(2)}, u32[]{:S(2)}) %collective-permute-start.11) | collective-permute-done | bytes 262176 | tf_op jit(solution)/shard_map/ppermute | solution.py:357
  68.0 13.6 %shard_map.90 = (bf16[16,64,512]{2,1,0:T(8,128)(2,1)}, bf16[128,1024]{1,0:T(8,128)(2,1)}, bf16[384,1024]{1,0:T(8,128)(2,1)}, bf16[128,1024]{1,0:T(8,128)(2,1)}, ...) custom-call(bf16[128,2048]{1,0:T(8,128)(2,1)} %shard_map.85.refs_0_, ...), custom_call_target="tpu_custom_call" | custom-call | flops 17179869184 | bytes 8388608 | tf_op jit(solution)/shard_map/pallas_call | solution.py:168
  81.7 4.3 %all-to-all-start = ((bf16[16,64,512]{2,1,0:T(8,128)(2,1)}), bf16[16,64,512]{2,1,0:T(8,128)(2,1)S(1)}, u32[]{:S(2)}, u32[]{:S(2)}) async-start(bf16[16,64,512]{2,1,0:T(8,128)(2,1)} %get-tuple-element.43), calls=%async_computation | async-start | bytes 2097152 | tf_op jit(solution)/shard_map/all_to_all | solution.py:387
  86.8 2.4 %collective-permute-done.20 = bf16[128,1024]{1,0:T(8,128)(2,1)S(1)} collective-permute-done((bf16[128,1024]{1,0:T(8,128)(2,1)}, bf16[128,1024]{1,0:T(8,128)(2,1)S(1)}, u32[]{:S(2)}, u32[]{:S(2)}) %collective-permute-start.20) | collective-permute-done | bytes 262176 | tf_op jit(solution)/shard_map/ppermute | solution.py:361
  90.3 3.8 %collective-permute-start.21 = (bf16[128,1024]{1,0:T(8,128)(2,1)S(1)}, bf16[128,1024]{1,0:T(8,128)(2,1)S(1)}, u32[]{:S(2)}, u32[]{:S(2)}) collective-permute-start(bf16[128,1024]{1,0:T(8,128)(2,1)S(1)} %add_convert_fusion.1), channel_id=1, source_target_pairs={{0,4},{1,5},{2,6},{3,7},{4,0},{5,1},{6,2},{7,3},{8,12},{9,13},{10,... | collective-permute-start | bytes 786440 | tf_op jit(solution)/shard_map/ppermute | solution.py:357
  94.1 6.9 %all-to-all-done.sent = bf16[16,64,512]{2,1,0:T(8,128)(2,1)S(1)} async-done(((bf16[16,64,512]{2,1,0:T(8,128)(2,1)}), bf16[16,64,512]{2,1,0:T(8,128)(2,1)S(1)}, u32[]{:S(2)}, u32[]{:S(2)}) %all-to-all-start) | async-done | bytes 1048608 | tf_op jit(solution)/shard_map/all_to_all | solution.py:387
  101.7 4.4 %collective-permute-start.19 = (bf16[64,128]{1,0:T(8,128)(2,1)S(1)}, bf16[64,128]{1,0:T(8,128)(2,1)S(1)}, u32[]{:S(2)}, u32[]{:S(2)}) collective-permute-start(bf16[64,128]{1,0:T(8,128)(2,1)S(1)} %get-tuple-element.46), channel_id=1, source_target_pairs={{0,0},{1,32},{2,64},{3,96},{4,128},{5,160},{6,192},{7,224},{8,8},{... | collective-permute-start | bytes 49160 | tf_op jit(solution)/shard_map/ppermute | solution.py:371
  106.5 3.6 %collective-permute-start.18 = (bf16[32,384]{1,0:T(8,128)(2,1)S(1)}, bf16[32,384]{1,0:T(8,128)(2,1)S(1)}, u32[]{:S(2)}, u32[]{:S(2)}) collective-permute-start(bf16[32,384]{1,0:T(8,128)(2,1)S(1)} %get-tuple-element.45), channel_id=1, source_target_pairs={{0,128},{8,136},{16,144},{24,152},{32,160},{40,168},{48,176},{56,1... | collective-permute-start | bytes 73736 | tf_op jit(solution)/shard_map/ppermute | solution.py:365
  111.3 2.6 %collective-permute-start.22 = (bf16[128,1024]{1,0:T(8,128)(2,1)S(1)}, bf16[128,1024]{1,0:T(8,128)(2,1)S(1)}, u32[]{:S(2)}, u32[]{:S(2)}) collective-permute-start(bf16[128,1024]{1,0:T(8,128)(2,1)S(1)} %get-tuple-element.50), channel_id=1, source_target_pairs={{0,6},{1,7},{2,0},{3,1},{4,2},{5,3},{6,4},{7,5},{8,14},{9,15},{10,... | collective-permute-start | bytes 786440 | tf_op jit(solution)/shard_map/ppermute | solution.py:357
  113.9 4.2 %collective-permute-start.27 = (bf16[32,640]{1,0:T(8,128)(2,1)S(1)}, bf16[32,640]{1,0:T(8,128)(2,1)S(1)}, u32[]{:S(2)}, u32[]{:S(2)}) collective-permute-start(bf16[32,640]{1,0:T(8,128)(2,1)S(1)} %pad_maximum_fusion.refs_0_), channel_id=1, source_target_pairs={{0,1},{1,0},{2,3},{3,2},{4,5},{5,4},{6,7},{7,6},{8,9},{9,8},{10,11... | collective-permute-start | bytes 122888 | tf_op jit(solution)/shard_map/ppermute | solution.py:361
  118.2 3.9 %collective-permute-start.26 = (bf16[32,640]{1,0:T(8,128)(2,1)S(1)}, bf16[32,640]{1,0:T(8,128)(2,1)S(1)}, u32[]{:S(2)}, u32[]{:S(2)}) collective-permute-start(bf16[32,640]{1,0:T(8,128)(2,1)S(1)} %pad_maximum_fusion.refs_0_), channel_id=1, source_target_pairs={{0,6},{1,7},{2,0},{3,1},{4,2},{5,3},{6,4},{7,5},{8,14},{9,15},{10,... | collective-permute-start | bytes 122888 | tf_op jit(solution)/shard_map/ppermute | solution.py:357
  124.4 4.9 %collective-permute-start.30 = (bf16[32,640]{1,0:T(8,128)(2,1)S(1)}, bf16[32,640]{1,0:T(8,128)(2,1)S(1)}, u32[]{:S(2)}, u32[]{:S(2)}) collective-permute-start(bf16[32,640]{1,0:T(8,128)(2,1)S(1)} %collective-permute-done.26.refs_3_), channel_id=1, source_target_pairs={{0,1},{1,0},{2,3},{3,2},{4,5},{5,4},{6,7},{7,6},{8,9},{9,8},{10,11... | collective-permute-start | bytes 122888 | tf_op jit(solution)/shard_map/ppermute | solution.py:361
  129.3 2.1 %collective-permute-done.25.refs_2_ = bf16[32,640]{1,0:T(8,128)(2,1)S(1)} collective-permute-done((bf16[32,640]{1,0:T(8,128)(2,1)S(1)}, bf16[32,640]{1,0:T(8,128)(2,1)S(1)}, u32[]{:S(2)}, u32[]{:S(2)}) %collective-permute-start.25) | collective-permute-done | bytes 40992 | tf_op jit(solution)/shard_map/ppermute | solution.py:357
  132.0 2.5 %collective-permute-start.28 = (bf16[32,640]{1,0:T(8,128)(2,1)S(1)}, bf16[32,640]{1,0:T(8,128)(2,1)S(1)}, u32[]{:S(2)}, u32[]{:S(2)}) collective-permute-start(bf16[32,640]{1,0:T(8,128)(2,1)S(1)} %collective-permute-done.24.refs_1_), channel_id=1, source_target_pairs={{0,1},{1,0},{2,3},{3,2},{4,5},{5,4},{6,7},{7,6},{8,9},{9,8},{10,11... | collective-permute-start | bytes 122888 | tf_op jit(solution)/shard_map/ppermute | solution.py:361
  (100 shorter events, 29.9 us)
Async XLA Ops:
  2.1 15.6 %collective-permute-start.1 = (bf16[64,128]{1,0:T(8,128)(2,1)}, bf16[64,128]{1,0:T(8,128)(2,1)S(1)}, u32[]{:S(2)}, u32[]{:S(2)}) collective-permute-start(bf16[64,128]{1,0:T(8,128)(2,1)} %get-tuple-element.30), channel_id=1, source_target_pairs={{0,0},{1,32},{2,64},{3,96},{4,128},{5,160},{6,192},{7,224},{8,8},{... | collective-permute-start | bytes 49160 | tf_op jit(solution)/shard_map/ppermute | solution.py:371
  6.6 11.1 %collective-permute-start = (bf16[32,384]{1,0:T(8,128)(2,1)}, bf16[32,384]{1,0:T(8,128)(2,1)S(1)}, u32[]{:S(2)}, u32[]{:S(2)}) collective-permute-start(bf16[32,384]{1,0:T(8,128)(2,1)} %get-tuple-element.29.w_part), channel_id=1, source_target_pairs={{0,128},{8,136},{16,144},{24,152},{32,160},{40,168},{48,176},{56,1... | collective-permute-start | bytes 73736 | tf_op jit(solution)/shard_map/ppermute | solution.py:365
  17.7 30.2 %collective-permute-start.6 = (bf16[128,2048]{1,0:T(8,128)(2,1)}, bf16[128,2048]{1,0:T(8,128)(2,1)S(1)}, u32[]{:S(2)}, u32[]{:S(2)}) collective-permute-start(bf16[128,2048]{1,0:T(8,128)(2,1)} %shard_map.85.refs_0_), channel_id=1, source_target_pairs={{0,6},{1,7},{2,0},{3,1},{4,2},{5,3},{6,4},{7,5},{8,14},{9,15},{10,... | collective-permute-start | bytes 1572872 | tf_op jit(solution)/shard_map/ppermute | solution.py:357
  19.7 28.2 %collective-permute-start.5 = (bf16[128,2048]{1,0:T(8,128)(2,1)}, bf16[128,2048]{1,0:T(8,128)(2,1)S(1)}, u32[]{:S(2)}, u32[]{:S(2)}) collective-permute-start(bf16[128,2048]{1,0:T(8,128)(2,1)} %shard_map.85.refs_0_), channel_id=1, source_target_pairs={{0,2},{1,3},{2,4},{3,5},{4,6},{5,7},{6,0},{7,1},{8,10},{9,11},{10,... | collective-permute-start | bytes 1572872 | tf_op jit(solution)/shard_map/ppermute | solution.py:357
  24.3 4.9 %collective-permute-start.3 = (bf16[64,512]{1,0:T(8,128)(2,1)S(1)}, bf16[64,512]{1,0:T(8,128)(2,1)S(1)}, u32[]{:S(2)}, u32[]{:S(2)}) collective-permute-start(bf16[64,512]{1,0:T(8,128)(2,1)S(1)} %shard_map.87.refs_0_), channel_id=1, source_target_pairs={{0,16},{8,24},{16,0},{24,8},{32,48},{40,56},{48,32},{56,40},{64,80... | collective-permute-start | bytes 196616 | tf_op jit(solution)/shard_map/ppermute | solution.py:382
  24.6 5.3 %collective-permute-start.2 = (bf16[64,512]{1,0:T(8,128)(2,1)S(1)}, bf16[64,512]{1,0:T(8,128)(2,1)S(1)}, u32[]{:S(2)}, u32[]{:S(2)}) collective-permute-start(bf16[64,512]{1,0:T(8,128)(2,1)S(1)} %shard_map.87.refs_0_), channel_id=1, source_target_pairs={{0,8},{8,16},{16,24},{24,0},{32,40},{40,48},{48,56},{56,32},{64,72... | collective-permute-start | bytes 196616 | tf_op jit(solution)/shard_map/ppermute | solution.py:382
  30.5 9.8 %collective-permute-start.9 = (bf16[4,64,512]{2,1,0:T(8,128)(2,1)S(1)}, bf16[4,64,512]{2,1,0:T(8,128)(2,1)S(1)}, u32[]{:S(2)}, u32[]{:S(2)}) collective-permute-start(bf16[4,64,512]{2,1,0:T(8,128)(2,1)S(1)} %shard_map.88.refs_6_), channel_id=1, source_target_pairs={{0,96},{8,104},{16,112},{24,120},{32,0},{40,8},{48,16},{56,24},{64... | collective-permute-start | bytes 786440 | tf_op jit(solution)/shard_map/ppermute | solution.py:382
  33.2 12.1 %collective-permute-start.8 = (bf16[4,64,512]{2,1,0:T(8,128)(2,1)S(1)}, bf16[4,64,512]{2,1,0:T(8,128)(2,1)S(1)}, u32[]{:S(2)}, u32[]{:S(2)}) collective-permute-start(bf16[4,64,512]{2,1,0:T(8,128)(2,1)S(1)} %shard_map.88.refs_6_), channel_id=1, source_target_pairs={{0,64},{8,72},{16,80},{24,88},{32,96},{40,104},{48,112},{56,120},{... | collective-permute-start | bytes 786440 | tf_op jit(solution)/shard_map/ppermute | solution.py:382
  33.2 14.7 %collective-permute-start.7 = (bf16[4,64,512]{2,1,0:T(8,128)(2,1)S(1)}, bf16[4,64,512]{2,1,0:T(8,128)(2,1)S(1)}, u32[]{:S(2)}, u32[]{:S(2)}) collective-permute-start(bf16[4,64,512]{2,1,0:T(8,128)(2,1)S(1)} %shard_map.88.refs_6_), channel_id=1, source_target_pairs={{0,32},{8,40},{16,48},{24,56},{32,64},{40,72},{48,80},{56,88},{64,... | collective-permute-start | bytes 786440 | tf_op jit(solution)/shard_map/ppermute | solution.py:382
  40.2 11.3 %collective-permute-start.12 = (bf16[128,2048]{1,0:T(8,128)(2,1)}, bf16[128,2048]{1,0:T(8,128)(2,1)S(1)}, u32[]{:S(2)}, u32[]{:S(2)}) collective-permute-start(bf16[128,2048]{1,0:T(8,128)(2,1)} %shard_map.85.refs_0_), channel_id=1, source_target_pairs={{0,1},{1,0},{2,3},{3,2},{4,5},{5,4},{6,7},{7,6},{8,9},{9,8},{10,11... | collective-permute-start | bytes 1572872 | tf_op jit(solution)/shard_map/ppermute | solution.py:361
  49.0 14.8 %collective-permute-start.11 = (bf16[64,2048]{1,0:T(8,128)(2,1)S(1)}, bf16[64,2048]{1,0:T(8,128)(2,1)S(1)}, u32[]{:S(2)}, u32[]{:S(2)}) collective-permute-start(bf16[64,2048]{1,0:T(8,128)(2,1)S(1)} %slice.22), channel_id=1, source_target_pairs={{0,6},{1,7},{2,0},{3,1},{4,2},{5,3},{6,4},{7,5},{8,14},{9,15},{10,... | collective-permute-start | bytes 786440 | tf_op jit(solution)/shard_map/ppermute | solution.py:357
  50.5 13.7 %collective-permute-start.10 = (bf16[64,2048]{1,0:T(8,128)(2,1)S(1)}, bf16[64,2048]{1,0:T(8,128)(2,1)S(1)}, u32[]{:S(2)}, u32[]{:S(2)}) collective-permute-start(bf16[64,2048]{1,0:T(8,128)(2,1)S(1)} %slice.21), channel_id=1, source_target_pairs={{0,2},{1,3},{2,4},{3,5},{4,6},{5,7},{6,0},{7,1},{8,10},{9,11},{10,... | collective-permute-start | bytes 786440 | tf_op jit(solution)/shard_map/ppermute | solution.py:357
  81.7 19.3 %all-to-all-start = ((bf16[16,64,512]{2,1,0:T(8,128)(2,1)}), bf16[16,64,512]{2,1,0:T(8,128)(2,1)S(1)}, u32[]{:S(2)}, u32[]{:S(2)}) async-start(bf16[16,64,512]{2,1,0:T(8,128)(2,1)} %get-tuple-element.43), calls=%async_computation | async-start | bytes 2097152 | tf_op jit(solution)/shard_map/all_to_all | solution.py:387
  86.0 20.1 %collective-permute-start.17 = (bf16[384,1024]{1,0:T(8,128)(2,1)}, bf16[384,1024]{1,0:T(8,128)(2,1)S(1)}, u32[]{:S(2)}, u32[]{:S(2)}) collective-permute-start(bf16[384,1024]{1,0:T(8,128)(2,1)} %get-tuple-element.41), channel_id=1, source_target_pairs={{0,1},{1,0},{2,3},{3,2},{4,5},{5,4},{6,7},{7,6},{8,9},{9,8},{10,11... | collective-permute-start | bytes 2359304 | tf_op jit(solution)/shard_map/ppermute | solution.py:361
  90.3 21.1 %collective-permute-start.21 = (bf16[128,1024]{1,0:T(8,128)(2,1)S(1)}, bf16[128,1024]{1,0:T(8,128)(2,1)S(1)}, u32[]{:S(2)}, u32[]{:S(2)}) collective-permute-start(bf16[128,1024]{1,0:T(8,128)(2,1)S(1)} %add_convert_fusion.1), channel_id=1, source_target_pairs={{0,4},{1,5},{2,6},{3,7},{4,0},{5,1},{6,2},{7,3},{8,12},{9,13},{10,... | collective-permute-start | bytes 786440 | tf_op jit(solution)/shard_map/ppermute | solution.py:357
  101.7 8.4 %collective-permute-start.19 = (bf16[64,128]{1,0:T(8,128)(2,1)S(1)}, bf16[64,128]{1,0:T(8,128)(2,1)S(1)}, u32[]{:S(2)}, u32[]{:S(2)}) collective-permute-start(bf16[64,128]{1,0:T(8,128)(2,1)S(1)} %get-tuple-element.46), channel_id=1, source_target_pairs={{0,0},{1,32},{2,64},{3,96},{4,128},{5,160},{6,192},{7,224},{8,8},{... | collective-permute-start | bytes 49160 | tf_op jit(solution)/shard_map/ppermute | solution.py:371
  106.5 4.8 %collective-permute-start.18 = (bf16[32,384]{1,0:T(8,128)(2,1)S(1)}, bf16[32,384]{1,0:T(8,128)(2,1)S(1)}, u32[]{:S(2)}, u32[]{:S(2)}) collective-permute-start(bf16[32,384]{1,0:T(8,128)(2,1)S(1)} %get-tuple-element.45), channel_id=1, source_target_pairs={{0,128},{8,136},{16,144},{24,152},{32,160},{40,168},{48,176},{56,1... | collective-permute-start | bytes 73736 | tf_op jit(solution)/shard_map/ppermute | solution.py:365
  111.3 25.5 %collective-permute-start.22 = (bf16[128,1024]{1,0:T(8,128)(2,1)S(1)}, bf16[128,1024]{1,0:T(8,128)(2,1)S(1)}, u32[]{:S(2)}, u32[]{:S(2)}) collective-permute-start(bf16[128,1024]{1,0:T(8,128)(2,1)S(1)} %get-tuple-element.50), channel_id=1, source_target_pairs={{0,6},{1,7},{2,0},{3,1},{4,2},{5,3},{6,4},{7,5},{8,14},{9,15},{10,... | collective-permute-start | bytes 786440 | tf_op jit(solution)/shard_map/ppermute | solution.py:357
  113.9 22.9 %collective-permute-start.23 = (bf16[128,1024]{1,0:T(8,128)(2,1)S(1)}, bf16[128,1024]{1,0:T(8,128)(2,1)S(1)}, u32[]{:S(2)}, u32[]{:S(2)}) collective-permute-start(bf16[128,1024]{1,0:T(8,128)(2,1)S(1)} %get-tuple-element.52), channel_id=1, source_target_pairs={{0,2},{1,3},{2,4},{3,5},{4,6},{5,7},{6,0},{7,1},{8,10},{9,11},{10,... | collective-permute-start | bytes 786440 | tf_op jit(solution)/shard_map/ppermute | solution.py:357
  113.9 8.4 %collective-permute-start.27 = (bf16[32,640]{1,0:T(8,128)(2,1)S(1)}, bf16[32,640]{1,0:T(8,128)(2,1)S(1)}, u32[]{:S(2)}, u32[]{:S(2)}) collective-permute-start(bf16[32,640]{1,0:T(8,128)(2,1)S(1)} %pad_maximum_fusion.refs_0_), channel_id=1, source_target_pairs={{0,1},{1,0},{2,3},{3,2},{4,5},{5,4},{6,7},{7,6},{8,9},{9,8},{10,11... | collective-permute-start | bytes 122888 | tf_op jit(solution)/shard_map/ppermute | solution.py:361
  118.2 6.2 %collective-permute-start.26 = (bf16[32,640]{1,0:T(8,128)(2,1)S(1)}, bf16[32,640]{1,0:T(8,128)(2,1)S(1)}, u32[]{:S(2)}, u32[]{:S(2)}) collective-permute-start(bf16[32,640]{1,0:T(8,128)(2,1)S(1)} %pad_maximum_fusion.refs_0_), channel_id=1, source_target_pairs={{0,6},{1,7},{2,0},{3,1},{4,2},{5,3},{6,4},{7,5},{8,14},{9,15},{10,... | collective-permute-start | bytes 122888 | tf_op jit(solution)/shard_map/ppermute | solution.py:357
  122.0 9.3 %collective-permute-start.25 = (bf16[32,640]{1,0:T(8,128)(2,1)S(1)}, bf16[32,640]{1,0:T(8,128)(2,1)S(1)}, u32[]{:S(2)}, u32[]{:S(2)}) collective-permute-start(bf16[32,640]{1,0:T(8,128)(2,1)S(1)} %pad_maximum_fusion.refs_0_), channel_id=1, source_target_pairs={{0,4},{1,5},{2,6},{3,7},{4,0},{5,1},{6,2},{7,3},{8,12},{9,13},{10,... | collective-permute-start | bytes 122888 | tf_op jit(solution)/shard_map/ppermute | solution.py:357
  122.4 9.6 %collective-permute-start.24 = (bf16[32,640]{1,0:T(8,128)(2,1)S(1)}, bf16[32,640]{1,0:T(8,128)(2,1)S(1)}, u32[]{:S(2)}, u32[]{:S(2)}) collective-permute-start(bf16[32,640]{1,0:T(8,128)(2,1)S(1)} %pad_maximum_fusion.refs_0_), channel_id=1, source_target_pairs={{0,2},{1,3},{2,4},{3,5},{4,6},{5,7},{6,0},{7,1},{8,10},{9,11},{10,... | collective-permute-start | bytes 122888 | tf_op jit(solution)/shard_map/ppermute | solution.py:357
  124.4 10.2 %collective-permute-start.30 = (bf16[32,640]{1,0:T(8,128)(2,1)S(1)}, bf16[32,640]{1,0:T(8,128)(2,1)S(1)}, u32[]{:S(2)}, u32[]{:S(2)}) collective-permute-start(bf16[32,640]{1,0:T(8,128)(2,1)S(1)} %collective-permute-done.26.refs_3_), channel_id=1, source_target_pairs={{0,1},{1,0},{2,3},{3,2},{4,5},{5,4},{6,7},{7,6},{8,9},{9,8},{10,11... | collective-permute-start | bytes 122888 | tf_op jit(solution)/shard_map/ppermute | solution.py:361
  (29 other events, 332.0 us)

commit v6 on v5

--- a/solution.py
+++ b/solution.py
@@ -434,8 +434,9 @@
     mine = after(mine, two)
     one, three = turn(after(one, mine), 3), turn(after(three, mine), 1)
     every = [mine] + [turn(mine, by) for by in range(1, Z)]
-    grad_q, grad_o = place(every + [swap(piece) for piece in every], where)
     branch = finish(image, row, (own, one, two, three))
+    every += [swap(piece) for piece in every]
+    grad_q, grad_o = place([after(mine, branch), *every[1:]], where)
     return branch[None], grad_q, grad_o
 
 

time: 139 us -> 137 us (0.986)
  starting transfers between devices: 68.9 us -> 67.1 us
    ppermute x11, starting transfers between devices: 20.6 us -> 18.3 us  [swap(): return lax.ppermute(x, 'space', [(i, i ^ 1) for i in range(2 * Z)])]
  transfers between devices with their start and end apart: 32 -> 32, of which waited for: 16 -> 13; matrix products, arithmetic and copies ran while one was open for 2% -> 2% of each run, Pallas kernels for 7% -> 7%
where the time goes in v6:
time: 137 us
  starting transfers between devices  67.1 us (49%)
  waiting for transfers between devices  36 us (26%)
  Pallas kernels  26.1 us (19%)
  local copies, waits for them, and re-layouts  4.61 us (3%)
  between operations  1.62 us (1%)
  other arithmetic  1.41 us (1%)
    ppermute x11, starting transfers between devices, swap(): return lax.ppermute(x, 'space', [(i, i ^ 1) for i in range(2 * Z)])  18.3 us
    ppermute x10, starting transfers between devices, turn(): return lax.ppermute(x, 'space', pairs)  17.7 us
    pallas_call x1, Pallas kernels, attention(): pl.pallas_call(attention_kernel, in_specs=[FAR] * (PIECES + 3), out_specs...  13.6 us
    ppermute x6, waiting for transfers between devices, turn_dp(): return lax.ppermute(x, 'dp', pairs)  13.5 us
    ppermute x2, starting transfers between devices, swap_lo(): return lax.ppermute(x, 'dp', [(i, i ^ XY) for i in range(2 * XY)])  10.6 us
    ppermute x10, waiting for transfers between devices, turn(): return lax.ppermute(x, 'space', pairs)  10.4 us
    ppermute x2, starting transfers between devices, transpose_devices(): return lax.ppermute(x, ('dp', 'space'), pairs)  8.93 us
    ppermute x6, starting transfers between devices, turn_dp(): return lax.ppermute(x, 'dp', pairs)  7.29 us
  transfers between devices with their start and end apart: 32, of which 13 were waited for; matrix products, arithmetic and copies ran while one was open for 2% of the time, Pallas kernels for 7%

profile of v6, /device:TPU:1, one launch (start us, length us, event | category | flops | bytes accessed | tf_op | source)
XLA Modules:
  0.0 136.8 jit_solution(11414484086876891198)
XLA Ops:
  2.1 4.5 %collective-permute-start.1 = (bf16[64,128]{1,0:T(8,128)(2,1)}, bf16[64,128]{1,0:T(8,128)(2,1)S(1)}, u32[]{:S(2)}, u32[]{:S(2)}) collective-permute-start(bf16[64,128]{1,0:T(8,128)(2,1)} %get-tuple-element.31), channel_id=1, source_target_pairs={{0,0},{1,32},{2,64},{3,96},{4,128},{5,160},{6,192},{7,224},{8,8},{... | collective-permute-start | bytes 49160 | tf_op jit(solution)/shard_map/ppermute | solution.py:371
  6.6 7.0 %collective-permute-start = (bf16[32,384]{1,0:T(8,128)(2,1)}, bf16[32,384]{1,0:T(8,128)(2,1)S(1)}, u32[]{:S(2)}, u32[]{:S(2)}) collective-permute-start(bf16[32,384]{1,0:T(8,128)(2,1)} %get-tuple-element.30.w_part), channel_id=1, source_target_pairs={{0,128},{8,136},{16,144},{24,152},{32,160},{40,168},{48,176},{56,1... | collective-permute-start | bytes 73736 | tf_op jit(solution)/shard_map/ppermute | solution.py:365
  21.4 2.8 %collective-permute-start.4 = (bf16[64,512]{1,0:T(8,128)(2,1)S(1)}, bf16[64,512]{1,0:T(8,128)(2,1)S(1)}, u32[]{:S(2)}, u32[]{:S(2)}) collective-permute-start(bf16[64,512]{1,0:T(8,128)(2,1)S(1)} %shard_map.87.refs_0_), channel_id=1, source_target_pairs={{0,24},{8,0},{16,8},{24,16},{32,56},{40,32},{48,40},{56,48},{64,88... | collective-permute-start | bytes 196616 | tf_op jit(solution)/shard_map/ppermute | solution.py:382
  25.6 3.6 %collective-permute-done.3.refs_2_ = bf16[64,512]{1,0:T(8,128)(2,1)S(1)} collective-permute-done((bf16[64,512]{1,0:T(8,128)(2,1)S(1)}, bf16[64,512]{1,0:T(8,128)(2,1)S(1)}, u32[]{:S(2)}, u32[]{:S(2)}) %collective-permute-start.3) | collective-permute-done | bytes 65568 | tf_op jit(solution)/shard_map/ppermute | solution.py:382
  30.5 2.8 %collective-permute-start.9 = (bf16[4,64,512]{2,1,0:T(8,128)(2,1)S(1)}, bf16[4,64,512]{2,1,0:T(8,128)(2,1)S(1)}, u32[]{:S(2)}, u32[]{:S(2)}) collective-permute-start(bf16[4,64,512]{2,1,0:T(8,128)(2,1)S(1)} %shard_map.88.refs_6_), channel_id=1, source_target_pairs={{0,96},{8,104},{16,112},{24,120},{32,0},{40,8},{48,16},{56,24},{64... | collective-permute-start | bytes 786440 | tf_op jit(solution)/shard_map/ppermute | solution.py:382
  33.9 6.3 %collective-permute-done.9.refs_9_ = bf16[4,64,512]{2,1,0:T(8,128)(2,1)S(1)} collective-permute-done((bf16[4,64,512]{2,1,0:T(8,128)(2,1)S(1)}, bf16[4,64,512]{2,1,0:T(8,128)(2,1)S(1)}, u32[]{:S(2)}, u32[]{:S(2)}) %collective-permute-start.9) | collective-permute-done | bytes 262176 | tf_op jit(solution)/shard_map/ppermute | solution.py:382
  40.2 5.1 %collective-permute-start.12 = (bf16[128,2048]{1,0:T(8,128)(2,1)}, bf16[128,2048]{1,0:T(8,128)(2,1)S(1)}, u32[]{:S(2)}, u32[]{:S(2)}) collective-permute-start(bf16[128,2048]{1,0:T(8,128)(2,1)} %shard_map.85.refs_0_), channel_id=1, source_target_pairs={{0,1},{1,0},{2,3},{3,2},{4,5},{5,4},{6,7},{7,6},{8,9},{9,8},{10,11... | collective-permute-start | bytes 1572872 | tf_op jit(solution)/shard_map/ppermute | solution.py:361
  45.4 2.6 %collective-permute-done.7.refs_7_ = bf16[4,64,512]{2,1,0:T(8,128)(2,1)S(1)} collective-permute-done((bf16[4,64,512]{2,1,0:T(8,128)(2,1)S(1)}, bf16[4,64,512]{2,1,0:T(8,128)(2,1)S(1)}, u32[]{:S(2)}, u32[]{:S(2)}) %collective-permute-start.7) | collective-permute-done | bytes 262176 | tf_op jit(solution)/shard_map/ppermute | solution.py:382
  53.3 4.5 %shard_map.89 = (bf16[768,512]{1,0:T(8,128)(2,1)}, bf16[1024,384]{1,0:T(8,128)(2,1)}, bf16[128,1024]{1,0:T(8,128)(2,1)}) custom-call(s32[4]{0:T(128)} %copy-done.4, bf16[128,2048]{1,0:T(8,128)(2,1)} %shard_map.85.refs_0_, bf16[128,2048]{1,0:T(8,128)(2,1)} %copy-done.7, bf16[128,2048]{1,0:T(8,128)(2,1)} %copy-done.6, bf16[128,2048]{1,0:T(8,128)(2,1)} %copy-done.8, ...), custom_call_target="tpu_custom_call" | custom-call | tf_op jit(solution)/shard_map/pallas_call | solution.py:65
  57.8 6.0 %collective-permute-done.11.refs_3_ = bf16[64,2048]{1,0:T(8,128)(2,1)S(1)} collective-permute-done((bf16[64,2048]{1,0:T(8,128)(2,1)S(1)}, bf16[64,2048]{1,0:T(8,128)(2,1)S(1)}, u32[]{:S(2)}, u32[]{:S(2)}) %collective-permute-start.11) | collective-permute-done | bytes 262176 | tf_op jit(solution)/shard_map/ppermute | solution.py:357
  68.0 13.6 %shard_map.90 = (bf16[16,64,512]{2,1,0:T(8,128)(2,1)}, bf16[128,1024]{1,0:T(8,128)(2,1)}, bf16[384,1024]{1,0:T(8,128)(2,1)}, bf16[128,1024]{1,0:T(8,128)(2,1)}, ...) custom-call(bf16[128,2048]{1,0:T(8,128)(2,1)} %shard_map.85.refs_0_, ...), custom_call_target="tpu_custom_call" | custom-call | flops 17179869184 | bytes 8388608 | tf_op jit(solution)/shard_map/pallas_call | solution.py:168
  81.7 4.3 %all-to-all-start = ((bf16[16,64,512]{2,1,0:T(8,128)(2,1)}), bf16[16,64,512]{2,1,0:T(8,128)(2,1)S(1)}, u32[]{:S(2)}, u32[]{:S(2)}) async-start(bf16[16,64,512]{2,1,0:T(8,128)(2,1)} %get-tuple-element.44), calls=%async_computation | async-start | bytes 2097152 | tf_op jit(solution)/shard_map/all_to_all | solution.py:387
  86.8 2.4 %collective-permute-done.20 = bf16[128,1024]{1,0:T(8,128)(2,1)S(1)} collective-permute-done((bf16[128,1024]{1,0:T(8,128)(2,1)}, bf16[128,1024]{1,0:T(8,128)(2,1)S(1)}, u32[]{:S(2)}, u32[]{:S(2)}) %collective-permute-start.20) | collective-permute-done | bytes 262176 | tf_op jit(solution)/shard_map/ppermute | solution.py:361
  90.3 3.8 %collective-permute-start.21 = (bf16[128,1024]{1,0:T(8,128)(2,1)S(1)}, bf16[128,1024]{1,0:T(8,128)(2,1)S(1)}, u32[]{:S(2)}, u32[]{:S(2)}) collective-permute-start(bf16[128,1024]{1,0:T(8,128)(2,1)S(1)} %add_convert_fusion.1), channel_id=1, source_target_pairs={{0,4},{1,5},{2,6},{3,7},{4,0},{5,1},{6,2},{7,3},{8,12},{9,13},{10,... | collective-permute-start | bytes 786440 | tf_op jit(solution)/shard_map/ppermute | solution.py:357
  94.1 6.9 %all-to-all-done.sent = bf16[16,64,512]{2,1,0:T(8,128)(2,1)S(1)} async-done(((bf16[16,64,512]{2,1,0:T(8,128)(2,1)}), bf16[16,64,512]{2,1,0:T(8,128)(2,1)S(1)}, u32[]{:S(2)}, u32[]{:S(2)}) %all-to-all-start) | async-done | bytes 1048608 | tf_op jit(solution)/shard_map/all_to_all | solution.py:387
  101.7 4.4 %collective-permute-start.19 = (bf16[64,128]{1,0:T(8,128)(2,1)S(1)}, bf16[64,128]{1,0:T(8,128)(2,1)S(1)}, u32[]{:S(2)}, u32[]{:S(2)}) collective-permute-start(bf16[64,128]{1,0:T(8,128)(2,1)S(1)} %get-tuple-element.47), channel_id=1, source_target_pairs={{0,0},{1,32},{2,64},{3,96},{4,128},{5,160},{6,192},{7,224},{8,8},{... | collective-permute-start | bytes 49160 | tf_op jit(solution)/shard_map/ppermute | solution.py:371
  106.5 3.6 %collective-permute-start.18 = (bf16[32,384]{1,0:T(8,128)(2,1)S(1)}, bf16[32,384]{1,0:T(8,128)(2,1)S(1)}, u32[]{:S(2)}, u32[]{:S(2)}) collective-permute-start(bf16[32,384]{1,0:T(8,128)(2,1)S(1)} %get-tuple-element.46), channel_id=1, source_target_pairs={{0,128},{8,136},{16,144},{24,152},{32,160},{40,168},{48,176},{56,1... | collective-permute-start | bytes 73736 | tf_op jit(solution)/shard_map/ppermute | solution.py:365
  111.3 2.6 %collective-permute-start.22 = (bf16[128,1024]{1,0:T(8,128)(2,1)S(1)}, bf16[128,1024]{1,0:T(8,128)(2,1)S(1)}, u32[]{:S(2)}, u32[]{:S(2)}) collective-permute-start(bf16[128,1024]{1,0:T(8,128)(2,1)S(1)} %get-tuple-element.51), channel_id=1, source_target_pairs={{0,6},{1,7},{2,0},{3,1},{4,2},{5,3},{6,4},{7,5},{8,14},{9,15},{10,... | collective-permute-start | bytes 786440 | tf_op jit(solution)/shard_map/ppermute | solution.py:357
  113.9 3.6 %collective-permute-start.26 = (bf16[32,640]{1,0:T(8,128)(2,1)S(1)}, bf16[32,640]{1,0:T(8,128)(2,1)S(1)}, u32[]{:S(2)}, u32[]{:S(2)}) collective-permute-start(bf16[32,640]{1,0:T(8,128)(2,1)S(1)} %pad_maximum_fusion.refs_0_), channel_id=1, source_target_pairs={{0,6},{1,7},{2,0},{3,1},{4,2},{5,3},{6,4},{7,5},{8,14},{9,15},{10,... | collective-permute-start | bytes 122888 | tf_op jit(solution)/shard_map/ppermute | solution.py:357
  117.5 2.9 %collective-permute-start.25 = (bf16[32,640]{1,0:T(8,128)(2,1)S(1)}, bf16[32,640]{1,0:T(8,128)(2,1)S(1)}, u32[]{:S(2)}, u32[]{:S(2)}) collective-permute-start(bf16[32,640]{1,0:T(8,128)(2,1)S(1)} %pad_maximum_fusion.refs_0_), channel_id=1, source_target_pairs={{0,4},{1,5},{2,6},{3,7},{4,0},{5,1},{6,2},{7,3},{8,12},{9,13},{10,... | collective-permute-start | bytes 122888 | tf_op jit(solution)/shard_map/ppermute | solution.py:357
  120.4 4.0 %collective-permute-done.26.refs_3_ = bf16[32,640]{1,0:T(8,128)(2,1)S(1)} collective-permute-done((bf16[32,640]{1,0:T(8,128)(2,1)S(1)}, bf16[32,640]{1,0:T(8,128)(2,1)S(1)}, u32[]{:S(2)}, u32[]{:S(2)}) %collective-permute-start.26) | collective-permute-done | bytes 40992 | tf_op jit(solution)/shard_map/ppermute | solution.py:357
  124.4 5.0 %collective-permute-start.27 = (bf16[32,640]{1,0:T(8,128)(2,1)S(1)}, bf16[32,640]{1,0:T(8,128)(2,1)S(1)}, u32[]{:S(2)}, u32[]{:S(2)}) collective-permute-start(bf16[32,640]{1,0:T(8,128)(2,1)S(1)} %pad_maximum_fusion.refs_0_), channel_id=1, source_target_pairs={{0,1},{1,0},{2,3},{3,2},{4,5},{5,4},{6,7},{7,6},{8,9},{9,8},{10,11... | collective-permute-start | bytes 122888 | tf_op jit(solution)/shard_map/ppermute | solution.py:361
  129.4 2.4 %collective-permute-start.30 = (bf16[32,640]{1,0:T(8,128)(2,1)S(1)}, bf16[32,640]{1,0:T(8,128)(2,1)S(1)}, u32[]{:S(2)}, u32[]{:S(2)}) collective-permute-start(bf16[32,640]{1,0:T(8,128)(2,1)S(1)} %collective-permute-done.26.refs_3_), channel_id=1, source_target_pairs={{0,1},{1,0},{2,3},{3,2},{4,5},{5,4},{6,7},{7,6},{8,9},{9,8},{10,11... | collective-permute-start | bytes 122888 | tf_op jit(solution)/shard_map/ppermute | solution.py:361
  131.8 2.3 %collective-permute-start.29 = (bf16[32,640]{1,0:T(8,128)(2,1)S(1)}, bf16[32,640]{1,0:T(8,128)(2,1)S(1)}, u32[]{:S(2)}, u32[]{:S(2)}) collective-permute-start(bf16[32,640]{1,0:T(8,128)(2,1)S(1)} %collective-permute-done.25.refs_2_), channel_id=1, source_target_pairs={{0,1},{1,0},{2,3},{3,2},{4,5},{5,4},{6,7},{7,6},{8,9},{9,8},{10,11... | collective-permute-start | bytes 122888 | tf_op jit(solution)/shard_map/ppermute | solution.py:361
  (100 shorter events, 28.1 us)
Async XLA Ops:
  2.1 15.6 %collective-permute-start.1 = (bf16[64,128]{1,0:T(8,128)(2,1)}, bf16[64,128]{1,0:T(8,128)(2,1)S(1)}, u32[]{:S(2)}, u32[]{:S(2)}) collective-permute-start(bf16[64,128]{1,0:T(8,128)(2,1)} %get-tuple-element.31), channel_id=1, source_target_pairs={{0,0},{1,32},{2,64},{3,96},{4,128},{5,160},{6,192},{7,224},{8,8},{... | collective-permute-start | bytes 49160 | tf_op jit(solution)/shard_map/ppermute | solution.py:371
  6.6 11.1 %collective-permute-start = (bf16[32,384]{1,0:T(8,128)(2,1)}, bf16[32,384]{1,0:T(8,128)(2,1)S(1)}, u32[]{:S(2)}, u32[]{:S(2)}) collective-permute-start(bf16[32,384]{1,0:T(8,128)(2,1)} %get-tuple-element.30.w_part), channel_id=1, source_target_pairs={{0,128},{8,136},{16,144},{24,152},{32,160},{40,168},{48,176},{56,1... | collective-permute-start | bytes 73736 | tf_op jit(solution)/shard_map/ppermute | solution.py:365
  17.7 30.2 %collective-permute-start.6 = (bf16[128,2048]{1,0:T(8,128)(2,1)}, bf16[128,2048]{1,0:T(8,128)(2,1)S(1)}, u32[]{:S(2)}, u32[]{:S(2)}) collective-permute-start(bf16[128,2048]{1,0:T(8,128)(2,1)} %shard_map.85.refs_0_), channel_id=1, source_target_pairs={{0,6},{1,7},{2,0},{3,1},{4,2},{5,3},{6,4},{7,5},{8,14},{9,15},{10,... | collective-permute-start | bytes 1572872 | tf_op jit(solution)/shard_map/ppermute | solution.py:357
  19.7 28.2 %collective-permute-start.5 = (bf16[128,2048]{1,0:T(8,128)(2,1)}, bf16[128,2048]{1,0:T(8,128)(2,1)S(1)}, u32[]{:S(2)}, u32[]{:S(2)}) collective-permute-start(bf16[128,2048]{1,0:T(8,128)(2,1)} %shard_map.85.refs_0_), channel_id=1, source_target_pairs={{0,2},{1,3},{2,4},{3,5},{4,6},{5,7},{6,0},{7,1},{8,10},{9,11},{10,... | collective-permute-start | bytes 1572872 | tf_op jit(solution)/shard_map/ppermute | solution.py:357
  24.3 4.9 %collective-permute-start.3 = (bf16[64,512]{1,0:T(8,128)(2,1)S(1)}, bf16[64,512]{1,0:T(8,128)(2,1)S(1)}, u32[]{:S(2)}, u32[]{:S(2)}) collective-permute-start(bf16[64,512]{1,0:T(8,128)(2,1)S(1)} %shard_map.87.refs_0_), channel_id=1, source_target_pairs={{0,16},{8,24},{16,0},{24,8},{32,48},{40,56},{48,32},{56,40},{64,80... | collective-permute-start | bytes 196616 | tf_op jit(solution)/shard_map/ppermute | solution.py:382
  24.6 5.3 %collective-permute-start.2 = (bf16[64,512]{1,0:T(8,128)(2,1)S(1)}, bf16[64,512]{1,0:T(8,128)(2,1)S(1)}, u32[]{:S(2)}, u32[]{:S(2)}) collective-permute-start(bf16[64,512]{1,0:T(8,128)(2,1)S(1)} %shard_map.87.refs_0_), channel_id=1, source_target_pairs={{0,8},{8,16},{16,24},{24,0},{32,40},{40,48},{48,56},{56,32},{64,72... | collective-permute-start | bytes 196616 | tf_op jit(solution)/shard_map/ppermute | solution.py:382
  30.5 9.8 %collective-permute-start.9 = (bf16[4,64,512]{2,1,0:T(8,128)(2,1)S(1)}, bf16[4,64,512]{2,1,0:T(8,128)(2,1)S(1)}, u32[]{:S(2)}, u32[]{:S(2)}) collective-permute-start(bf16[4,64,512]{2,1,0:T(8,128)(2,1)S(1)} %shard_map.88.refs_6_), channel_id=1, source_target_pairs={{0,96},{8,104},{16,112},{24,120},{32,0},{40,8},{48,16},{56,24},{64... | collective-permute-start | bytes 786440 | tf_op jit(solution)/shard_map/ppermute | solution.py:382
  33.2 12.1 %collective-permute-start.8 = (bf16[4,64,512]{2,1,0:T(8,128)(2,1)S(1)}, bf16[4,64,512]{2,1,0:T(8,128)(2,1)S(1)}, u32[]{:S(2)}, u32[]{:S(2)}) collective-permute-start(bf16[4,64,512]{2,1,0:T(8,128)(2,1)S(1)} %shard_map.88.refs_6_), channel_id=1, source_target_pairs={{0,64},{8,72},{16,80},{24,88},{32,96},{40,104},{48,112},{56,120},{... | collective-permute-start | bytes 786440 | tf_op jit(solution)/shard_map/ppermute | solution.py:382
  33.2 14.7 %collective-permute-start.7 = (bf16[4,64,512]{2,1,0:T(8,128)(2,1)S(1)}, bf16[4,64,512]{2,1,0:T(8,128)(2,1)S(1)}, u32[]{:S(2)}, u32[]{:S(2)}) collective-permute-start(bf16[4,64,512]{2,1,0:T(8,128)(2,1)S(1)} %shard_map.88.refs_6_), channel_id=1, source_target_pairs={{0,32},{8,40},{16,48},{24,56},{32,64},{40,72},{48,80},{56,88},{64,... | collective-permute-start | bytes 786440 | tf_op jit(solution)/shard_map/ppermute | solution.py:382
  40.2 11.3 %collective-permute-start.12 = (bf16[128,2048]{1,0:T(8,128)(2,1)}, bf16[128,2048]{1,0:T(8,128)(2,1)S(1)}, u32[]{:S(2)}, u32[]{:S(2)}) collective-permute-start(bf16[128,2048]{1,0:T(8,128)(2,1)} %shard_map.85.refs_0_), channel_id=1, source_target_pairs={{0,1},{1,0},{2,3},{3,2},{4,5},{5,4},{6,7},{7,6},{8,9},{9,8},{10,11... | collective-permute-start | bytes 1572872 | tf_op jit(solution)/shard_map/ppermute | solution.py:361
  49.0 14.8 %collective-permute-start.11 = (bf16[64,2048]{1,0:T(8,128)(2,1)S(1)}, bf16[64,2048]{1,0:T(8,128)(2,1)S(1)}, u32[]{:S(2)}, u32[]{:S(2)}) collective-permute-start(bf16[64,2048]{1,0:T(8,128)(2,1)S(1)} %slice.22), channel_id=1, source_target_pairs={{0,6},{1,7},{2,0},{3,1},{4,2},{5,3},{6,4},{7,5},{8,14},{9,15},{10,... | collective-permute-start | bytes 786440 | tf_op jit(solution)/shard_map/ppermute | solution.py:357
  50.5 13.7 %collective-permute-start.10 = (bf16[64,2048]{1,0:T(8,128)(2,1)S(1)}, bf16[64,2048]{1,0:T(8,128)(2,1)S(1)}, u32[]{:S(2)}, u32[]{:S(2)}) collective-permute-start(bf16[64,2048]{1,0:T(8,128)(2,1)S(1)} %slice.21), channel_id=1, source_target_pairs={{0,2},{1,3},{2,4},{3,5},{4,6},{5,7},{6,0},{7,1},{8,10},{9,11},{10,... | collective-permute-start | bytes 786440 | tf_op jit(solution)/shard_map/ppermute | solution.py:357
  81.7 19.3 %all-to-all-start = ((bf16[16,64,512]{2,1,0:T(8,128)(2,1)}), bf16[16,64,512]{2,1,0:T(8,128)(2,1)S(1)}, u32[]{:S(2)}, u32[]{:S(2)}) async-start(bf16[16,64,512]{2,1,0:T(8,128)(2,1)} %get-tuple-element.44), calls=%async_computation | async-start | bytes 2097152 | tf_op jit(solution)/shard_map/all_to_all | solution.py:387
  86.0 20.1 %collective-permute-start.17 = (bf16[384,1024]{1,0:T(8,128)(2,1)}, bf16[384,1024]{1,0:T(8,128)(2,1)S(1)}, u32[]{:S(2)}, u32[]{:S(2)}) collective-permute-start(bf16[384,1024]{1,0:T(8,128)(2,1)} %get-tuple-element.42), channel_id=1, source_target_pairs={{0,1},{1,0},{2,3},{3,2},{4,5},{5,4},{6,7},{7,6},{8,9},{9,8},{10,11... | collective-permute-start | bytes 2359304 | tf_op jit(solution)/shard_map/ppermute | solution.py:361
  90.3 21.1 %collective-permute-start.21 = (bf16[128,1024]{1,0:T(8,128)(2,1)S(1)}, bf16[128,1024]{1,0:T(8,128)(2,1)S(1)}, u32[]{:S(2)}, u32[]{:S(2)}) collective-permute-start(bf16[128,1024]{1,0:T(8,128)(2,1)S(1)} %add_convert_fusion.1), channel_id=1, source_target_pairs={{0,4},{1,5},{2,6},{3,7},{4,0},{5,1},{6,2},{7,3},{8,12},{9,13},{10,... | collective-permute-start | bytes 786440 | tf_op jit(solution)/shard_map/ppermute | solution.py:357
  101.7 8.4 %collective-permute-start.19 = (bf16[64,128]{1,0:T(8,128)(2,1)S(1)}, bf16[64,128]{1,0:T(8,128)(2,1)S(1)}, u32[]{:S(2)}, u32[]{:S(2)}) collective-permute-start(bf16[64,128]{1,0:T(8,128)(2,1)S(1)} %get-tuple-element.47), channel_id=1, source_target_pairs={{0,0},{1,32},{2,64},{3,96},{4,128},{5,160},{6,192},{7,224},{8,8},{... | collective-permute-start | bytes 49160 | tf_op jit(solution)/shard_map/ppermute | solution.py:371
  106.5 4.8 %collective-permute-start.18 = (bf16[32,384]{1,0:T(8,128)(2,1)S(1)}, bf16[32,384]{1,0:T(8,128)(2,1)S(1)}, u32[]{:S(2)}, u32[]{:S(2)}) collective-permute-start(bf16[32,384]{1,0:T(8,128)(2,1)S(1)} %get-tuple-element.46), channel_id=1, source_target_pairs={{0,128},{8,136},{16,144},{24,152},{32,160},{40,168},{48,176},{56,1... | collective-permute-start | bytes 73736 | tf_op jit(solution)/shard_map/ppermute | solution.py:365
  111.3 22.8 %collective-permute-start.22 = (bf16[128,1024]{1,0:T(8,128)(2,1)S(1)}, bf16[128,1024]{1,0:T(8,128)(2,1)S(1)}, u32[]{:S(2)}, u32[]{:S(2)}) collective-permute-start(bf16[128,1024]{1,0:T(8,128)(2,1)S(1)} %get-tuple-element.51), channel_id=1, source_target_pairs={{0,6},{1,7},{2,0},{3,1},{4,2},{5,3},{6,4},{7,5},{8,14},{9,15},{10,... | collective-permute-start | bytes 786440 | tf_op jit(solution)/shard_map/ppermute | solution.py:357
  113.9 20.2 %collective-permute-start.23 = (bf16[128,1024]{1,0:T(8,128)(2,1)S(1)}, bf16[128,1024]{1,0:T(8,128)(2,1)S(1)}, u32[]{:S(2)}, u32[]{:S(2)}) collective-permute-start(bf16[128,1024]{1,0:T(8,128)(2,1)S(1)} %get-tuple-element.53), channel_id=1, source_target_pairs={{0,2},{1,3},{2,4},{3,5},{4,6},{5,7},{6,0},{7,1},{8,10},{9,11},{10,... | collective-permute-start | bytes 786440 | tf_op jit(solution)/shard_map/ppermute | solution.py:357
  113.9 10.5 %collective-permute-start.26 = (bf16[32,640]{1,0:T(8,128)(2,1)S(1)}, bf16[32,640]{1,0:T(8,128)(2,1)S(1)}, u32[]{:S(2)}, u32[]{:S(2)}) collective-permute-start(bf16[32,640]{1,0:T(8,128)(2,1)S(1)} %pad_maximum_fusion.refs_0_), channel_id=1, source_target_pairs={{0,6},{1,7},{2,0},{3,1},{4,2},{5,3},{6,4},{7,5},{8,14},{9,15},{10,... | collective-permute-start | bytes 122888 | tf_op jit(solution)/shard_map/ppermute | solution.py:357
  117.5 11.9 %collective-permute-start.25 = (bf16[32,640]{1,0:T(8,128)(2,1)S(1)}, bf16[32,640]{1,0:T(8,128)(2,1)S(1)}, u32[]{:S(2)}, u32[]{:S(2)}) collective-permute-start(bf16[32,640]{1,0:T(8,128)(2,1)S(1)} %pad_maximum_fusion.refs_0_), channel_id=1, source_target_pairs={{0,4},{1,5},{2,6},{3,7},{4,0},{5,1},{6,2},{7,3},{8,12},{9,13},{10,... | collective-permute-start | bytes 122888 | tf_op jit(solution)/shard_map/ppermute | solution.py:357
  120.4 11.4 %collective-permute-start.24 = (bf16[32,640]{1,0:T(8,128)(2,1)S(1)}, bf16[32,640]{1,0:T(8,128)(2,1)S(1)}, u32[]{:S(2)}, u32[]{:S(2)}) collective-permute-start(bf16[32,640]{1,0:T(8,128)(2,1)S(1)} %pad_maximum_fusion.refs_0_), channel_id=1, source_target_pairs={{0,2},{1,3},{2,4},{3,5},{4,6},{5,7},{6,0},{7,1},{8,10},{9,11},{10,... | collective-permute-start | bytes 122888 | tf_op jit(solution)/shard_map/ppermute | solution.py:357
  124.4 10.9 %collective-permute-start.27 = (bf16[32,640]{1,0:T(8,128)(2,1)S(1)}, bf16[32,640]{1,0:T(8,128)(2,1)S(1)}, u32[]{:S(2)}, u32[]{:S(2)}) collective-permute-start(bf16[32,640]{1,0:T(8,128)(2,1)S(1)} %pad_maximum_fusion.refs_0_), channel_id=1, source_target_pairs={{0,1},{1,0},{2,3},{3,2},{4,5},{5,4},{6,7},{7,6},{8,9},{9,8},{10,11... | collective-permute-start | bytes 122888 | tf_op jit(solution)/shard_map/ppermute | solution.py:361
  129.4 5.9 %collective-permute-start.30 = (bf16[32,640]{1,0:T(8,128)(2,1)S(1)}, bf16[32,640]{1,0:T(8,128)(2,1)S(1)}, u32[]{:S(2)}, u32[]{:S(2)}) collective-permute-start(bf16[32,640]{1,0:T(8,128)(2,1)S(1)} %collective-permute-done.26.refs_3_), channel_id=1, source_target_pairs={{0,1},{1,0},{2,3},{3,2},{4,5},{5,4},{6,7},{7,6},{8,9},{9,8},{10,11... | collective-permute-start | bytes 122888 | tf_op jit(solution)/shard_map/ppermute | solution.py:361
  (29 other events, 324.6 us)

commit v7 on v6

--- a/solution.py
+++ b/solution.py
@@ -74,8 +74,8 @@
 
 def attention_kernel(*refs):
     pieces, rest = refs[:PIECES], refs[PIECES:]
-    first, wq_far, wo_far, grads, *results = rest[:10]
-    x, wq, wo, qkv, att, dqkv, turned, sent, terms, sems = rest[10:]
+    first, wq_far, wo_far, grads, dqkv_far = rest[:5]
+    x, wq, wo, qkv, att, dqkv, turned, sent, sems = rest[5:]
     starts = (0, 128, 256, 320, 384, 512, 640, 768, 832, 896)
     late = (2, 3, 7, 8)
     copies = [pltpu.make_async_copy(wq_far, wq, sems.at[PIECES])]
@@ -133,6 +133,8 @@
             turned[PAIR:, :] += dv
 
     dqkv[:, PAIR:] = turned[...].T.astype(BF16)
+    early = pltpu.make_async_copy(dqkv, dqkv_far, sems.at[PIECES])
+    early.start()
     for copy in rest_of_x:
         copy.wait()
     grad = tn(dqkv[...], x[:, :C]).T.astype(BF16)
@@ -148,33 +150,41 @@
             sent[xy, lo * ROWS : (lo + 1) * ROWS, QKV:] = grad[
                 y * ROWS : (y + 1) * ROWS, at : at + PAIR
             ]
-    copies = [pltpu.make_async_copy(sent, grads, sems.at[0])]
-    copies[0].start()
-    far, near = results[0], results[1]
+    copy = pltpu.make_async_copy(sent, grads, sems.at[0])
+    copy.start()
+    copy.wait()
+    early.wait()
+
+
+def terms_kernel(dqkv, wq, far, near, two, own, one, three):
     order = [(Z + 2, far)]
     order += [(Z + spot, near.at[i * CELLS : (i + 1) * CELLS]) for i, spot in enumerate((0, 1, 3))]
-    order += list(zip((2, 0, 1, 3), results[2:]))
-    for i, (spot, to) in enumerate(order):
+    order += [(2, two), (0, own), (1, one), (3, three)]
+    for spot, to in order:
         rows = slice(spot * CELLS, (spot + 1) * CELLS)
-        terms[rows, :] = nt(dqkv[rows, :], wq[...]).astype(BF16)
-        copies.append(pltpu.make_async_copy(terms.at[rows, :], to, sems.at[i + 1]))
-        copies[-1].start()
-    for copy in copies:
-        copy.wait()
-
-
-def attention(pieces, first, wq, wo):
-    cells = 8 * CELLS
-    return pl.pallas_call(
-        attention_kernel,
-        in_specs=[FAR] * (PIECES + 3),
-        out_specs=[FAR] * 7,
+        to[...] = nt(dqkv[rows, :], wq[...]).astype(BF16)
+
+
+def dnormed_terms(dqkv, wq):
+    return pl.pallas_call(
+        terms_kernel,
         out_shape=(
-            struct((XY, 2 * ROWS, QKV + PAIR)),
             struct((CELLS, C)),
             struct((3 * CELLS, C)),
             *[struct((CELLS, C))] * Z,
         ),
+        compiler_params=pltpu.CompilerParams(vmem_limit_bytes=16 * 2**20),
+        cost_estimate=pl.CostEstimate(flops=2**34, bytes_accessed=2**23, transcendentals=0),
+    )(dqkv, wq)
+
+
+def attention(pieces, first, wq, wo):
+    cells = 8 * CELLS
+    return pl.pallas_call(
+        attention_kernel,
+        in_specs=[FAR] * (PIECES + 3),
+        out_specs=[FAR] * 2,
+        out_shape=(struct((XY, 2 * ROWS, QKV + PAIR)), struct((cells, QKV))),
         scratch_shapes=[
             pltpu.VMEM((cells, 2 * C), BF16),
             pltpu.VMEM((C, QKV), BF16),
@@ -184,7 +194,6 @@
             pltpu.VMEM((cells, QKV), BF16),
             pltpu.VMEM((2 * PAIR, cells), F32),
             pltpu.VMEM((XY, 2 * ROWS, QKV + PAIR), BF16),
-            pltpu.VMEM((cells, C), BF16),
             pltpu.SemaphoreType.DMA((PIECES + 6,)),
         ],
         compiler_params=PARAMS,
@@ -418,8 +427,9 @@
     two = after(two, first)
     pieces = [x, one, *two, three]
     pieces += [others[0], others[1], *[swap(piece) for piece in two], others[2]]
-    grads, far, near, two, own, one, three = attention(pieces, first, wq, wo)
+    grads, dqkv = attention(pieces, first, wq, wo)
     grads = over_xy(grads)
+    far, near, two, own, one, three = dnormed_terms(dqkv, wq)
 
     two = turn(add(two, swap(far)), 2)
     near = swap(near)

time: 137 us -> 135 us (0.985)
  starting transfers between devices: 67.1 us -> 64.6 us
    ppermute x11, starting transfers between devices: 18.3 us -> 16.1 us  [swap(): return lax.ppermute(x, 'space', [(i, i ^ 1) for i in range(2 * Z)])]
    pallas_call x0 -> x1, Pallas kernels: none -> 2.08 us  [dnormed_terms(): pl.pallas_call(terms_kernel, out_shape=(struct((CELLS, C)), struct((3 * C...]
    ppermute x10, waiting for transfers between devices: 10.4 us -> 12.4 us  [turn(): return lax.ppermute(x, 'space', pairs)]
    all_to_all x1, waiting for transfers between devices: 6.9 us -> 5.04 us  [over_xy(): return lax.all_to_all(x, 'dp', 0, 0, axis_index_groups=groups, tiled=True)]
    pallas_call x1, Pallas kernels: 13.6 us -> 11.9 us  [attention(): pl.pallas_call(attention_kernel, in_specs=[FAR] * (PIECES + 3), out_specs...]
    unnamed x42 -> x40, local copies, waits for them, and re-layouts: 3.21 us -> 4.32 us
  transfers between devices with their start and end apart: 32 -> 32, of which waited for: 13 -> 13; matrix products, arithmetic and copies ran while one was open for 2% -> 1% of each run, Pallas kernels for 7% -> 9%
where the time goes in v7:
time: 135 us
  starting transfers between devices  64.6 us (48%)
  waiting for transfers between devices  36.1 us (27%)
  Pallas kernels  26.4 us (20%)
  local copies, waits for them, and re-layouts  5.73 us (4%)
  between operations  1.59 us (1%)
    ppermute x10, starting transfers between devices, turn(): return lax.ppermute(x, 'space', pairs)  17.3 us
    ppermute x11, starting transfers between devices, swap(): return lax.ppermute(x, 'space', [(i, i ^ 1) for i in range(2 * Z)])  16.1 us
    ppermute x6, waiting for transfers between devices, turn_dp(): return lax.ppermute(x, 'dp', pairs)  13.5 us
    ppermute x10, waiting for transfers between devices, turn(): return lax.ppermute(x, 'space', pairs)  12.4 us
    pallas_call x1, Pallas kernels, attention(): pl.pallas_call(attention_kernel, in_specs=[FAR] * (PIECES + 3), out_specs...  11.9 us
    ppermute x2, starting transfers between devices, swap_lo(): return lax.ppermute(x, 'dp', [(i, i ^ XY) for i in range(2 * XY)])  10.6 us
    ppermute x2, starting transfers between devices, transpose_devices(): return lax.ppermute(x, ('dp', 'space'), pairs)  9.11 us
    ppermute x6, starting transfers between devices, turn_dp(): return lax.ppermute(x, 'dp', pairs)  7.29 us
  transfers between devices with their start and end apart: 32, of which 13 were waited for; matrix products, arithmetic and copies ran while one was open for 1% of the time, Pallas kernels for 9%

profile of v7, /device:TPU:1, one launch (start us, length us, event | category | flops | bytes accessed | tf_op | source)
XLA Modules:
  0.0 134.9 jit_solution(1577799907685988311)
XLA Ops:
  2.1 4.5 %collective-permute-start.1 = (bf16[64,128]{1,0:T(8,128)(2,1)}, bf16[64,128]{1,0:T(8,128)(2,1)S(1)}, u32[]{:S(2)}, u32[]{:S(2)}) collective-permute-start(bf16[64,128]{1,0:T(8,128)(2,1)} %get-tuple-element.32), channel_id=1, source_target_pairs={{0,0},{1,32},{2,64},{3,96},{4,128},{5,160},{6,192},{7,224},{8,8},{... | collective-permute-start | bytes 49160 | tf_op jit(solution)/shard_map/ppermute | solution.py:380
  6.6 7.0 %collective-permute-start = (bf16[32,384]{1,0:T(8,128)(2,1)}, bf16[32,384]{1,0:T(8,128)(2,1)S(1)}, u32[]{:S(2)}, u32[]{:S(2)}) collective-permute-start(bf16[32,384]{1,0:T(8,128)(2,1)} %get-tuple-element.31.w_part), channel_id=1, source_target_pairs={{0,128},{8,136},{16,144},{24,152},{32,160},{40,168},{48,176},{56,1... | collective-permute-start | bytes 73736 | tf_op jit(solution)/shard_map/ppermute | solution.py:374
  15.6 2.1 %shard_map.85.refs_0_ = bf16[128,2048]{1,0:T(8,128)(2,1)} custom-call(bf16[128,1024]{1,0:T(8,128)(2,1)} %bitcast.11, bf16[128,1024]{1,0:T(8,128)(2,1)} %bitcast.13, bf16[1,2048]{1,0:T(2,128)(2,1)} %constant_dynamic-slice_fusion.row), custom_call_target="tpu_custom_call" | custom-call | tf_op jit(solution)/shard_map/pallas_call | solution.py:220
  21.4 2.8 %collective-permute-start.4 = (bf16[64,512]{1,0:T(8,128)(2,1)S(1)}, bf16[64,512]{1,0:T(8,128)(2,1)S(1)}, u32[]{:S(2)}, u32[]{:S(2)}) collective-permute-start(bf16[64,512]{1,0:T(8,128)(2,1)S(1)} %shard_map.87.refs_0_), channel_id=1, source_target_pairs={{0,24},{8,0},{16,8},{24,16},{32,56},{40,32},{48,40},{56,48},{64,88... | collective-permute-start | bytes 196616 | tf_op jit(solution)/shard_map/ppermute | solution.py:391
  25.6 3.6 %collective-permute-done.3.refs_2_ = bf16[64,512]{1,0:T(8,128)(2,1)S(1)} collective-permute-done((bf16[64,512]{1,0:T(8,128)(2,1)S(1)}, bf16[64,512]{1,0:T(8,128)(2,1)S(1)}, u32[]{:S(2)}, u32[]{:S(2)}) %collective-permute-start.3) | collective-permute-done | bytes 65568 | tf_op jit(solution)/shard_map/ppermute | solution.py:391
  30.5 2.8 %collective-permute-start.9 = (bf16[4,64,512]{2,1,0:T(8,128)(2,1)S(1)}, bf16[4,64,512]{2,1,0:T(8,128)(2,1)S(1)}, u32[]{:S(2)}, u32[]{:S(2)}) collective-permute-start(bf16[4,64,512]{2,1,0:T(8,128)(2,1)S(1)} %shard_map.88.refs_6_), channel_id=1, source_target_pairs={{0,96},{8,104},{16,112},{24,120},{32,0},{40,8},{48,16},{56,24},{64... | collective-permute-start | bytes 786440 | tf_op jit(solution)/shard_map/ppermute | solution.py:391
  33.9 6.3 %collective-permute-done.9.refs_9_ = bf16[4,64,512]{2,1,0:T(8,128)(2,1)S(1)} collective-permute-done((bf16[4,64,512]{2,1,0:T(8,128)(2,1)S(1)}, bf16[4,64,512]{2,1,0:T(8,128)(2,1)S(1)}, u32[]{:S(2)}, u32[]{:S(2)}) %collective-permute-start.9) | collective-permute-done | bytes 262176 | tf_op jit(solution)/shard_map/ppermute | solution.py:391
  40.2 5.1 %collective-permute-start.12 = (bf16[128,2048]{1,0:T(8,128)(2,1)}, bf16[128,2048]{1,0:T(8,128)(2,1)S(1)}, u32[]{:S(2)}, u32[]{:S(2)}) collective-permute-start(bf16[128,2048]{1,0:T(8,128)(2,1)} %shard_map.85.refs_0_), channel_id=1, source_target_pairs={{0,1},{1,0},{2,3},{3,2},{4,5},{5,4},{6,7},{7,6},{8,9},{9,8},{10,11... | collective-permute-start | bytes 1572872 | tf_op jit(solution)/shard_map/ppermute | solution.py:370
  45.4 2.6 %collective-permute-done.7.refs_7_ = bf16[4,64,512]{2,1,0:T(8,128)(2,1)S(1)} collective-permute-done((bf16[4,64,512]{2,1,0:T(8,128)(2,1)S(1)}, bf16[4,64,512]{2,1,0:T(8,128)(2,1)S(1)}, u32[]{:S(2)}, u32[]{:S(2)}) %collective-permute-start.7) | collective-permute-done | bytes 262176 | tf_op jit(solution)/shard_map/ppermute | solution.py:391
  53.3 4.5 %shard_map.89 = (bf16[768,512]{1,0:T(8,128)(2,1)}, bf16[1024,384]{1,0:T(8,128)(2,1)}, bf16[128,1024]{1,0:T(8,128)(2,1)}) custom-call(s32[4]{0:T(128)} %copy-done.4, bf16[128,2048]{1,0:T(8,128)(2,1)} %shard_map.85.refs_0_, bf16[128,2048]{1,0:T(8,128)(2,1)} %copy-done.9, bf16[128,2048]{1,0:T(8,128)(2,1)} %copy-done.8, bf16[128,2048]{1,0:T(8,128)(2,1)} %copy-done.10, ...), custom_call_target="tpu_custom_call" | custom-call | tf_op jit(solution)/shard_map/pallas_call | solution.py:65
  57.8 6.1 %collective-permute-done.11.refs_3_ = bf16[64,2048]{1,0:T(8,128)(2,1)S(1)} collective-permute-done((bf16[64,2048]{1,0:T(8,128)(2,1)S(1)}, bf16[64,2048]{1,0:T(8,128)(2,1)S(1)}, u32[]{:S(2)}, u32[]{:S(2)}) %collective-permute-start.11) | collective-permute-done | bytes 262176 | tf_op jit(solution)/shard_map/ppermute | solution.py:366
  68.0 11.9 %shard_map.90 = (bf16[16,64,512]{2,1,0:T(8,128)(2,1)}, bf16[1024,384]{1,0:T(8,128)(2,1)}) custom-call(bf16[128,2048]{1,0:T(8,128)(2,1)} %shard_map.85.refs_0_, bf16[128,2048]{1,0:T(8,128)(2,1)} %copy-done.9, bf16[64,2048]{1,0:T(8,128)(2,1)} %copy-done.17, bf16[64,2048]{1,0:T(8,128)(2,1)} %copy-done.16, bf16[128,2048]{1,0:T(8,128)(2,1)} %copy-done.8, ...), custom_call_target="tpu_custom_call" | custom-call | flops 17179869184 | bytes 8388608 | tf_op jit(solution)/shard_map/pallas_call | solution.py:183
  79.9 4.2 %all-to-all-start = ((bf16[16,64,512]{2,1,0:T(8,128)(2,1)}), bf16[16,64,512]{2,1,0:T(8,128)(2,1)S(1)}, u32[]{:S(2)}, u32[]{:S(2)}) async-start(bf16[16,64,512]{2,1,0:T(8,128)(2,1)} %get-tuple-element.46), calls=%async_computation | async-start | bytes 2097152 | tf_op jit(solution)/shard_map/all_to_all | solution.py:396
  88.2 2.2 %collective-permute-done.20 = bf16[128,1024]{1,0:T(8,128)(2,1)S(1)} collective-permute-done((bf16[128,1024]{1,0:T(8,128)(2,1)S(1)}, bf16[128,1024]{1,0:T(8,128)(2,1)S(1)}, u32[]{:S(2)}, u32[]{:S(2)}) %collective-permute-start.20) | collective-permute-done | bytes 262176 | tf_op jit(solution)/shard_map/ppermute | solution.py:370
  90.4 3.6 %collective-permute-start.21 = (bf16[128,1024]{1,0:T(8,128)(2,1)S(1)}, bf16[128,1024]{1,0:T(8,128)(2,1)S(1)}, u32[]{:S(2)}, u32[]{:S(2)}) collective-permute-start(bf16[128,1024]{1,0:T(8,128)(2,1)S(1)} %add_convert_fusion.1), channel_id=1, source_target_pairs={{0,4},{1,5},{2,6},{3,7},{4,0},{5,1},{6,2},{7,3},{8,12},{9,13},{10,... | collective-permute-start | bytes 786440 | tf_op jit(solution)/shard_map/ppermute | solution.py:366
  94.0 5.0 %all-to-all-done.sent = bf16[16,64,512]{2,1,0:T(8,128)(2,1)S(1)} async-done(((bf16[16,64,512]{2,1,0:T(8,128)(2,1)}), bf16[16,64,512]{2,1,0:T(8,128)(2,1)S(1)}, u32[]{:S(2)}, u32[]{:S(2)}) %all-to-all-start) | async-done | bytes 1048608 | tf_op jit(solution)/shard_map/all_to_all | solution.py:396
  99.8 4.6 %collective-permute-start.19 = (bf16[64,128]{1,0:T(8,128)(2,1)S(1)}, bf16[64,128]{1,0:T(8,128)(2,1)S(1)}, u32[]{:S(2)}, u32[]{:S(2)}) collective-permute-start(bf16[64,128]{1,0:T(8,128)(2,1)S(1)} %get-tuple-element.49), channel_id=1, source_target_pairs={{0,0},{1,32},{2,64},{3,96},{4,128},{5,160},{6,192},{7,224},{8,8},{... | collective-permute-start | bytes 49160 | tf_op jit(solution)/shard_map/ppermute | solution.py:380
  104.7 3.6 %collective-permute-start.18 = (bf16[32,384]{1,0:T(8,128)(2,1)S(1)}, bf16[32,384]{1,0:T(8,128)(2,1)S(1)}, u32[]{:S(2)}, u32[]{:S(2)}) collective-permute-start(bf16[32,384]{1,0:T(8,128)(2,1)S(1)} %get-tuple-element.48), channel_id=1, source_target_pairs={{0,128},{8,136},{16,144},{24,152},{32,160},{40,168},{48,176},{56,1... | collective-permute-start | bytes 73736 | tf_op jit(solution)/shard_map/ppermute | solution.py:374
  109.8 2.7 %collective-permute-start.22 = (bf16[128,1024]{1,0:T(8,128)(2,1)S(1)}, bf16[128,1024]{1,0:T(8,128)(2,1)S(1)}, u32[]{:S(2)}, u32[]{:S(2)}) collective-permute-start(bf16[128,1024]{1,0:T(8,128)(2,1)S(1)} %get-tuple-element.53), channel_id=1, source_target_pairs={{0,6},{1,7},{2,0},{3,1},{4,2},{5,3},{6,4},{7,5},{8,14},{9,15},{10,... | collective-permute-start | bytes 786440 | tf_op jit(solution)/shard_map/ppermute | solution.py:366
  112.5 3.6 %collective-permute-start.26 = (bf16[32,640]{1,0:T(8,128)(2,1)S(1)}, bf16[32,640]{1,0:T(8,128)(2,1)S(1)}, u32[]{:S(2)}, u32[]{:S(2)}) collective-permute-start(bf16[32,640]{1,0:T(8,128)(2,1)S(1)} %pad_maximum_fusion.refs_0_), channel_id=1, source_target_pairs={{0,6},{1,7},{2,0},{3,1},{4,2},{5,3},{6,4},{7,5},{8,14},{9,15},{10,... | collective-permute-start | bytes 122888 | tf_op jit(solution)/shard_map/ppermute | solution.py:366
  116.1 2.6 %collective-permute-start.25 = (bf16[32,640]{1,0:T(8,128)(2,1)S(1)}, bf16[32,640]{1,0:T(8,128)(2,1)S(1)}, u32[]{:S(2)}, u32[]{:S(2)}) collective-permute-start(bf16[32,640]{1,0:T(8,128)(2,1)S(1)} %pad_maximum_fusion.refs_0_), channel_id=1, source_target_pairs={{0,4},{1,5},{2,6},{3,7},{4,0},{5,1},{6,2},{7,3},{8,12},{9,13},{10,... | collective-permute-start | bytes 122888 | tf_op jit(solution)/shard_map/ppermute | solution.py:366
  118.7 6.0 %collective-permute-done.26.refs_3_ = bf16[32,640]{1,0:T(8,128)(2,1)S(1)} collective-permute-done((bf16[32,640]{1,0:T(8,128)(2,1)S(1)}, bf16[32,640]{1,0:T(8,128)(2,1)S(1)}, u32[]{:S(2)}, u32[]{:S(2)}) %collective-permute-start.26) | collective-permute-done | bytes 40992 | tf_op jit(solution)/shard_map/ppermute | solution.py:366
  124.7 3.1 %collective-permute-start.27 = (bf16[32,640]{1,0:T(8,128)(2,1)S(1)}, bf16[32,640]{1,0:T(8,128)(2,1)S(1)}, u32[]{:S(2)}, u32[]{:S(2)}) collective-permute-start(bf16[32,640]{1,0:T(8,128)(2,1)S(1)} %pad_maximum_fusion.refs_0_), channel_id=1, source_target_pairs={{0,1},{1,0},{2,3},{3,2},{4,5},{5,4},{6,7},{7,6},{8,9},{9,8},{10,11... | collective-permute-start | bytes 122888 | tf_op jit(solution)/shard_map/ppermute | solution.py:370
  128.6 3.6 %collective-permute-start.29 = (bf16[32,640]{1,0:T(8,128)(2,1)S(1)}, bf16[32,640]{1,0:T(8,128)(2,1)S(1)}, u32[]{:S(2)}, u32[]{:S(2)}) collective-permute-start(bf16[32,640]{1,0:T(8,128)(2,1)S(1)} %collective-permute-done.25.refs_2_), channel_id=1, source_target_pairs={{0,1},{1,0},{2,3},{3,2},{4,5},{5,4},{6,7},{7,6},{8,9},{9,8},{10,11... | collective-permute-start | bytes 122888 | tf_op jit(solution)/shard_map/ppermute | solution.py:370
  (99 shorter events, 29.3 us)
Async XLA Ops:
  2.1 15.6 %collective-permute-start.1 = (bf16[64,128]{1,0:T(8,128)(2,1)}, bf16[64,128]{1,0:T(8,128)(2,1)S(1)}, u32[]{:S(2)}, u32[]{:S(2)}) collective-permute-start(bf16[64,128]{1,0:T(8,128)(2,1)} %get-tuple-element.32), channel_id=1, source_target_pairs={{0,0},{1,32},{2,64},{3,96},{4,128},{5,160},{6,192},{7,224},{8,8},{... | collective-permute-start | bytes 49160 | tf_op jit(solution)/shard_map/ppermute | solution.py:380
  6.6 11.1 %collective-permute-start = (bf16[32,384]{1,0:T(8,128)(2,1)}, bf16[32,384]{1,0:T(8,128)(2,1)S(1)}, u32[]{:S(2)}, u32[]{:S(2)}) collective-permute-start(bf16[32,384]{1,0:T(8,128)(2,1)} %get-tuple-element.31.w_part), channel_id=1, source_target_pairs={{0,128},{8,136},{16,144},{24,152},{32,160},{40,168},{48,176},{56,1... | collective-permute-start | bytes 73736 | tf_op jit(solution)/shard_map/ppermute | solution.py:374
  17.7 30.2 %collective-permute-start.6 = (bf16[128,2048]{1,0:T(8,128)(2,1)}, bf16[128,2048]{1,0:T(8,128)(2,1)S(1)}, u32[]{:S(2)}, u32[]{:S(2)}) collective-permute-start(bf16[128,2048]{1,0:T(8,128)(2,1)} %shard_map.85.refs_0_), channel_id=1, source_target_pairs={{0,6},{1,7},{2,0},{3,1},{4,2},{5,3},{6,4},{7,5},{8,14},{9,15},{10,... | collective-permute-start | bytes 1572872 | tf_op jit(solution)/shard_map/ppermute | solution.py:366
  19.7 28.2 %collective-permute-start.5 = (bf16[128,2048]{1,0:T(8,128)(2,1)}, bf16[128,2048]{1,0:T(8,128)(2,1)S(1)}, u32[]{:S(2)}, u32[]{:S(2)}) collective-permute-start(bf16[128,2048]{1,0:T(8,128)(2,1)} %shard_map.85.refs_0_), channel_id=1, source_target_pairs={{0,2},{1,3},{2,4},{3,5},{4,6},{5,7},{6,0},{7,1},{8,10},{9,11},{10,... | collective-permute-start | bytes 1572872 | tf_op jit(solution)/shard_map/ppermute | solution.py:366
  24.3 4.9 %collective-permute-start.3 = (bf16[64,512]{1,0:T(8,128)(2,1)S(1)}, bf16[64,512]{1,0:T(8,128)(2,1)S(1)}, u32[]{:S(2)}, u32[]{:S(2)}) collective-permute-start(bf16[64,512]{1,0:T(8,128)(2,1)S(1)} %shard_map.87.refs_0_), channel_id=1, source_target_pairs={{0,16},{8,24},{16,0},{24,8},{32,48},{40,56},{48,32},{56,40},{64,80... | collective-permute-start | bytes 196616 | tf_op jit(solution)/shard_map/ppermute | solution.py:391
  24.6 5.3 %collective-permute-start.2 = (bf16[64,512]{1,0:T(8,128)(2,1)S(1)}, bf16[64,512]{1,0:T(8,128)(2,1)S(1)}, u32[]{:S(2)}, u32[]{:S(2)}) collective-permute-start(bf16[64,512]{1,0:T(8,128)(2,1)S(1)} %shard_map.87.refs_0_), channel_id=1, source_target_pairs={{0,8},{8,16},{16,24},{24,0},{32,40},{40,48},{48,56},{56,32},{64,72... | collective-permute-start | bytes 196616 | tf_op jit(solution)/shard_map/ppermute | solution.py:391
  30.5 9.8 %collective-permute-start.9 = (bf16[4,64,512]{2,1,0:T(8,128)(2,1)S(1)}, bf16[4,64,512]{2,1,0:T(8,128)(2,1)S(1)}, u32[]{:S(2)}, u32[]{:S(2)}) collective-permute-start(bf16[4,64,512]{2,1,0:T(8,128)(2,1)S(1)} %shard_map.88.refs_6_), channel_id=1, source_target_pairs={{0,96},{8,104},{16,112},{24,120},{32,0},{40,8},{48,16},{56,24},{64... | collective-permute-start | bytes 786440 | tf_op jit(solution)/shard_map/ppermute | solution.py:391
  33.2 12.1 %collective-permute-start.8 = (bf16[4,64,512]{2,1,0:T(8,128)(2,1)S(1)}, bf16[4,64,512]{2,1,0:T(8,128)(2,1)S(1)}, u32[]{:S(2)}, u32[]{:S(2)}) collective-permute-start(bf16[4,64,512]{2,1,0:T(8,128)(2,1)S(1)} %shard_map.88.refs_6_), channel_id=1, source_target_pairs={{0,64},{8,72},{16,80},{24,88},{32,96},{40,104},{48,112},{56,120},{... | collective-permute-start | bytes 786440 | tf_op jit(solution)/shard_map/ppermute | solution.py:391
  33.2 14.7 %collective-permute-start.7 = (bf16[4,64,512]{2,1,0:T(8,128)(2,1)S(1)}, bf16[4,64,512]{2,1,0:T(8,128)(2,1)S(1)}, u32[]{:S(2)}, u32[]{:S(2)}) collective-permute-start(bf16[4,64,512]{2,1,0:T(8,128)(2,1)S(1)} %shard_map.88.refs_6_), channel_id=1, source_target_pairs={{0,32},{8,40},{16,48},{24,56},{32,64},{40,72},{48,80},{56,88},{64,... | collective-permute-start | bytes 786440 | tf_op jit(solution)/shard_map/ppermute | solution.py:391
  40.2 11.3 %collective-permute-start.12 = (bf16[128,2048]{1,0:T(8,128)(2,1)}, bf16[128,2048]{1,0:T(8,128)(2,1)S(1)}, u32[]{:S(2)}, u32[]{:S(2)}) collective-permute-start(bf16[128,2048]{1,0:T(8,128)(2,1)} %shard_map.85.refs_0_), channel_id=1, source_target_pairs={{0,1},{1,0},{2,3},{3,2},{4,5},{5,4},{6,7},{7,6},{8,9},{9,8},{10,11... | collective-permute-start | bytes 1572872 | tf_op jit(solution)/shard_map/ppermute | solution.py:370
  49.0 14.8 %collective-permute-start.11 = (bf16[64,2048]{1,0:T(8,128)(2,1)S(1)}, bf16[64,2048]{1,0:T(8,128)(2,1)S(1)}, u32[]{:S(2)}, u32[]{:S(2)}) collective-permute-start(bf16[64,2048]{1,0:T(8,128)(2,1)S(1)} %slice.22), channel_id=1, source_target_pairs={{0,6},{1,7},{2,0},{3,1},{4,2},{5,3},{6,4},{7,5},{8,14},{9,15},{10,... | collective-permute-start | bytes 786440 | tf_op jit(solution)/shard_map/ppermute | solution.py:366
  50.5 13.7 %collective-permute-start.10 = (bf16[64,2048]{1,0:T(8,128)(2,1)S(1)}, bf16[64,2048]{1,0:T(8,128)(2,1)S(1)}, u32[]{:S(2)}, u32[]{:S(2)}) collective-permute-start(bf16[64,2048]{1,0:T(8,128)(2,1)S(1)} %slice.21), channel_id=1, source_target_pairs={{0,2},{1,3},{2,4},{3,5},{4,6},{5,7},{6,0},{7,1},{8,10},{9,11},{10,... | collective-permute-start | bytes 786440 | tf_op jit(solution)/shard_map/ppermute | solution.py:366
  79.9 19.2 %all-to-all-start = ((bf16[16,64,512]{2,1,0:T(8,128)(2,1)}), bf16[16,64,512]{2,1,0:T(8,128)(2,1)S(1)}, u32[]{:S(2)}, u32[]{:S(2)}) async-start(bf16[16,64,512]{2,1,0:T(8,128)(2,1)} %get-tuple-element.46), calls=%async_computation | async-start | bytes 2097152 | tf_op jit(solution)/shard_map/all_to_all | solution.py:396
  87.3 17.1 %collective-permute-start.17 = (bf16[384,1024]{1,0:T(8,128)(2,1)}, bf16[384,1024]{1,0:T(8,128)(2,1)S(1)}, u32[]{:S(2)}, u32[]{:S(2)}) collective-permute-start(bf16[384,1024]{1,0:T(8,128)(2,1)} %get-tuple-element.44), channel_id=1, source_target_pairs={{0,1},{1,0},{2,3},{3,2},{4,5},{5,4},{6,7},{7,6},{8,9},{9,8},{10,11... | collective-permute-start | bytes 2359304 | tf_op jit(solution)/shard_map/ppermute | solution.py:370
  90.4 19.4 %collective-permute-start.21 = (bf16[128,1024]{1,0:T(8,128)(2,1)S(1)}, bf16[128,1024]{1,0:T(8,128)(2,1)S(1)}, u32[]{:S(2)}, u32[]{:S(2)}) collective-permute-start(bf16[128,1024]{1,0:T(8,128)(2,1)S(1)} %add_convert_fusion.1), channel_id=1, source_target_pairs={{0,4},{1,5},{2,6},{3,7},{4,0},{5,1},{6,2},{7,3},{8,12},{9,13},{10,... | collective-permute-start | bytes 786440 | tf_op jit(solution)/shard_map/ppermute | solution.py:366
  99.8 8.6 %collective-permute-start.19 = (bf16[64,128]{1,0:T(8,128)(2,1)S(1)}, bf16[64,128]{1,0:T(8,128)(2,1)S(1)}, u32[]{:S(2)}, u32[]{:S(2)}) collective-permute-start(bf16[64,128]{1,0:T(8,128)(2,1)S(1)} %get-tuple-element.49), channel_id=1, source_target_pairs={{0,0},{1,32},{2,64},{3,96},{4,128},{5,160},{6,192},{7,224},{8,8},{... | collective-permute-start | bytes 49160 | tf_op jit(solution)/shard_map/ppermute | solution.py:380
  104.7 5.0 %collective-permute-start.18 = (bf16[32,384]{1,0:T(8,128)(2,1)S(1)}, bf16[32,384]{1,0:T(8,128)(2,1)S(1)}, u32[]{:S(2)}, u32[]{:S(2)}) collective-permute-start(bf16[32,384]{1,0:T(8,128)(2,1)S(1)} %get-tuple-element.48), channel_id=1, source_target_pairs={{0,128},{8,136},{16,144},{24,152},{32,160},{40,168},{48,176},{56,1... | collective-permute-start | bytes 73736 | tf_op jit(solution)/shard_map/ppermute | solution.py:374
  109.8 22.4 %collective-permute-start.22 = (bf16[128,1024]{1,0:T(8,128)(2,1)S(1)}, bf16[128,1024]{1,0:T(8,128)(2,1)S(1)}, u32[]{:S(2)}, u32[]{:S(2)}) collective-permute-start(bf16[128,1024]{1,0:T(8,128)(2,1)S(1)} %get-tuple-element.53), channel_id=1, source_target_pairs={{0,6},{1,7},{2,0},{3,1},{4,2},{5,3},{6,4},{7,5},{8,14},{9,15},{10,... | collective-permute-start | bytes 786440 | tf_op jit(solution)/shard_map/ppermute | solution.py:366
  112.5 19.7 %collective-permute-start.23 = (bf16[128,1024]{1,0:T(8,128)(2,1)S(1)}, bf16[128,1024]{1,0:T(8,128)(2,1)S(1)}, u32[]{:S(2)}, u32[]{:S(2)}) collective-permute-start(bf16[128,1024]{1,0:T(8,128)(2,1)S(1)} %get-tuple-element.55), channel_id=1, source_target_pairs={{0,2},{1,3},{2,4},{3,5},{4,6},{5,7},{6,0},{7,1},{8,10},{9,11},{10,... | collective-permute-start | bytes 786440 | tf_op jit(solution)/shard_map/ppermute | solution.py:366
  112.5 12.2 %collective-permute-start.26 = (bf16[32,640]{1,0:T(8,128)(2,1)S(1)}, bf16[32,640]{1,0:T(8,128)(2,1)S(1)}, u32[]{:S(2)}, u32[]{:S(2)}) collective-permute-start(bf16[32,640]{1,0:T(8,128)(2,1)S(1)} %pad_maximum_fusion.refs_0_), channel_id=1, source_target_pairs={{0,6},{1,7},{2,0},{3,1},{4,2},{5,3},{6,4},{7,5},{8,14},{9,15},{10,... | collective-permute-start | bytes 122888 | tf_op jit(solution)/shard_map/ppermute | solution.py:366
  116.1 11.7 %collective-permute-start.25 = (bf16[32,640]{1,0:T(8,128)(2,1)S(1)}, bf16[32,640]{1,0:T(8,128)(2,1)S(1)}, u32[]{:S(2)}, u32[]{:S(2)}) collective-permute-start(bf16[32,640]{1,0:T(8,128)(2,1)S(1)} %pad_maximum_fusion.refs_0_), channel_id=1, source_target_pairs={{0,4},{1,5},{2,6},{3,7},{4,0},{5,1},{6,2},{7,3},{8,12},{9,13},{10,... | collective-permute-start | bytes 122888 | tf_op jit(solution)/shard_map/ppermute | solution.py:366
  118.7 9.9 %collective-permute-start.24 = (bf16[32,640]{1,0:T(8,128)(2,1)S(1)}, bf16[32,640]{1,0:T(8,128)(2,1)S(1)}, u32[]{:S(2)}, u32[]{:S(2)}) collective-permute-start(bf16[32,640]{1,0:T(8,128)(2,1)S(1)} %pad_maximum_fusion.refs_0_), channel_id=1, source_target_pairs={{0,2},{1,3},{2,4},{3,5},{4,6},{5,7},{6,0},{7,1},{8,10},{9,11},{10,... | collective-permute-start | bytes 122888 | tf_op jit(solution)/shard_map/ppermute | solution.py:366
  124.7 8.8 %collective-permute-start.27 = (bf16[32,640]{1,0:T(8,128)(2,1)S(1)}, bf16[32,640]{1,0:T(8,128)(2,1)S(1)}, u32[]{:S(2)}, u32[]{:S(2)}) collective-permute-start(bf16[32,640]{1,0:T(8,128)(2,1)S(1)} %pad_maximum_fusion.refs_0_), channel_id=1, source_target_pairs={{0,1},{1,0},{2,3},{3,2},{4,5},{5,4},{6,7},{7,6},{8,9},{9,8},{10,11... | collective-permute-start | bytes 122888 | tf_op jit(solution)/shard_map/ppermute | solution.py:370
  127.8 5.7 %collective-permute-start.30 = (bf16[32,640]{1,0:T(8,128)(2,1)S(1)}, bf16[32,640]{1,0:T(8,128)(2,1)S(1)}, u32[]{:S(2)}, u32[]{:S(2)}) collective-permute-start(bf16[32,640]{1,0:T(8,128)(2,1)S(1)} %collective-permute-done.26.refs_3_), channel_id=1, source_target_pairs={{0,1},{1,0},{2,3},{3,2},{4,5},{5,4},{6,7},{7,6},{8,9},{9,8},{10,11... | collective-permute-start | bytes 122888 | tf_op jit(solution)/shard_map/ppermute | solution.py:370
  (28 other events, 235.2 us)

commit v8 on v7

--- a/solution.py
+++ b/solution.py
@@ -173,7 +173,7 @@
             struct((3 * CELLS, C)),
             *[struct((CELLS, C))] * Z,
         ),
-        compiler_params=pltpu.CompilerParams(vmem_limit_bytes=16 * 2**20),
+        compiler_params=pltpu.CompilerParams(vmem_limit_bytes=8 * 2**20),
         cost_estimate=pl.CostEstimate(flops=2**34, bytes_accessed=2**23, transcendentals=0),
     )(dqkv, wq)
 

time: 135 us -> 135 us (level)
  no operation moved by 1% of the time
where the time goes in v8:
time: 135 us
  starting transfers between devices  64.6 us (48%)
  waiting for transfers between devices  36.1 us (27%)
  Pallas kernels  26.4 us (20%)
  local copies, waits for them, and re-layouts  5.73 us (4%)
  between operations  1.59 us (1%)
    ppermute x10, starting transfers between devices, turn(): return lax.ppermute(x, 'space', pairs)  17.3 us
    ppermute x11, starting transfers between devices, swap(): return lax.ppermute(x, 'space', [(i, i ^ 1) for i in range(2 * Z)])  16.1 us
    ppermute x6, waiting for transfers between devices, turn_dp(): return lax.ppermute(x, 'dp', pairs)  13.5 us
    ppermute x10, waiting for transfers between devices, turn(): return lax.ppermute(x, 'space', pairs)  12.4 us
    pallas_call x1, Pallas kernels, attention(): pl.pallas_call(attention_kernel, in_specs=[FAR] * (PIECES + 3), out_specs...  11.9 us
    ppermute x2, starting transfers between devices, swap_lo(): return lax.ppermute(x, 'dp', [(i, i ^ XY) for i in range(2 * XY)])  10.6 us
    ppermute x2, starting transfers between devices, transpose_devices(): return lax.ppermute(x, ('dp', 'space'), pairs)  9.11 us
    ppermute x6, starting transfers between devices, turn_dp(): return lax.ppermute(x, 'dp', pairs)  7.29 us
  transfers between devices with their start and end apart: 32, of which 13 were waited for; matrix products, arithmetic and copies ran while one was open for 1% of the time, Pallas kernels for 9%

profile of v8, /device:TPU:1, one launch (start us, length us, event | category | flops | bytes accessed | tf_op | source)
XLA Modules:
  0.0 134.9 jit_solution(5174582504006665204)
XLA Ops:
  2.1 4.5 %collective-permute-start.1 = (bf16[64,128]{1,0:T(8,128)(2,1)}, bf16[64,128]{1,0:T(8,128)(2,1)S(1)}, u32[]{:S(2)}, u32[]{:S(2)}) collective-permute-start(bf16[64,128]{1,0:T(8,128)(2,1)} %get-tuple-element.32), channel_id=1, source_target_pairs={{0,0},{1,32},{2,64},{3,96},{4,128},{5,160},{6,192},{7,224},{8,8},{... | collective-permute-start | bytes 49160 | tf_op jit(solution)/shard_map/ppermute | solution.py:380
  6.6 7.0 %collective-permute-start = (bf16[32,384]{1,0:T(8,128)(2,1)}, bf16[32,384]{1,0:T(8,128)(2,1)S(1)}, u32[]{:S(2)}, u32[]{:S(2)}) collective-permute-start(bf16[32,384]{1,0:T(8,128)(2,1)} %get-tuple-element.31.w_part), channel_id=1, source_target_pairs={{0,128},{8,136},{16,144},{24,152},{32,160},{40,168},{48,176},{56,1... | collective-permute-start | bytes 73736 | tf_op jit(solution)/shard_map/ppermute | solution.py:374
  15.6 2.1 %shard_map.85.refs_0_ = bf16[128,2048]{1,0:T(8,128)(2,1)} custom-call(bf16[128,1024]{1,0:T(8,128)(2,1)} %bitcast.11, bf16[128,1024]{1,0:T(8,128)(2,1)} %bitcast.13, bf16[1,2048]{1,0:T(2,128)(2,1)} %constant_dynamic-slice_fusion.row), custom_call_target="tpu_custom_call" | custom-call | tf_op jit(solution)/shard_map/pallas_call | solution.py:220
  21.4 2.8 %collective-permute-start.4 = (bf16[64,512]{1,0:T(8,128)(2,1)S(1)}, bf16[64,512]{1,0:T(8,128)(2,1)S(1)}, u32[]{:S(2)}, u32[]{:S(2)}) collective-permute-start(bf16[64,512]{1,0:T(8,128)(2,1)S(1)} %shard_map.87.refs_0_), channel_id=1, source_target_pairs={{0,24},{8,0},{16,8},{24,16},{32,56},{40,32},{48,40},{56,48},{64,88... | collective-permute-start | bytes 196616 | tf_op jit(solution)/shard_map/ppermute | solution.py:391
  25.6 3.6 %collective-permute-done.3.refs_2_ = bf16[64,512]{1,0:T(8,128)(2,1)S(1)} collective-permute-done((bf16[64,512]{1,0:T(8,128)(2,1)S(1)}, bf16[64,512]{1,0:T(8,128)(2,1)S(1)}, u32[]{:S(2)}, u32[]{:S(2)}) %collective-permute-start.3) | collective-permute-done | bytes 65568 | tf_op jit(solution)/shard_map/ppermute | solution.py:391
  30.5 2.8 %collective-permute-start.9 = (bf16[4,64,512]{2,1,0:T(8,128)(2,1)S(1)}, bf16[4,64,512]{2,1,0:T(8,128)(2,1)S(1)}, u32[]{:S(2)}, u32[]{:S(2)}) collective-permute-start(bf16[4,64,512]{2,1,0:T(8,128)(2,1)S(1)} %shard_map.88.refs_6_), channel_id=1, source_target_pairs={{0,96},{8,104},{16,112},{24,120},{32,0},{40,8},{48,16},{56,24},{64... | collective-permute-start | bytes 786440 | tf_op jit(solution)/shard_map/ppermute | solution.py:391
  33.9 6.3 %collective-permute-done.9.refs_9_ = bf16[4,64,512]{2,1,0:T(8,128)(2,1)S(1)} collective-permute-done((bf16[4,64,512]{2,1,0:T(8,128)(2,1)S(1)}, bf16[4,64,512]{2,1,0:T(8,128)(2,1)S(1)}, u32[]{:S(2)}, u32[]{:S(2)}) %collective-permute-start.9) | collective-permute-done | bytes 262176 | tf_op jit(solution)/shard_map/ppermute | solution.py:391
  40.2 5.1 %collective-permute-start.12 = (bf16[128,2048]{1,0:T(8,128)(2,1)}, bf16[128,2048]{1,0:T(8,128)(2,1)S(1)}, u32[]{:S(2)}, u32[]{:S(2)}) collective-permute-start(bf16[128,2048]{1,0:T(8,128)(2,1)} %shard_map.85.refs_0_), channel_id=1, source_target_pairs={{0,1},{1,0},{2,3},{3,2},{4,5},{5,4},{6,7},{7,6},{8,9},{9,8},{10,11... | collective-permute-start | bytes 1572872 | tf_op jit(solution)/shard_map/ppermute | solution.py:370
  45.4 2.6 %collective-permute-done.7.refs_7_ = bf16[4,64,512]{2,1,0:T(8,128)(2,1)S(1)} collective-permute-done((bf16[4,64,512]{2,1,0:T(8,128)(2,1)S(1)}, bf16[4,64,512]{2,1,0:T(8,128)(2,1)S(1)}, u32[]{:S(2)}, u32[]{:S(2)}) %collective-permute-start.7) | collective-permute-done | bytes 262176 | tf_op jit(solution)/shard_map/ppermute | solution.py:391
  53.3 4.5 %shard_map.89 = (bf16[768,512]{1,0:T(8,128)(2,1)}, bf16[1024,384]{1,0:T(8,128)(2,1)}, bf16[128,1024]{1,0:T(8,128)(2,1)}) custom-call(s32[4]{0:T(128)} %copy-done.4, bf16[128,2048]{1,0:T(8,128)(2,1)} %shard_map.85.refs_0_, bf16[128,2048]{1,0:T(8,128)(2,1)} %copy-done.9, bf16[128,2048]{1,0:T(8,128)(2,1)} %copy-done.8, bf16[128,2048]{1,0:T(8,128)(2,1)} %copy-done.10, ...), custom_call_target="tpu_custom_call" | custom-call | tf_op jit(solution)/shard_map/pallas_call | solution.py:65
  57.8 6.1 %collective-permute-done.11.refs_3_ = bf16[64,2048]{1,0:T(8,128)(2,1)S(1)} collective-permute-done((bf16[64,2048]{1,0:T(8,128)(2,1)S(1)}, bf16[64,2048]{1,0:T(8,128)(2,1)S(1)}, u32[]{:S(2)}, u32[]{:S(2)}) %collective-permute-start.11) | collective-permute-done | bytes 262176 | tf_op jit(solution)/shard_map/ppermute | solution.py:366
  68.0 11.9 %shard_map.90 = (bf16[16,64,512]{2,1,0:T(8,128)(2,1)}, bf16[1024,384]{1,0:T(8,128)(2,1)}) custom-call(bf16[128,2048]{1,0:T(8,128)(2,1)} %shard_map.85.refs_0_, bf16[128,2048]{1,0:T(8,128)(2,1)} %copy-done.9, bf16[64,2048]{1,0:T(8,128)(2,1)} %copy-done.17, bf16[64,2048]{1,0:T(8,128)(2,1)} %copy-done.16, bf16[128,2048]{1,0:T(8,128)(2,1)} %copy-done.8, ...), custom_call_target="tpu_custom_call" | custom-call | flops 17179869184 | bytes 8388608 | tf_op jit(solution)/shard_map/pallas_call | solution.py:183
  79.9 4.2 %all-to-all-start = ((bf16[16,64,512]{2,1,0:T(8,128)(2,1)}), bf16[16,64,512]{2,1,0:T(8,128)(2,1)S(1)}, u32[]{:S(2)}, u32[]{:S(2)}) async-start(bf16[16,64,512]{2,1,0:T(8,128)(2,1)} %get-tuple-element.46), calls=%async_computation | async-start | bytes 2097152 | tf_op jit(solution)/shard_map/all_to_all | solution.py:396
  88.2 2.2 %collective-permute-done.20 = bf16[128,1024]{1,0:T(8,128)(2,1)S(1)} collective-permute-done((bf16[128,1024]{1,0:T(8,128)(2,1)S(1)}, bf16[128,1024]{1,0:T(8,128)(2,1)S(1)}, u32[]{:S(2)}, u32[]{:S(2)}) %collective-permute-start.20) | collective-permute-done | bytes 262176 | tf_op jit(solution)/shard_map/ppermute | solution.py:370
  90.4 3.6 %collective-permute-start.21 = (bf16[128,1024]{1,0:T(8,128)(2,1)S(1)}, bf16[128,1024]{1,0:T(8,128)(2,1)S(1)}, u32[]{:S(2)}, u32[]{:S(2)}) collective-permute-start(bf16[128,1024]{1,0:T(8,128)(2,1)S(1)} %add_convert_fusion.1), channel_id=1, source_target_pairs={{0,4},{1,5},{2,6},{3,7},{4,0},{5,1},{6,2},{7,3},{8,12},{9,13},{10,... | collective-permute-start | bytes 786440 | tf_op jit(solution)/shard_map/ppermute | solution.py:366
  94.0 5.0 %all-to-all-done.sent = bf16[16,64,512]{2,1,0:T(8,128)(2,1)S(1)} async-done(((bf16[16,64,512]{2,1,0:T(8,128)(2,1)}), bf16[16,64,512]{2,1,0:T(8,128)(2,1)S(1)}, u32[]{:S(2)}, u32[]{:S(2)}) %all-to-all-start) | async-done | bytes 1048608 | tf_op jit(solution)/shard_map/all_to_all | solution.py:396
  99.8 4.6 %collective-permute-start.19 = (bf16[64,128]{1,0:T(8,128)(2,1)S(1)}, bf16[64,128]{1,0:T(8,128)(2,1)S(1)}, u32[]{:S(2)}, u32[]{:S(2)}) collective-permute-start(bf16[64,128]{1,0:T(8,128)(2,1)S(1)} %get-tuple-element.49), channel_id=1, source_target_pairs={{0,0},{1,32},{2,64},{3,96},{4,128},{5,160},{6,192},{7,224},{8,8},{... | collective-permute-start | bytes 49160 | tf_op jit(solution)/shard_map/ppermute | solution.py:380
  104.7 3.6 %collective-permute-start.18 = (bf16[32,384]{1,0:T(8,128)(2,1)S(1)}, bf16[32,384]{1,0:T(8,128)(2,1)S(1)}, u32[]{:S(2)}, u32[]{:S(2)}) collective-permute-start(bf16[32,384]{1,0:T(8,128)(2,1)S(1)} %get-tuple-element.48), channel_id=1, source_target_pairs={{0,128},{8,136},{16,144},{24,152},{32,160},{40,168},{48,176},{56,1... | collective-permute-start | bytes 73736 | tf_op jit(solution)/shard_map/ppermute | solution.py:374
  109.8 2.7 %collective-permute-start.22 = (bf16[128,1024]{1,0:T(8,128)(2,1)S(1)}, bf16[128,1024]{1,0:T(8,128)(2,1)S(1)}, u32[]{:S(2)}, u32[]{:S(2)}) collective-permute-start(bf16[128,1024]{1,0:T(8,128)(2,1)S(1)} %get-tuple-element.53), channel_id=1, source_target_pairs={{0,6},{1,7},{2,0},{3,1},{4,2},{5,3},{6,4},{7,5},{8,14},{9,15},{10,... | collective-permute-start | bytes 786440 | tf_op jit(solution)/shard_map/ppermute | solution.py:366
  112.5 3.6 %collective-permute-start.26 = (bf16[32,640]{1,0:T(8,128)(2,1)S(1)}, bf16[32,640]{1,0:T(8,128)(2,1)S(1)}, u32[]{:S(2)}, u32[]{:S(2)}) collective-permute-start(bf16[32,640]{1,0:T(8,128)(2,1)S(1)} %pad_maximum_fusion.refs_0_), channel_id=1, source_target_pairs={{0,6},{1,7},{2,0},{3,1},{4,2},{5,3},{6,4},{7,5},{8,14},{9,15},{10,... | collective-permute-start | bytes 122888 | tf_op jit(solution)/shard_map/ppermute | solution.py:366
  116.1 2.6 %collective-permute-start.25 = (bf16[32,640]{1,0:T(8,128)(2,1)S(1)}, bf16[32,640]{1,0:T(8,128)(2,1)S(1)}, u32[]{:S(2)}, u32[]{:S(2)}) collective-permute-start(bf16[32,640]{1,0:T(8,128)(2,1)S(1)} %pad_maximum_fusion.refs_0_), channel_id=1, source_target_pairs={{0,4},{1,5},{2,6},{3,7},{4,0},{5,1},{6,2},{7,3},{8,12},{9,13},{10,... | collective-permute-start | bytes 122888 | tf_op jit(solution)/shard_map/ppermute | solution.py:366
  118.7 6.0 %collective-permute-done.26.refs_3_ = bf16[32,640]{1,0:T(8,128)(2,1)S(1)} collective-permute-done((bf16[32,640]{1,0:T(8,128)(2,1)S(1)}, bf16[32,640]{1,0:T(8,128)(2,1)S(1)}, u32[]{:S(2)}, u32[]{:S(2)}) %collective-permute-start.26) | collective-permute-done | bytes 40992 | tf_op jit(solution)/shard_map/ppermute | solution.py:366
  124.7 3.1 %collective-permute-start.27 = (bf16[32,640]{1,0:T(8,128)(2,1)S(1)}, bf16[32,640]{1,0:T(8,128)(2,1)S(1)}, u32[]{:S(2)}, u32[]{:S(2)}) collective-permute-start(bf16[32,640]{1,0:T(8,128)(2,1)S(1)} %pad_maximum_fusion.refs_0_), channel_id=1, source_target_pairs={{0,1},{1,0},{2,3},{3,2},{4,5},{5,4},{6,7},{7,6},{8,9},{9,8},{10,11... | collective-permute-start | bytes 122888 | tf_op jit(solution)/shard_map/ppermute | solution.py:370
  128.6 3.6 %collective-permute-start.29 = (bf16[32,640]{1,0:T(8,128)(2,1)S(1)}, bf16[32,640]{1,0:T(8,128)(2,1)S(1)}, u32[]{:S(2)}, u32[]{:S(2)}) collective-permute-start(bf16[32,640]{1,0:T(8,128)(2,1)S(1)} %collective-permute-done.25.refs_2_), channel_id=1, source_target_pairs={{0,1},{1,0},{2,3},{3,2},{4,5},{5,4},{6,7},{7,6},{8,9},{9,8},{10,11... | collective-permute-start | bytes 122888 | tf_op jit(solution)/shard_map/ppermute | solution.py:370
  (99 shorter events, 29.3 us)
Async XLA Ops:
  2.1 15.6 %collective-permute-start.1 = (bf16[64,128]{1,0:T(8,128)(2,1)}, bf16[64,128]{1,0:T(8,128)(2,1)S(1)}, u32[]{:S(2)}, u32[]{:S(2)}) collective-permute-start(bf16[64,128]{1,0:T(8,128)(2,1)} %get-tuple-element.32), channel_id=1, source_target_pairs={{0,0},{1,32},{2,64},{3,96},{4,128},{5,160},{6,192},{7,224},{8,8},{... | collective-permute-start | bytes 49160 | tf_op jit(solution)/shard_map/ppermute | solution.py:380
  6.6 11.1 %collective-permute-start = (bf16[32,384]{1,0:T(8,128)(2,1)}, bf16[32,384]{1,0:T(8,128)(2,1)S(1)}, u32[]{:S(2)}, u32[]{:S(2)}) collective-permute-start(bf16[32,384]{1,0:T(8,128)(2,1)} %get-tuple-element.31.w_part), channel_id=1, source_target_pairs={{0,128},{8,136},{16,144},{24,152},{32,160},{40,168},{48,176},{56,1... | collective-permute-start | bytes 73736 | tf_op jit(solution)/shard_map/ppermute | solution.py:374
  17.7 30.2 %collective-permute-start.6 = (bf16[128,2048]{1,0:T(8,128)(2,1)}, bf16[128,2048]{1,0:T(8,128)(2,1)S(1)}, u32[]{:S(2)}, u32[]{:S(2)}) collective-permute-start(bf16[128,2048]{1,0:T(8,128)(2,1)} %shard_map.85.refs_0_), channel_id=1, source_target_pairs={{0,6},{1,7},{2,0},{3,1},{4,2},{5,3},{6,4},{7,5},{8,14},{9,15},{10,... | collective-permute-start | bytes 1572872 | tf_op jit(solution)/shard_map/ppermute | solution.py:366
  19.7 28.2 %collective-permute-start.5 = (bf16[128,2048]{1,0:T(8,128)(2,1)}, bf16[128,2048]{1,0:T(8,128)(2,1)S(1)}, u32[]{:S(2)}, u32[]{:S(2)}) collective-permute-start(bf16[128,2048]{1,0:T(8,128)(2,1)} %shard_map.85.refs_0_), channel_id=1, source_target_pairs={{0,2},{1,3},{2,4},{3,5},{4,6},{5,7},{6,0},{7,1},{8,10},{9,11},{10,... | collective-permute-start | bytes 1572872 | tf_op jit(solution)/shard_map/ppermute | solution.py:366
  24.3 4.9 %collective-permute-start.3 = (bf16[64,512]{1,0:T(8,128)(2,1)S(1)}, bf16[64,512]{1,0:T(8,128)(2,1)S(1)}, u32[]{:S(2)}, u32[]{:S(2)}) collective-permute-start(bf16[64,512]{1,0:T(8,128)(2,1)S(1)} %shard_map.87.refs_0_), channel_id=1, source_target_pairs={{0,16},{8,24},{16,0},{24,8},{32,48},{40,56},{48,32},{56,40},{64,80... | collective-permute-start | bytes 196616 | tf_op jit(solution)/shard_map/ppermute | solution.py:391
  24.6 5.3 %collective-permute-start.2 = (bf16[64,512]{1,0:T(8,128)(2,1)S(1)}, bf16[64,512]{1,0:T(8,128)(2,1)S(1)}, u32[]{:S(2)}, u32[]{:S(2)}) collective-permute-start(bf16[64,512]{1,0:T(8,128)(2,1)S(1)} %shard_map.87.refs_0_), channel_id=1, source_target_pairs={{0,8},{8,16},{16,24},{24,0},{32,40},{40,48},{48,56},{56,32},{64,72... | collective-permute-start | bytes 196616 | tf_op jit(solution)/shard_map/ppermute | solution.py:391
  30.5 9.8 %collective-permute-start.9 = (bf16[4,64,512]{2,1,0:T(8,128)(2,1)S(1)}, bf16[4,64,512]{2,1,0:T(8,128)(2,1)S(1)}, u32[]{:S(2)}, u32[]{:S(2)}) collective-permute-start(bf16[4,64,512]{2,1,0:T(8,128)(2,1)S(1)} %shard_map.88.refs_6_), channel_id=1, source_target_pairs={{0,96},{8,104},{16,112},{24,120},{32,0},{40,8},{48,16},{56,24},{64... | collective-permute-start | bytes 786440 | tf_op jit(solution)/shard_map/ppermute | solution.py:391
  33.2 12.1 %collective-permute-start.8 = (bf16[4,64,512]{2,1,0:T(8,128)(2,1)S(1)}, bf16[4,64,512]{2,1,0:T(8,128)(2,1)S(1)}, u32[]{:S(2)}, u32[]{:S(2)}) collective-permute-start(bf16[4,64,512]{2,1,0:T(8,128)(2,1)S(1)} %shard_map.88.refs_6_), channel_id=1, source_target_pairs={{0,64},{8,72},{16,80},{24,88},{32,96},{40,104},{48,112},{56,120},{... | collective-permute-start | bytes 786440 | tf_op jit(solution)/shard_map/ppermute | solution.py:391
  33.2 14.7 %collective-permute-start.7 = (bf16[4,64,512]{2,1,0:T(8,128)(2,1)S(1)}, bf16[4,64,512]{2,1,0:T(8,128)(2,1)S(1)}, u32[]{:S(2)}, u32[]{:S(2)}) collective-permute-start(bf16[4,64,512]{2,1,0:T(8,128)(2,1)S(1)} %shard_map.88.refs_6_), channel_id=1, source_target_pairs={{0,32},{8,40},{16,48},{24,56},{32,64},{40,72},{48,80},{56,88},{64,... | collective-permute-start | bytes 786440 | tf_op jit(solution)/shard_map/ppermute | solution.py:391
  40.2 11.3 %collective-permute-start.12 = (bf16[128,2048]{1,0:T(8,128)(2,1)}, bf16[128,2048]{1,0:T(8,128)(2,1)S(1)}, u32[]{:S(2)}, u32[]{:S(2)}) collective-permute-start(bf16[128,2048]{1,0:T(8,128)(2,1)} %shard_map.85.refs_0_), channel_id=1, source_target_pairs={{0,1},{1,0},{2,3},{3,2},{4,5},{5,4},{6,7},{7,6},{8,9},{9,8},{10,11... | collective-permute-start | bytes 1572872 | tf_op jit(solution)/shard_map/ppermute | solution.py:370
  49.0 14.8 %collective-permute-start.11 = (bf16[64,2048]{1,0:T(8,128)(2,1)S(1)}, bf16[64,2048]{1,0:T(8,128)(2,1)S(1)}, u32[]{:S(2)}, u32[]{:S(2)}) collective-permute-start(bf16[64,2048]{1,0:T(8,128)(2,1)S(1)} %slice.22), channel_id=1, source_target_pairs={{0,6},{1,7},{2,0},{3,1},{4,2},{5,3},{6,4},{7,5},{8,14},{9,15},{10,... | collective-permute-start | bytes 786440 | tf_op jit(solution)/shard_map/ppermute | solution.py:366
  50.5 13.7 %collective-permute-start.10 = (bf16[64,2048]{1,0:T(8,128)(2,1)S(1)}, bf16[64,2048]{1,0:T(8,128)(2,1)S(1)}, u32[]{:S(2)}, u32[]{:S(2)}) collective-permute-start(bf16[64,2048]{1,0:T(8,128)(2,1)S(1)} %slice.21), channel_id=1, source_target_pairs={{0,2},{1,3},{2,4},{3,5},{4,6},{5,7},{6,0},{7,1},{8,10},{9,11},{10,... | collective-permute-start | bytes 786440 | tf_op jit(solution)/shard_map/ppermute | solution.py:366
  79.9 19.2 %all-to-all-start = ((bf16[16,64,512]{2,1,0:T(8,128)(2,1)}), bf16[16,64,512]{2,1,0:T(8,128)(2,1)S(1)}, u32[]{:S(2)}, u32[]{:S(2)}) async-start(bf16[16,64,512]{2,1,0:T(8,128)(2,1)} %get-tuple-element.46), calls=%async_computation | async-start | bytes 2097152 | tf_op jit(solution)/shard_map/all_to_all | solution.py:396
  87.3 17.1 %collective-permute-start.17 = (bf16[384,1024]{1,0:T(8,128)(2,1)}, bf16[384,1024]{1,0:T(8,128)(2,1)S(1)}, u32[]{:S(2)}, u32[]{:S(2)}) collective-permute-start(bf16[384,1024]{1,0:T(8,128)(2,1)} %get-tuple-element.44), channel_id=1, source_target_pairs={{0,1},{1,0},{2,3},{3,2},{4,5},{5,4},{6,7},{7,6},{8,9},{9,8},{10,11... | collective-permute-start | bytes 2359304 | tf_op jit(solution)/shard_map/ppermute | solution.py:370
  90.4 19.4 %collective-permute-start.21 = (bf16[128,1024]{1,0:T(8,128)(2,1)S(1)}, bf16[128,1024]{1,0:T(8,128)(2,1)S(1)}, u32[]{:S(2)}, u32[]{:S(2)}) collective-permute-start(bf16[128,1024]{1,0:T(8,128)(2,1)S(1)} %add_convert_fusion.1), channel_id=1, source_target_pairs={{0,4},{1,5},{2,6},{3,7},{4,0},{5,1},{6,2},{7,3},{8,12},{9,13},{10,... | collective-permute-start | bytes 786440 | tf_op jit(solution)/shard_map/ppermute | solution.py:366
  99.8 8.6 %collective-permute-start.19 = (bf16[64,128]{1,0:T(8,128)(2,1)S(1)}, bf16[64,128]{1,0:T(8,128)(2,1)S(1)}, u32[]{:S(2)}, u32[]{:S(2)}) collective-permute-start(bf16[64,128]{1,0:T(8,128)(2,1)S(1)} %get-tuple-element.49), channel_id=1, source_target_pairs={{0,0},{1,32},{2,64},{3,96},{4,128},{5,160},{6,192},{7,224},{8,8},{... | collective-permute-start | bytes 49160 | tf_op jit(solution)/shard_map/ppermute | solution.py:380
  104.7 5.0 %collective-permute-start.18 = (bf16[32,384]{1,0:T(8,128)(2,1)S(1)}, bf16[32,384]{1,0:T(8,128)(2,1)S(1)}, u32[]{:S(2)}, u32[]{:S(2)}) collective-permute-start(bf16[32,384]{1,0:T(8,128)(2,1)S(1)} %get-tuple-element.48), channel_id=1, source_target_pairs={{0,128},{8,136},{16,144},{24,152},{32,160},{40,168},{48,176},{56,1... | collective-permute-start | bytes 73736 | tf_op jit(solution)/shard_map/ppermute | solution.py:374
  109.8 22.4 %collective-permute-start.22 = (bf16[128,1024]{1,0:T(8,128)(2,1)S(1)}, bf16[128,1024]{1,0:T(8,128)(2,1)S(1)}, u32[]{:S(2)}, u32[]{:S(2)}) collective-permute-start(bf16[128,1024]{1,0:T(8,128)(2,1)S(1)} %get-tuple-element.53), channel_id=1, source_target_pairs={{0,6},{1,7},{2,0},{3,1},{4,2},{5,3},{6,4},{7,5},{8,14},{9,15},{10,... | collective-permute-start | bytes 786440 | tf_op jit(solution)/shard_map/ppermute | solution.py:366
  112.5 19.7 %collective-permute-start.23 = (bf16[128,1024]{1,0:T(8,128)(2,1)S(1)}, bf16[128,1024]{1,0:T(8,128)(2,1)S(1)}, u32[]{:S(2)}, u32[]{:S(2)}) collective-permute-start(bf16[128,1024]{1,0:T(8,128)(2,1)S(1)} %get-tuple-element.55), channel_id=1, source_target_pairs={{0,2},{1,3},{2,4},{3,5},{4,6},{5,7},{6,0},{7,1},{8,10},{9,11},{10,... | collective-permute-start | bytes 786440 | tf_op jit(solution)/shard_map/ppermute | solution.py:366
  112.5 12.2 %collective-permute-start.26 = (bf16[32,640]{1,0:T(8,128)(2,1)S(1)}, bf16[32,640]{1,0:T(8,128)(2,1)S(1)}, u32[]{:S(2)}, u32[]{:S(2)}) collective-permute-start(bf16[32,640]{1,0:T(8,128)(2,1)S(1)} %pad_maximum_fusion.refs_0_), channel_id=1, source_target_pairs={{0,6},{1,7},{2,0},{3,1},{4,2},{5,3},{6,4},{7,5},{8,14},{9,15},{10,... | collective-permute-start | bytes 122888 | tf_op jit(solution)/shard_map/ppermute | solution.py:366
  116.1 11.7 %collective-permute-start.25 = (bf16[32,640]{1,0:T(8,128)(2,1)S(1)}, bf16[32,640]{1,0:T(8,128)(2,1)S(1)}, u32[]{:S(2)}, u32[]{:S(2)}) collective-permute-start(bf16[32,640]{1,0:T(8,128)(2,1)S(1)} %pad_maximum_fusion.refs_0_), channel_id=1, source_target_pairs={{0,4},{1,5},{2,6},{3,7},{4,0},{5,1},{6,2},{7,3},{8,12},{9,13},{10,... | collective-permute-start | bytes 122888 | tf_op jit(solution)/shard_map/ppermute | solution.py:366
  118.7 9.9 %collective-permute-start.24 = (bf16[32,640]{1,0:T(8,128)(2,1)S(1)}, bf16[32,640]{1,0:T(8,128)(2,1)S(1)}, u32[]{:S(2)}, u32[]{:S(2)}) collective-permute-start(bf16[32,640]{1,0:T(8,128)(2,1)S(1)} %pad_maximum_fusion.refs_0_), channel_id=1, source_target_pairs={{0,2},{1,3},{2,4},{3,5},{4,6},{5,7},{6,0},{7,1},{8,10},{9,11},{10,... | collective-permute-start | bytes 122888 | tf_op jit(solution)/shard_map/ppermute | solution.py:366
  124.7 8.8 %collective-permute-start.27 = (bf16[32,640]{1,0:T(8,128)(2,1)S(1)}, bf16[32,640]{1,0:T(8,128)(2,1)S(1)}, u32[]{:S(2)}, u32[]{:S(2)}) collective-permute-start(bf16[32,640]{1,0:T(8,128)(2,1)S(1)} %pad_maximum_fusion.refs_0_), channel_id=1, source_target_pairs={{0,1},{1,0},{2,3},{3,2},{4,5},{5,4},{6,7},{7,6},{8,9},{9,8},{10,11... | collective-permute-start | bytes 122888 | tf_op jit(solution)/shard_map/ppermute | solution.py:370
  127.8 5.7 %collective-permute-start.30 = (bf16[32,640]{1,0:T(8,128)(2,1)S(1)}, bf16[32,640]{1,0:T(8,128)(2,1)S(1)}, u32[]{:S(2)}, u32[]{:S(2)}) collective-permute-start(bf16[32,640]{1,0:T(8,128)(2,1)S(1)} %collective-permute-done.26.refs_3_), channel_id=1, source_target_pairs={{0,1},{1,0},{2,3},{3,2},{4,5},{5,4},{6,7},{7,6},{8,9},{9,8},{10,11... | collective-permute-start | bytes 122888 | tf_op jit(solution)/shard_map/ppermute | solution.py:370
  (28 other events, 235.2 us)
